TPU v7x, 32 devices: a whole 2x2x4 slice. The times are simulated.
32 devices in a mesh: dp: 8 (over z, x), mp: 4 (over y, core).
Axes of the slice: x: 2, y: 2, z: 4, core: 2. Of those that a mesh axis runs over, the one named last changes fastest.
Arguments:
- features: bfloat16 [1024, 1536], P('dp', 'mp'), may hold values from -240 to 240
- proj_weight: bfloat16 [1536, 1152], P('mp'), may hold values from -0.15625 to 0.15625
- texts: bfloat16 [1024, 1152], P(('dp', 'mp')), may hold values from -6 to 6
Outputs:
- grad_features: bfloat16 [1024, 1536], P('dp', 'mp')
- grad_weight: float32 [1536, 1152], P('mp')
All inputs are finite; a program needn't handle non-finite values.
Results may differ from a plain program's by a relative error of at most 0.011.
Values may be sent and summed in bfloat16 or wider, within the bound.
No kernel may reach another device: no remote copies, remote signals or barrier semaphores. Data moves between devices by JAX's collectives and lax.ppermute only.
A program may use at most 64 MiB of HBM per device.

v0:
```python
import functools

import jax
import jax.numpy as jnp
from jax import lax
from jax.experimental import pallas as pl
from jax.experimental.pallas import tpu as pltpu
from jax.sharding import PartitionSpec as P

logit_scale = 100.0
logit_bias = -10.0
epsilon = 1e-06
LANES = 128
GATHER_BYTES = 8 << 20
VMEM_BYTES = 40 << 20


def unit_rows(values):
    return values * lax.rsqrt(jnp.sum(values * values, axis=1, keepdims=True) + epsilon)


def add_texts(unit_img_b, image_ids, piece, piece_ids):
    unit_txt_b = unit_rows(piece.astype(jnp.float32)).astype(jnp.bfloat16)
    logits = (
        logit_scale * jnp.dot(unit_img_b, unit_txt_b.T, preferred_element_type=jnp.float32)
        + logit_bias
    )
    labels = jnp.where(image_ids[:, None] == piece_ids[None, :], 1.0, -1.0).astype(jnp.float32)
    slopes = (-labels * jax.nn.sigmoid(-labels * logits)).astype(jnp.bfloat16)
    return logit_scale * jnp.dot(slopes, unit_txt_b, preferred_element_type=jnp.float32)


def shards_summed(features, proj_weight, texts):
    local_rows = features.shape[0]
    width_local = features.shape[1]
    mp_count = lax.axis_size("mp")
    full_width = width_local * mp_count
    mp_index = lax.axis_index("mp")
    dp_index = lax.axis_index("dp")
    text_rows = texts.shape[0]
    inputs = features.astype(jnp.float32)
    mean_in = lax.psum(jnp.sum(inputs, axis=1, keepdims=True), "mp") / full_width
    centred = inputs - mean_in
    normed_b = centred.astype(jnp.bfloat16)
    partial_proj = jnp.dot(normed_b, proj_weight, preferred_element_type=jnp.float32)
    project = lax.psum(partial_proj, "mp")
    inv_norm = lax.rsqrt(jnp.sum(project * project, axis=1, keepdims=True) + epsilon)
    unit_img = project * inv_norm
    unit_img_b = unit_img.astype(jnp.bfloat16)
    image_ids = dp_index * local_rows + jnp.arange(local_rows, dtype=jnp.int32)
    piece = lax.all_gather(texts, "dp", axis=0, tiled=True)
    positions = jnp.arange(piece.shape[0], dtype=jnp.int32)
    shard_of = positions // text_rows
    piece_ids = (shard_of * mp_count + mp_index) * text_rows + positions % text_rows
    grad_unit = add_texts(unit_img_b, image_ids, piece, piece_ids)
    grad_unit = lax.psum(grad_unit, "mp")
    grad_proj = inv_norm * (
        grad_unit - unit_img * jnp.sum(unit_img * grad_unit, axis=1, keepdims=True)
    )
    grad_proj_b = grad_proj.astype(jnp.bfloat16)
    weight_part = jnp.dot(normed_b.T, grad_proj_b, preferred_element_type=jnp.float32)
    grad_weight = lax.psum(weight_part, "dp")
    grad_normed = jnp.dot(grad_proj_b, proj_weight.T, preferred_element_type=jnp.float32)
    grad_total = lax.psum(jnp.sum(grad_normed, axis=1, keepdims=True), "mp")
    grad_in = grad_normed - grad_total / full_width
    return (grad_in.astype(jnp.bfloat16), grad_weight)


def split_terms(value, count):
    terms = []
    for _ in range(count):
        term = value.astype(jnp.bfloat16).astype(jnp.float32)
        terms.append(term)
        value = value - term
    return terms


def kernel_call(body, outs, scratch=(), flops=0, **names):
    return pl.pallas_call(
        body,
        out_shape=outs,
        scratch_shapes=scratch,
        compiler_params=pltpu.CompilerParams(vmem_limit_bytes=VMEM_BYTES),
        cost_estimate=pl.CostEstimate(flops=flops, bytes_accessed=0, transcendentals=0),
        **names,
    )


def texts_body(texts_ref, out_ref):
    out_ref[...] = unit_rows(texts_ref[...].astype(jnp.float32)).astype(jnp.bfloat16)


def store_sums(extra_ref, column_sum, sum_row):
    extra_ref[...] = jnp.zeros_like(extra_ref)
    at = 0
    for term in split_terms(column_sum, 2):
        for i in range(column_sum.shape[1] // LANES):
            extra_ref[at : at + 1, :] = term[:, i * LANES : (i + 1) * LANES]
            at += 1
    for term in split_terms(sum_row, 3):
        extra_ref[at : at + 1, :] = term
        at += 1
    return extra_ref[...].astype(jnp.bfloat16)


def load_sums(extra, embed):
    chunks = embed // LANES
    extra = extra.astype(jnp.float32)
    column_sum = jnp.concatenate(
        [extra[i : i + 1] + extra[chunks + i : chunks + i + 1] for i in range(chunks)], axis=1
    )
    at = 2 * chunks
    return column_sum, extra[at : at + 1] + extra[at + 1 : at + 2] + extra[at + 2 : at + 3]


def pick_rows(sum_row, rows, group):
    row = lax.broadcasted_iota(jnp.int32, (rows, LANES), 0)
    lane = lax.broadcasted_iota(jnp.int32, (rows, LANES), 1)
    return jnp.sum(jnp.where(lane == row + group * rows, sum_row, 0.0), axis=1, keepdims=True)


def project_body(
    rows, mp_count, place_ref, features_ref, weight_ref,
    keep_ref, send_ref, column_sum_ref, sum_row_ref, extra_ref,
):
    embed = weight_ref.shape[1]
    local_rows, width = features_ref.shape
    values = features_ref[...].astype(jnp.float32)
    row_sum = jnp.sum(values, axis=1, keepdims=True)
    column_sum = jnp.sum(weight_ref[...].astype(jnp.float32), axis=0, keepdims=True)
    row = lax.broadcasted_iota(jnp.int32, (local_rows, LANES), 0)
    lane = lax.broadcasted_iota(jnp.int32, (local_rows, LANES), 1)
    sum_row = jnp.sum(jnp.where(row == lane, row_sum, 0.0), axis=0, keepdims=True)
    ordered = []
    for flip in list(range(0, mp_count, 2)) + list(range(1, mp_count, 2)):
        start = pl.multiple_of(((place_ref[0] ^ flip) & (mp_count - 1)) * rows, rows)
        block = features_ref[pl.ds(start, rows), :].astype(jnp.float32)
        ordered.append(block - jnp.sum(block, axis=1, keepdims=True) / width)
    centred = jnp.concatenate(ordered, axis=0).astype(jnp.bfloat16)
    product = jnp.dot(centred, weight_ref[...], preferred_element_type=jnp.float32)
    half = local_rows // 2
    keep_ref[...] = product[:half]
    send_ref[:, :embed] = product[half:].astype(jnp.bfloat16)
    extra = store_sums(extra_ref, column_sum, sum_row)
    for i in range(half // rows):
        send_ref[i * rows : (i + 1) * rows, embed:] = extra
    column_sum_ref[...] = column_sum
    sum_row_ref[...] = sum_row


def chip_body(
    width, mp_count, place_ref, keep_ref, received_ref, column_sum_ref, sum_row_ref,
    own_ref, send_ref, chip_column_ref, chip_row_ref, extra_ref,
):
    rows = own_ref.shape[0]
    embed = own_ref.shape[1]
    columns = [column_sum_ref[...], None]
    sum_rows = [sum_row_ref[...], None]
    columns[1], sum_rows[1] = load_sums(received_ref[:rows, embed:], embed)
    chip_column = columns[0] + columns[1]
    chip_row = sum_rows[0] + sum_rows[1]
    for i in range(2):
        group = (place_ref[0] ^ (2 * i)) & (mp_count - 1)
        mean = pick_rows(chip_row, rows, group) / (2 * width)
        here = slice(i * rows, (i + 1) * rows)
        total = keep_ref[here, :] + received_ref[here, :embed].astype(jnp.float32)
        for column, sum_row in zip(columns, sum_rows):
            total = total + (pick_rows(sum_row, rows, group) / width - mean) * column
        if i == 0:
            own_ref[...] = total
        else:
            send_ref[:, :embed] = total.astype(jnp.bfloat16)
    send_ref[:, embed:] = store_sums(extra_ref, chip_column, chip_row)
    chip_column_ref[...] = chip_column
    chip_row_ref[...] = chip_row


def rows_body(
    full_width, mp_count, place_ref, own_ref, received_ref, column_sum_ref, sum_row_ref,
    project_ref, weight_sum_ref,
):
    rows, embed = own_ref.shape
    columns = [column_sum_ref[...], None]
    sum_rows = [sum_row_ref[...], None]
    columns[1], sum_rows[1] = load_sums(received_ref[:, embed:], embed)
    group = place_ref[0] & (mp_count - 1)
    mean = pick_rows(sum_rows[0] + sum_rows[1], rows, group) / full_width
    project = own_ref[...] + received_ref[:, :embed].astype(jnp.float32)
    for column, sum_row in zip(columns, sum_rows):
        part_mean = pick_rows(sum_row, rows, group) / (full_width // 2)
        project = project + (part_mean - mean) * column
    project_ref[:, :embed] = project.astype(jnp.bfloat16)
    lane = lax.broadcasted_iota(jnp.int32, (rows, LANES), 1)
    extra = jnp.zeros((rows, LANES), jnp.float32)
    for i, term in enumerate(split_terms(mean, 3)):
        extra = jnp.where(lane == i, term, extra)
    project_ref[:, embed:] = extra.astype(jnp.bfloat16)
    weight_sum_ref[...] = columns[0] + columns[1]


def grad_body(first, project_ref, *refs):
    (*texts, out_ref) = refs
    embed = texts[0].shape[1]
    project = project_ref[:, :embed].astype(jnp.float32)
    inv_norm = lax.rsqrt(jnp.sum(project * project, axis=1, keepdims=True) + epsilon)
    unit_img = project * inv_norm
    unit_img_b = unit_img.astype(jnp.bfloat16)
    grad_unit = jnp.zeros_like(project)
    at = 0
    for ref in texts:
        unit_txt_b = ref[...]
        logits = (
            logit_scale
            * lax.dot_general(
                unit_img_b,
                unit_txt_b,
                (((1,), (1,)), ((), ())),
                preferred_element_type=jnp.float32,
            )
            + logit_bias
        )
        text = lax.broadcasted_iota(jnp.int32, logits.shape, 1) + at
        image = lax.broadcasted_iota(jnp.int32, logits.shape, 0) + first
        labels = jnp.where(text == image, 1.0, -1.0)
        slopes = (-labels / (1.0 + jnp.exp(labels * logits))).astype(jnp.bfloat16)
        grad_unit = grad_unit + jnp.dot(slopes, unit_txt_b, preferred_element_type=jnp.float32)
        at += unit_txt_b.shape[0]
    grad_unit = logit_scale * grad_unit
    grad_proj = inv_norm * (
        grad_unit - unit_img * jnp.sum(unit_img * grad_unit, axis=1, keepdims=True)
    )
    out_ref[:, :embed] = grad_proj.astype(jnp.bfloat16)
    out_ref[:, embed:] = project_ref[:, embed:]


def weight_body(
    rows, mp_count, gather_order, orders, tiles, place_ref, features_ref, *refs
):
    count = 2 * len(orders)
    arrays = refs[:count]
    previous = refs[count : count + 1] if len(refs) - count > (1 if tiles == 1 else 3) else ()
    outs = refs[count + len(previous) :]
    embed = outs[0].shape[1]
    blocks = []
    for at, order in enumerate(orders):
        for i in range(2):
            extra = arrays[2 * at + i][:, embed:].astype(jnp.float32)
            mean = extra[:, 0:1] + extra[:, 1:2] + extra[:, 2:3]
            for k, flip in enumerate(order):
                group = (place_ref[0] ^ flip ^ i) & (mp_count - 1)
                start = (gather_order.index(flip - flip % mp_count) * mp_count + group) * rows
                block = features_ref[pl.ds(pl.multiple_of(start, rows), rows), :]
                blocks.append(block.astype(jnp.float32) - mean[k * rows : (k + 1) * rows])
    normed = jnp.concatenate(blocks, axis=0).astype(jnp.bfloat16)
    gradient = jnp.concatenate([array[:, :embed] for array in arrays], axis=0)
    if tiles == 1:
        total = lax.dot_general(
            normed, gradient, (((0,), (0,)), ((), ())), preferred_element_type=jnp.float32
        )
        for ref in previous:
            total = total + ref[...]
        outs[0][...] = total
        return
    out_hbm, total_ref, sent = outs
    wide = gradient.shape[1] // tiles
    copies = []
    for k in range(tiles):
        here = slice(k * wide, (k + 1) * wide)
        total = lax.dot_general(
            normed, gradient[:, here], (((0,), (0,)), ((), ())), preferred_element_type=jnp.float32
        )
        for ref in previous:
            total = total + ref[:, here]
        total_ref[:, here] = total
        copies.append(
            pltpu.make_async_copy(total_ref.at[:, here], out_hbm.at[:, here], sent.at[k])
        )
        copies[-1].start()
    for copy in copies:
        copy.wait()


def features_body(full_width, rows, mp_count, place_ref, weight_ref, weight_sum_ref, *refs):
    (*parts, out_ref, group_ref) = refs
    for flip, part in enumerate(parts):
        start = pl.multiple_of(((place_ref[0] ^ flip) & (mp_count - 1)) * rows, rows)
        group_ref[pl.ds(start, rows), :] = part[:rows, : group_ref.shape[1]]
    group = group_ref[...]
    grad_normed = lax.dot_general(
        group, weight_ref[...], (((1,), (1,)), ((), ())), preferred_element_type=jnp.float32
    )
    grad_total = jnp.sum(group.astype(jnp.float32) * weight_sum_ref[...], axis=1, keepdims=True)
    out_ref[...] = (grad_normed - grad_total / full_width).astype(jnp.bfloat16)


def shards_gathered(features, proj_weight, texts):
    axes = ("dp", "mp")
    dp_count, mp_count = lax.axis_size("dp"), lax.axis_size("mp")
    count = dp_count * mp_count
    plane_count = 2 * mp_count
    local_rows, width = features.shape
    embed = proj_weight.shape[1]
    rows = texts.shape[0]
    half = local_rows // 2
    full_width = width * mp_count
    place = (lax.axis_index("dp") * mp_count + lax.axis_index("mp")).astype(jnp.int32).reshape(1)
    core, across, column = 1, 2, mp_count
    line = list(range(plane_count, count, plane_count))

    def swap(value, flip):
        return lax.ppermute(value, axes, [(i, i ^ flip) for i in range(count)])

    def struct(dims, kind=jnp.bfloat16):
        return jax.ShapeDtypeStruct(dims, kind)

    def along_line(value, order):
        return jnp.concatenate([value] + [swap(value, flip) for flip in order], axis=0)

    smem = pl.BlockSpec(memory_space=pltpu.SMEM)
    vmem = pl.BlockSpec(memory_space=pltpu.VMEM)
    sums = [struct((1, embed), jnp.float32), struct((1, LANES), jnp.float32)]
    extra = pltpu.VMEM((rows, LANES), jnp.float32)

    keep, send, column_sum, sum_row = kernel_call(
        functools.partial(project_body, rows, mp_count),
        [struct((half, embed), jnp.float32), struct((half, embed + LANES))] + sums,
        scratch=[extra],
        in_specs=[smem, vmem, vmem],
        flops=2 * local_rows * width * embed,
        name="project",
    )(place, features, proj_weight)
    own, send, column_sum, sum_row = kernel_call(
        functools.partial(chip_body, width, mp_count),
        [struct((rows, embed), jnp.float32), struct((rows, embed + LANES))] + sums,
        scratch=[extra],
        in_specs=[smem] + [vmem] * 4,
        name="chip_project",
    )(place, keep, swap(send, core), column_sum, sum_row)
    far, near = line[1], line[0]
    order = [0, far, near, far ^ near]
    plane = [0, across, column, column | across]
    unit_txt_b = kernel_call(texts_body, struct(texts.shape), name="unit_texts")(texts)
    txt_line = jnp.concatenate(
        [unit_txt_b] + [swap(unit_txt_b, flip) for flip in order[1:]], axis=0
    )
    features_x = swap(features, column)
    send, features_x = lax.optimization_barrier((send, features_x))
    send, txt_line = lax.optimization_barrier((send, txt_line))
    middle = local_rows // 2

    def diagonal(by_y, by_x):
        return jnp.concatenate(
            [swap(by_x[:middle], across), swap(by_y[middle:], column)], axis=0
        )

    txt_y, txt_x = swap(txt_line, across), swap(txt_line, column)
    txt_plane = [txt_line, txt_y, txt_x, diagonal(txt_y, txt_x)]

    project, weight_sum = kernel_call(
        functools.partial(rows_body, full_width, mp_count),
        [
            struct((rows, embed + LANES)),
            struct((1, embed), jnp.float32),
        ],
        in_specs=[smem] + [vmem] * 4,
        name="project_rows",
    )(place, own, swap(send, across), column_sum, sum_row)

    gathered = jnp.concatenate([features, features_x], axis=0)
    far_rows = swap(project, far)
    far_rows, gathered = lax.optimization_barrier((far_rows, gathered))
    line_rows = jnp.concatenate([project, far_rows], axis=0)
    line_rows = jnp.concatenate([line_rows, swap(line_rows, near)], axis=0)
    features_far = swap(gathered, far)
    line_rows, features_far, txt_plane[1], txt_plane[2] = lax.optimization_barrier(
        (line_rows, features_far, txt_plane[1], txt_plane[2])
    )
    gathered = jnp.concatenate([gathered, features_far], axis=0)
    features_near = swap(gathered, near)
    gather_order = sum([[o, o ^ column] for o in order], [])
    all_texts = [jnp.concatenate(txt_plane, axis=0)]
    all_texts.append(swap(all_texts[0], core))
    rows_y, rows_x = swap(line_rows, across), swap(line_rows, column)
    diagonal_rows = [swap(rows_x[:middle], across), swap(rows_y[middle:], column)]
    plane_rows = [line_rows, rows_y, rows_x]

    def gradient(index):
        return kernel_call(
            functools.partial(grad_body, index * local_rows),
            struct(line_rows.shape),
            flops=4 * local_rows * count * rows * embed,
            name="grad",
        )(plane_rows[index], *all_texts)

    grads = [gradient(0)]
    others = [swap(grads[0], core)]
    grads.append(gradient(1))
    others.append(swap(grads[1], core))
    gathered = jnp.concatenate([gathered, features_near], axis=0)

    def add_product(indices, previous, final=False):
        arrays = sum([[grads[i], others[i]] for i in indices], [])
        orders = [[o ^ plane[i] for o in order] for i in indices]
        tiles = 3 if final else 1
        scratch = [
            pltpu.VMEM(proj_weight.shape, jnp.float32),
            pltpu.SemaphoreType.DMA((tiles,)),
        ]
        return kernel_call(
            functools.partial(weight_body, rows, mp_count, gather_order, orders, tiles),
            struct(proj_weight.shape, jnp.float32),
            scratch=scratch if final else (),
            in_specs=[smem] + [vmem] * (1 + len(arrays) + len(previous)),
            out_specs=pl.BlockSpec(memory_space=pl.ANY) if final else vmem,
            flops=4 * width * embed * local_rows * len(indices),
            name="weight",
        )(place, gathered, *arrays, *previous)

    grad_features = kernel_call(
        functools.partial(features_body, full_width, rows, mp_count),
        struct(features.shape),
        scratch=[pltpu.VMEM((local_rows, embed), jnp.bfloat16)],
        in_specs=[smem] + [vmem] * (2 + mp_count),
        flops=2 * local_rows * width * embed,
        name="grad_features",
    )(place, proj_weight, weight_sum, grads[0], others[0], grads[1], others[1])
    first = [0]
    grad_weight = add_product(first, [])
    grads.append(gradient(2))
    others.append(swap(grads[2], core))
    *diagonal_rows, _, _ = lax.optimization_barrier((*diagonal_rows, grads[2], grad_weight))
    plane_rows.append(jnp.concatenate(diagonal_rows, axis=0))
    grads.append(gradient(3))
    others.append(swap(grads[3], core))
    grad_weight = add_product([1, 2], [grad_weight])
    grad_weight = add_product([3], [grad_weight], True)
    return grad_features, grad_weight


def shards(features, proj_weight, texts):
    dp_count, mp_count = lax.axis_size("dp"), lax.axis_size("mp")
    count = dp_count * mp_count
    rows = texts.shape[0]
    embed = texts.shape[1]
    fits = (
        count * rows * (embed + LANES) * 2 <= GATHER_BYTES
        and count & (count - 1) == 0
        and mp_count == 4
        and count == 8 * mp_count
        and features.shape[0] == LANES == mp_count * rows
        and embed % LANES == 0
        and 2 * (embed // LANES) + 3 <= rows
        and rows % 16 == 0
    )
    plan = shards_gathered if fits else shards_summed
    return plan(features, proj_weight, texts)


def solution(mesh):
    return jax.shard_map(
        shards,
        mesh=mesh,
        in_specs=(P("dp", "mp"), P("mp", None), P(("dp", "mp"), None)),
        out_specs=(P("dp", "mp"), P("mp", None)),
        check_vma=False,
    )
```

profile of v0, /device:TPU:0, one launch (start us, length us, event | category | flops | bytes accessed | tf_op | source)
XLA Modules:
  0.0 58.3 jit_solution(468199868546963003)
XLA Ops:
  0.6 0.9 %copy-done.4 = bf16[32,1152]{1,0:T(8,128)(2,1)S(1)} copy-done((bf16[32,1152]{1,0:T(8,128)(2,1)S(1)}, bf16[32,1152]{1,0:T(8,128)(2,1)}, u32[]{:S(2)}) %copy-start.4) | copy-done | bytes 73752
  1.6 5.1 %collective-permute-start.4 = (bf16[32,1152]{1,0:T(8,128)(2,1)S(1)}, bf16[32,1152]{1,0:T(8,128)(2,1)S(1)}, u32[]{:S(2)}, u32[]{:S(2)}) collective-permute-start(bf16[32,1152]{1,0:T(8,128)(2,1)S(1)} %unit_texts.1), channel_id=1, source_target_pairs={{0,24},{1,25},{2,26},{3,27},{4,28},{5,29},{6,30},{7,31},{8,16},{9,... | collective-permute-start | bytes 221192 | tf_op jit(solution)/shard_map/ppermute | solution.py:311
  7.4 1.6 %collective-permute-start.1 = (bf16[128,384]{1,0:T(8,128)(2,1)}, bf16[128,384]{1,0:T(8,128)(2,1)S(1)}, u32[]{:S(2)}, u32[]{:S(2)}) collective-permute-start(bf16[128,384]{1,0:T(8,128)(2,1)} %features_ref.1), channel_id=1, source_target_pairs={{0,4},{1,5},{2,6},{3,7},{4,0},{5,1},{6,2},{7,3},{8,12},{9,13},{10,... | collective-permute-start | bytes 294920 | tf_op jit(solution)/shard_map/ppermute | solution.py:311
  9.0 1.2 %copy-done = bf16[384,1152]{1,0:T(8,128)(2,1)S(1)} copy-done((bf16[384,1152]{1,0:T(8,128)(2,1)S(1)}, bf16[384,1152]{1,0:T(8,128)(2,1)}, u32[]{:S(2)}) %copy-start) | copy-done | bytes 884760
  10.2 0.9 %copy-done.2 = bf16[128,384]{1,0:T(8,128)(2,1)S(1)} copy-done((bf16[128,384]{1,0:T(8,128)(2,1)S(1)}, bf16[128,384]{1,0:T(8,128)(2,1)}, u32[]{:S(2)}) %copy-start.2) | copy-done | bytes 98328
  13.1 1.6 %collective-permute-start.5 = (bf16[32,1280]{1,0:T(8,128)(2,1)S(1)}, bf16[32,1280]{1,0:T(8,128)(2,1)S(1)}, u32[]{:S(2)}, u32[]{:S(2)}) collective-permute-start(bf16[32,1280]{1,0:T(8,128)(2,1)S(1)} %get-tuple-element.31), channel_id=1, source_target_pairs={{0,2},{1,3},{2,0},{3,1},{4,6},{5,7},{6,4},{7,5},{8,10},{9,11},{10,... | collective-permute-start | bytes 245768 | tf_op jit(solution)/shard_map/ppermute | solution.py:311
  15.2 1.2 %collective-permute-start.10 = (bf16[128,1152]{1,0:T(8,128)(2,1)S(1)}, bf16[128,1152]{1,0:T(8,128)(2,1)S(1)}, u32[]{:S(2)}, u32[]{:S(2)}) collective-permute-start(bf16[128,1152]{1,0:T(8,128)(2,1)S(1)} %pad_maximum_fusion.3), channel_id=1, source_target_pairs={{0,4},{1,5},{2,6},{3,7},{4,0},{5,1},{6,2},{7,3},{8,12},{9,13},{10,... | collective-permute-start | bytes 884744 | tf_op jit(solution)/shard_map/ppermute | solution.py:311
  16.4 1.8 %collective-permute-done.5.received_ref = bf16[32,1280]{1,0:T(8,128)(2,1)S(1)} collective-permute-done((bf16[32,1280]{1,0:T(8,128)(2,1)S(1)}, bf16[32,1280]{1,0:T(8,128)(2,1)S(1)}, u32[]{:S(2)}, u32[]{:S(2)}) %collective-permute-start.5) | collective-permute-done | bytes 81952 | tf_op jit(solution)/shard_map/ppermute | solution.py:311
  18.4 2.2 %collective-permute-start.6 = (bf16[32,1280]{1,0:T(8,128)(2,1)S(1)}, bf16[32,1280]{1,0:T(8,128)(2,1)S(1)}, u32[]{:S(2)}, u32[]{:S(2)}) collective-permute-start(bf16[32,1280]{1,0:T(8,128)(2,1)S(1)} %get-tuple-element.35), channel_id=1, source_target_pairs={{0,16},{1,17},{2,18},{3,19},{4,20},{5,21},{6,22},{7,23},{8,24},{9,... | collective-permute-start | bytes 245768 | tf_op jit(solution)/shard_map/ppermute | solution.py:311
  20.6 4.2 %collective-permute-done.6 = bf16[32,1280]{1,0:T(8,128)(2,1)S(1)} collective-permute-done((bf16[32,1280]{1,0:T(8,128)(2,1)S(1)}, bf16[32,1280]{1,0:T(8,128)(2,1)S(1)}, u32[]{:S(2)}, u32[]{:S(2)}) %collective-permute-start.6) | collective-permute-done | bytes 81952 | tf_op jit(solution)/shard_map/ppermute | solution.py:311
  25.3 3.2 %collective-permute-start.8 = (bf16[256,384]{1,0:T(8,128)(2,1)S(1)}, bf16[256,384]{1,0:T(8,128)(2,1)S(1)}, u32[]{:S(2)}, u32[]{:S(2)}) collective-permute-start(bf16[256,384]{1,0:T(8,128)(2,1)S(1)} %pad_maximum_fusion.4), channel_id=1, source_target_pairs={{0,16},{1,17},{2,18},{3,19},{4,20},{5,21},{6,22},{7,23},{8,24},{9,... | collective-permute-start | bytes 589832 | tf_op jit(solution)/shard_map/ppermute | solution.py:311
  28.5 1.8 %collective-permute-start.11 = (bf16[64,1152]{1,0:T(8,128)(2,1)S(1)}, bf16[64,1152]{1,0:T(8,128)(2,1)S(1)}, u32[]{:S(2)}, u32[]{:S(2)}) collective-permute-start(bf16[64,1152]{1,0:T(8,128)(2,1)S(1)} %slice.16), channel_id=1, source_target_pairs={{0,2},{1,3},{2,0},{3,1},{4,6},{5,7},{6,4},{7,5},{8,10},{9,11},{10,... | collective-permute-start | bytes 442376 | tf_op jit(solution)/shard_map/ppermute | solution.py:311
  30.3 1.4 %collective-permute-start.12 = (bf16[64,1152]{1,0:T(8,128)(2,1)S(1)}, bf16[64,1152]{1,0:T(8,128)(2,1)S(1)}, u32[]{:S(2)}, u32[]{:S(2)}) collective-permute-start(bf16[64,1152]{1,0:T(8,128)(2,1)S(1)} %slice.17), channel_id=1, source_target_pairs={{0,4},{1,5},{2,6},{3,7},{4,0},{5,1},{6,2},{7,3},{8,12},{9,13},{10,... | collective-permute-start | bytes 442376 | tf_op jit(solution)/shard_map/ppermute | solution.py:311
  31.7 3.3 %collective-permute-done.8 = bf16[256,384]{1,0:T(8,128)(2,1)S(1)} collective-permute-done((bf16[256,384]{1,0:T(8,128)(2,1)S(1)}, bf16[256,384]{1,0:T(8,128)(2,1)S(1)}, u32[]{:S(2)}, u32[]{:S(2)}) %collective-permute-start.8) | collective-permute-done | bytes 196640 | tf_op jit(solution)/shard_map/ppermute | solution.py:311
  35.8 1.8 %collective-permute-start.18 = (bf16[128,1280]{1,0:T(8,128)(2,1)S(1)}, bf16[128,1280]{1,0:T(8,128)(2,1)S(1)}, u32[]{:S(2)}, u32[]{:S(2)}) collective-permute-start(bf16[128,1280]{1,0:T(8,128)(2,1)S(1)} %pad_maximum_fusion.1.project_ref), channel_id=1, source_target_pairs={{0,4},{1,5},{2,6},{3,7},{4,0},{5,1},{6,2},{7,3},{8,12},{9,13},{10,... | collective-permute-start | bytes 983048 | tf_op jit(solution)/shard_map/ppermute | solution.py:311
  38.5 1.6 %grad.4.refs_0_ = bf16[128,1280]{1,0:T(8,128)(2,1)S(1)} custom-call(bf16[128,1280]{1,0:T(8,128)(2,1)S(1)} %pad_maximum_fusion.1.project_ref, bf16[512,1152]{1,0:T(8,128)(2,1)S(1)} %constant_dynamic-update-slice_fusion.refs_0_, bf16[512,1152]{1,0:T(8,128)(2,1)S(1)} %collective-permute-done.13.refs_1_), custom_call_target="tpu_custom_call" | custom-call | flops 603979776 | tf_op jit(solution)/shard_map/grad/pallas_call | solution.py:388
  40.3 5.6 %collective-permute-done.18.project_ref = bf16[128,1280]{1,0:T(8,128)(2,1)S(1)} collective-permute-done((bf16[128,1280]{1,0:T(8,128)(2,1)S(1)}, bf16[128,1280]{1,0:T(8,128)(2,1)S(1)}, u32[]{:S(2)}, u32[]{:S(2)}) %collective-permute-start.18) | collective-permute-done | bytes 327712 | tf_op jit(solution)/shard_map/ppermute | solution.py:311
  45.9 1.2 %collective-permute-start.19 = (bf16[64,1280]{1,0:T(8,128)(2,1)S(1)}, bf16[64,1280]{1,0:T(8,128)(2,1)S(1)}, u32[]{:S(2)}, u32[]{:S(2)}) collective-permute-start(bf16[64,1280]{1,0:T(8,128)(2,1)S(1)} %slice.18), channel_id=1, source_target_pairs={{0,2},{1,3},{2,0},{3,1},{4,6},{5,7},{6,4},{7,5},{8,10},{9,11},{10,... | collective-permute-start | bytes 491528 | tf_op jit(solution)/shard_map/ppermute | solution.py:311
  48.0 1.6 %grad.5.refs_2_.refs_0_ = bf16[128,1280]{1,0:T(8,128)(2,1)S(1)} custom-call(bf16[128,1280]{1,0:T(8,128)(2,1)S(1)} %collective-permute-done.15.project_ref, bf16[512,1152]{1,0:T(8,128)(2,1)S(1)} %constant_dynamic-update-slice_fusion.refs_0_, bf16[512,1152]{1,0:T(8,128)(2,1)S(1)} %collective-permute-done.13.refs_1_), custom_call_target="tpu_custom_call" | custom-call | flops 603979776 | tf_op jit(solution)/shard_map/grad/pallas_call | solution.py:388
  49.7 1.6 %grad.6.refs_2_ = bf16[128,1280]{1,0:T(8,128)(2,1)S(1)} custom-call(bf16[128,1280]{1,0:T(8,128)(2,1)S(1)} %collective-permute-done.18.project_ref, bf16[512,1152]{1,0:T(8,128)(2,1)S(1)} %constant_dynamic-update-slice_fusion.refs_0_, bf16[512,1152]{1,0:T(8,128)(2,1)S(1)} %collective-permute-done.13.refs_1_), custom_call_target="tpu_custom_call" | custom-call | flops 603979776 | tf_op jit(solution)/shard_map/grad/pallas_call | solution.py:388
  52.8 1.6 %grad.7.refs_0_ = bf16[128,1280]{1,0:T(8,128)(2,1)S(1)} custom-call(bf16[128,1280]{1,0:T(8,128)(2,1)S(1)} %pad_maximum_fusion.2.project_ref, bf16[512,1152]{1,0:T(8,128)(2,1)S(1)} %constant_dynamic-update-slice_fusion.refs_0_, bf16[512,1152]{1,0:T(8,128)(2,1)S(1)} %collective-permute-done.13.refs_1_), custom_call_target="tpu_custom_call" | custom-call | flops 603979776 | tf_op jit(solution)/shard_map/grad/pallas_call | solution.py:388
  54.6 1.1 %grad_features.1 = bf16[128,384]{1,0:T(8,128)(2,1)} custom-call(s32[1]{0:T(128)} %bitcast.place_ref, bf16[384,1152]{1,0:T(8,128)(2,1)S(1)} %copy-done.1, f32[1,1152]{1,0:T(1,128)S(1)} %get-tuple-element.34.weight_sum_ref, bf16[128,1280]{1,0:T(8,128)(2,1)S(1)} %grad.4.refs_0_, bf16[128,1280]{1,0:T(8,128)(2,1)S(1)} %collective-permute-done.14.refs_1_, ...), custom_call_target="tpu_custom_call" | custom-call | flops 113246208 | tf_op jit(solution)/shard_map/grad_features/pallas_call | solution.py:419
  55.6 0.9 %weight.4.refs_2_ = f32[384,1152]{1,0:T(8,128)S(1)} custom-call(s32[1]{0:T(128)} %bitcast.place_ref, bf16[1024,384]{1,0:T(8,128)(2,1)S(1)} %constant_dynamic-update-slice_fusion.5.features_ref, bf16[128,1280]{1,0:T(8,128)(2,1)S(1)} %grad.5.refs_2_.refs_0_, bf16[128,1280]{1,0:T(8,128)(2,1)S(1)} %collective-permute-done.16.refs_3_.refs_1_, ...), custom_call_target="tpu_custom_call" | custom-call | flops 452984832 | tf_op jit(solution)/shard_map/weight/pallas_call | solution.py:409
  56.6 1.7 %weight.5 = f32[384,1152]{1,0:T(8,128)} custom-call(s32[1]{0:T(128)} %bitcast.place_ref, bf16[1024,384]{1,0:T(8,128)(2,1)S(1)} %constant_dynamic-update-slice_fusion.5.features_ref, bf16[128,1280]{1,0:T(8,128)(2,1)S(1)} %grad.7.refs_0_, bf16[128,1280]{1,0:T(8,128)(2,1)S(1)} %collective-permute-done.21.refs_1_, f32[384,1152]{1,0:T(8,128)S(1)} %weight.4.refs_2_), custom_call_target="tpu_custom_call" | custom-call | flops 226492416 | tf_op jit(solution)/shard_map/weight/pallas_call | solution.py:409
  (62 shorter events, 8.2 us)
Async XLA Ops:
  1.5 19.1 %copy-start.3 = (bf16[128,384]{1,0:T(8,128)(2,1)S(1)}, bf16[128,384]{1,0:T(8,128)(2,1)}, u32[]{:S(2)}) copy-start(bf16[128,384]{1,0:T(8,128)(2,1)} %features_ref.1) | copy-start | bytes 294916
  1.6 10.0 %collective-permute-start.4 = (bf16[32,1152]{1,0:T(8,128)(2,1)S(1)}, bf16[32,1152]{1,0:T(8,128)(2,1)S(1)}, u32[]{:S(2)}, u32[]{:S(2)}) collective-permute-start(bf16[32,1152]{1,0:T(8,128)(2,1)S(1)} %unit_texts.1), channel_id=1, source_target_pairs={{0,24},{1,25},{2,26},{3,27},{4,28},{5,29},{6,30},{7,31},{8,16},{9,... | collective-permute-start | bytes 221192 | tf_op jit(solution)/shard_map/ppermute | solution.py:311
  6.7 5.0 %collective-permute-start.3 = (bf16[32,1152]{1,0:T(8,128)(2,1)S(1)}, bf16[32,1152]{1,0:T(8,128)(2,1)S(1)}, u32[]{:S(2)}, u32[]{:S(2)}) collective-permute-start(bf16[32,1152]{1,0:T(8,128)(2,1)S(1)} %unit_texts.1), channel_id=1, source_target_pairs={{0,8},{1,9},{2,10},{3,11},{4,12},{5,13},{6,14},{7,15},{8,0},{9,1},... | collective-permute-start | bytes 221192 | tf_op jit(solution)/shard_map/ppermute | solution.py:311
  6.7 5.8 %collective-permute-start.2 = (bf16[32,1152]{1,0:T(8,128)(2,1)S(1)}, bf16[32,1152]{1,0:T(8,128)(2,1)S(1)}, u32[]{:S(2)}, u32[]{:S(2)}) collective-permute-start(bf16[32,1152]{1,0:T(8,128)(2,1)S(1)} %unit_texts.1), channel_id=1, source_target_pairs={{0,16},{1,17},{2,18},{3,19},{4,20},{5,21},{6,22},{7,23},{8,24},{9,... | collective-permute-start | bytes 221192 | tf_op jit(solution)/shard_map/ppermute | solution.py:311
  7.4 5.7 %collective-permute-start.1 = (bf16[128,384]{1,0:T(8,128)(2,1)}, bf16[128,384]{1,0:T(8,128)(2,1)S(1)}, u32[]{:S(2)}, u32[]{:S(2)}) collective-permute-start(bf16[128,384]{1,0:T(8,128)(2,1)} %features_ref.1), channel_id=1, source_target_pairs={{0,4},{1,5},{2,6},{3,7},{4,0},{5,1},{6,2},{7,3},{8,12},{9,13},{10,... | collective-permute-start | bytes 294920 | tf_op jit(solution)/shard_map/ppermute | solution.py:311
  11.5 1.5 %collective-permute-start = (bf16[64,1280]{1,0:T(8,128)(2,1)S(1)}, bf16[64,1280]{1,0:T(8,128)(2,1)S(1)}, u32[]{:S(2)}, u32[]{:S(2)}) collective-permute-start(bf16[64,1280]{1,0:T(8,128)(2,1)S(1)} %get-tuple-element.25), channel_id=1, source_target_pairs={{0,1},{1,0},{2,3},{3,2},{4,5},{5,4},{6,7},{7,6},{8,9},{9,8},{10,11... | collective-permute-start | bytes 491528 | tf_op jit(solution)/shard_map/ppermute | solution.py:311
  13.1 5.2 %collective-permute-start.5 = (bf16[32,1280]{1,0:T(8,128)(2,1)S(1)}, bf16[32,1280]{1,0:T(8,128)(2,1)S(1)}, u32[]{:S(2)}, u32[]{:S(2)}) collective-permute-start(bf16[32,1280]{1,0:T(8,128)(2,1)S(1)} %get-tuple-element.31), channel_id=1, source_target_pairs={{0,2},{1,3},{2,0},{3,1},{4,6},{5,7},{6,4},{7,5},{8,10},{9,11},{10,... | collective-permute-start | bytes 245768 | tf_op jit(solution)/shard_map/ppermute | solution.py:311
  14.7 15.6 %collective-permute-start.9 = (bf16[128,1152]{1,0:T(8,128)(2,1)S(1)}, bf16[128,1152]{1,0:T(8,128)(2,1)S(1)}, u32[]{:S(2)}, u32[]{:S(2)}) collective-permute-start(bf16[128,1152]{1,0:T(8,128)(2,1)S(1)} %pad_maximum_fusion.3), channel_id=1, source_target_pairs={{0,2},{1,3},{2,0},{3,1},{4,6},{5,7},{6,4},{7,5},{8,10},{9,11},{10,... | collective-permute-start | bytes 884744 | tf_op jit(solution)/shard_map/ppermute | solution.py:311
  15.2 13.2 %collective-permute-start.10 = (bf16[128,1152]{1,0:T(8,128)(2,1)S(1)}, bf16[128,1152]{1,0:T(8,128)(2,1)S(1)}, u32[]{:S(2)}, u32[]{:S(2)}) collective-permute-start(bf16[128,1152]{1,0:T(8,128)(2,1)S(1)} %pad_maximum_fusion.3), channel_id=1, source_target_pairs={{0,4},{1,5},{2,6},{3,7},{4,0},{5,1},{6,2},{7,3},{8,12},{9,13},{10,... | collective-permute-start | bytes 884744 | tf_op jit(solution)/shard_map/ppermute | solution.py:311
  18.4 6.4 %collective-permute-start.6 = (bf16[32,1280]{1,0:T(8,128)(2,1)S(1)}, bf16[32,1280]{1,0:T(8,128)(2,1)S(1)}, u32[]{:S(2)}, u32[]{:S(2)}) collective-permute-start(bf16[32,1280]{1,0:T(8,128)(2,1)S(1)} %get-tuple-element.35), channel_id=1, source_target_pairs={{0,16},{1,17},{2,18},{3,19},{4,20},{5,21},{6,22},{7,23},{8,24},{9,... | collective-permute-start | bytes 245768 | tf_op jit(solution)/shard_map/ppermute | solution.py:311
  24.8 6.9 %collective-permute-start.7 = (bf16[64,1280]{1,0:T(8,128)(2,1)S(1)}, bf16[64,1280]{1,0:T(8,128)(2,1)S(1)}, u32[]{:S(2)}, u32[]{:S(2)}) collective-permute-start(bf16[64,1280]{1,0:T(8,128)(2,1)S(1)} %pad_maximum_fusion.5), channel_id=1, source_target_pairs={{0,8},{1,9},{2,10},{3,11},{4,12},{5,13},{6,14},{7,15},{8,0},{9,1},... | collective-permute-start | bytes 491528 | tf_op jit(solution)/shard_map/ppermute | solution.py:311
  25.3 9.8 %collective-permute-start.8 = (bf16[256,384]{1,0:T(8,128)(2,1)S(1)}, bf16[256,384]{1,0:T(8,128)(2,1)S(1)}, u32[]{:S(2)}, u32[]{:S(2)}) collective-permute-start(bf16[256,384]{1,0:T(8,128)(2,1)S(1)} %pad_maximum_fusion.4), channel_id=1, source_target_pairs={{0,16},{1,17},{2,18},{3,19},{4,20},{5,21},{6,22},{7,23},{8,24},{9,... | collective-permute-start | bytes 589832 | tf_op jit(solution)/shard_map/ppermute | solution.py:311
  28.5 6.6 %collective-permute-start.11 = (bf16[64,1152]{1,0:T(8,128)(2,1)S(1)}, bf16[64,1152]{1,0:T(8,128)(2,1)S(1)}, u32[]{:S(2)}, u32[]{:S(2)}) collective-permute-start(bf16[64,1152]{1,0:T(8,128)(2,1)S(1)} %slice.16), channel_id=1, source_target_pairs={{0,2},{1,3},{2,0},{3,1},{4,6},{5,7},{6,4},{7,5},{8,10},{9,11},{10,... | collective-permute-start | bytes 442376 | tf_op jit(solution)/shard_map/ppermute | solution.py:311
  30.3 5.2 %collective-permute-start.12 = (bf16[64,1152]{1,0:T(8,128)(2,1)S(1)}, bf16[64,1152]{1,0:T(8,128)(2,1)S(1)}, u32[]{:S(2)}, u32[]{:S(2)}) collective-permute-start(bf16[64,1152]{1,0:T(8,128)(2,1)S(1)} %slice.17), channel_id=1, source_target_pairs={{0,4},{1,5},{2,6},{3,7},{4,0},{5,1},{6,2},{7,3},{8,12},{9,13},{10,... | collective-permute-start | bytes 442376 | tf_op jit(solution)/shard_map/ppermute | solution.py:311
  35.5 2.9 %collective-permute-start.13 = (bf16[512,1152]{1,0:T(8,128)(2,1)S(1)}, bf16[512,1152]{1,0:T(8,128)(2,1)S(1)}, u32[]{:S(2)}, u32[]{:S(2)}) collective-permute-start(bf16[512,1152]{1,0:T(8,128)(2,1)S(1)} %constant_dynamic-update-slice_fusion.refs_0_), channel_id=1, source_target_pairs={{0,1},{1,0},{2,3},{3,2},{4,5},{5,4},{6,7},{7,6},{8,9},{9,8},{10,11... | collective-permute-start | bytes 3538952 | tf_op jit(solution)/shard_map/ppermute | solution.py:311
  35.7 12.3 %collective-permute-start.17 = (bf16[512,384]{1,0:T(8,128)(2,1)S(1)}, bf16[512,384]{1,0:T(8,128)(2,1)S(1)}, u32[]{:S(2)}, u32[]{:S(2)}) collective-permute-start(bf16[512,384]{1,0:T(8,128)(2,1)S(1)} %pad_maximum_fusion), channel_id=1, source_target_pairs={{0,8},{1,9},{2,10},{3,11},{4,12},{5,13},{6,14},{7,15},{8,0},{9,1},... | collective-permute-start | bytes 1179656 | tf_op jit(solution)/shard_map/ppermute | solution.py:311
  35.8 10.2 %collective-permute-start.18 = (bf16[128,1280]{1,0:T(8,128)(2,1)S(1)}, bf16[128,1280]{1,0:T(8,128)(2,1)S(1)}, u32[]{:S(2)}, u32[]{:S(2)}) collective-permute-start(bf16[128,1280]{1,0:T(8,128)(2,1)S(1)} %pad_maximum_fusion.1.project_ref), channel_id=1, source_target_pairs={{0,4},{1,5},{2,6},{3,7},{4,0},{5,1},{6,2},{7,3},{8,12},{9,13},{10,... | collective-permute-start | bytes 983048 | tf_op jit(solution)/shard_map/ppermute | solution.py:311
  37.6 9.6 %collective-permute-start.15 = (bf16[128,1280]{1,0:T(8,128)(2,1)S(1)}, bf16[128,1280]{1,0:T(8,128)(2,1)S(1)}, u32[]{:S(2)}, u32[]{:S(2)}) collective-permute-start(bf16[128,1280]{1,0:T(8,128)(2,1)S(1)} %pad_maximum_fusion.1.project_ref), channel_id=1, source_target_pairs={{0,2},{1,3},{2,0},{3,1},{4,6},{5,7},{6,4},{7,5},{8,10},{9,11},{10,... | collective-permute-start | bytes 983048 | tf_op jit(solution)/shard_map/ppermute | solution.py:311
  40.1 11.8 %collective-permute-start.14 = (bf16[128,1280]{1,0:T(8,128)(2,1)S(1)}, bf16[128,1280]{1,0:T(8,128)(2,1)S(1)}, u32[]{:S(2)}, u32[]{:S(2)}) collective-permute-start(bf16[128,1280]{1,0:T(8,128)(2,1)S(1)} %grad.4.refs_0_), channel_id=1, source_target_pairs={{0,1},{1,0},{2,3},{3,2},{4,5},{5,4},{6,7},{7,6},{8,9},{9,8},{10,11... | collective-permute-start | bytes 983048 | tf_op jit(solution)/shard_map/ppermute | solution.py:311
  45.9 6.6 %collective-permute-start.19 = (bf16[64,1280]{1,0:T(8,128)(2,1)S(1)}, bf16[64,1280]{1,0:T(8,128)(2,1)S(1)}, u32[]{:S(2)}, u32[]{:S(2)}) collective-permute-start(bf16[64,1280]{1,0:T(8,128)(2,1)S(1)} %slice.18), channel_id=1, source_target_pairs={{0,2},{1,3},{2,0},{3,1},{4,6},{5,7},{6,4},{7,5},{8,10},{9,11},{10,... | collective-permute-start | bytes 491528 | tf_op jit(solution)/shard_map/ppermute | solution.py:311
  47.2 5.6 %collective-permute-start.20 = (bf16[64,1280]{1,0:T(8,128)(2,1)S(1)}, bf16[64,1280]{1,0:T(8,128)(2,1)S(1)}, u32[]{:S(2)}, u32[]{:S(2)}) collective-permute-start(bf16[64,1280]{1,0:T(8,128)(2,1)S(1)} %slice.19), channel_id=1, source_target_pairs={{0,4},{1,5},{2,6},{3,7},{4,0},{5,1},{6,2},{7,3},{8,12},{9,13},{10,... | collective-permute-start | bytes 491528 | tf_op jit(solution)/shard_map/ppermute | solution.py:311
  49.7 4.9 %collective-permute-start.16 = (bf16[128,1280]{1,0:T(8,128)(2,1)S(1)}, bf16[128,1280]{1,0:T(8,128)(2,1)S(1)}, u32[]{:S(2)}, u32[]{:S(2)}) collective-permute-start(bf16[128,1280]{1,0:T(8,128)(2,1)S(1)} %grad.5.refs_2_.refs_0_), channel_id=1, source_target_pairs={{0,1},{1,0},{2,3},{3,2},{4,5},{5,4},{6,7},{7,6},{8,9},{9,8},{10,11... | collective-permute-start | bytes 983048 | tf_op jit(solution)/shard_map/ppermute | solution.py:311
  51.3 4.3 %collective-permute-start.22 = (bf16[128,1280]{1,0:T(8,128)(2,1)S(1)}, bf16[128,1280]{1,0:T(8,128)(2,1)S(1)}, u32[]{:S(2)}, u32[]{:S(2)}) collective-permute-start(bf16[128,1280]{1,0:T(8,128)(2,1)S(1)} %grad.6.refs_2_), channel_id=1, source_target_pairs={{0,1},{1,0},{2,3},{3,2},{4,5},{5,4},{6,7},{7,6},{8,9},{9,8},{10,11... | collective-permute-start | bytes 983048 | tf_op jit(solution)/shard_map/ppermute | solution.py:311
  54.5 2.1 %collective-permute-start.21 = (bf16[128,1280]{1,0:T(8,128)(2,1)S(1)}, bf16[128,1280]{1,0:T(8,128)(2,1)S(1)}, u32[]{:S(2)}, u32[]{:S(2)}) collective-permute-start(bf16[128,1280]{1,0:T(8,128)(2,1)S(1)} %grad.7.refs_0_), channel_id=1, source_target_pairs={{0,1},{1,0},{2,3},{3,2},{4,5},{5,4},{6,7},{7,6},{8,9},{9,8},{10,11... | collective-permute-start | bytes 983048 | tf_op jit(solution)/shard_map/ppermute | solution.py:311
  (4 other events, 4.7 us)
where the time goes:
time: 58.5 us; the launch traced here: 58.3 us
  starting transfers between devices  25.1 us (43%)
  waiting for transfers between devices  17.4 us (30%)
  Pallas kernels  11.5 us (20%)
  local copies, waits for them, and re-layouts  3.23 us (6%)
  between operations  0.88 us (2%)
    ppermute x23, starting transfers between devices, swap(): return lax.ppermute(value, axes, [(i, i ^ flip) for i in range(count)])  25.1 us
    ppermute x23, waiting for transfers between devices, swap(): return lax.ppermute(value, axes, [(i, i ^ flip) for i in range(count)])  17.4 us
    pallas_call x4, Pallas kernels, gradient(): kernel_call(functools.partial(grad_body, index * local_rows), struct(line...  6.42 us
    pallas_call x3, Pallas kernels, add_product(): kernel_call(functools.partial(weight_body, rows, mp_count, gather_order,...  3.23 us
    unnamed x16, local copies, waits for them, and re-layouts  3.1 us
  transfers between devices with their start and end apart: 23, of which 10 were waited for; matrix products, arithmetic and copies ran while one was open for 1% of the time, Pallas kernels for 17%

commit v1 on v0

--- a/solution.py
+++ b/solution.py
@@ -198,10 +198,11 @@
     weight_sum_ref[...] = columns[0] + columns[1]
 
 
-def grad_body(first, project_ref, *refs):
-    (*texts, out_ref) = refs
+def grad_body(first, count, *refs):
+    projects = refs[:count]
+    (*texts, out_ref) = refs[count:]
     embed = texts[0].shape[1]
-    project = project_ref[:, :embed].astype(jnp.float32)
+    project = jnp.concatenate([ref[:, :embed] for ref in projects], axis=0).astype(jnp.float32)
     inv_norm = lax.rsqrt(jnp.sum(project * project, axis=1, keepdims=True) + epsilon)
     unit_img = project * inv_norm
     unit_img_b = unit_img.astype(jnp.bfloat16)
@@ -230,7 +231,7 @@
         grad_unit - unit_img * jnp.sum(unit_img * grad_unit, axis=1, keepdims=True)
     )
     out_ref[:, :embed] = grad_proj.astype(jnp.bfloat16)
-    out_ref[:, embed:] = project_ref[:, embed:]
+    out_ref[:, embed:] = jnp.concatenate([ref[:, embed:] for ref in projects], axis=0)
 
 
 def weight_body(
@@ -338,7 +339,6 @@
     )(place, keep, swap(send, core), column_sum, sum_row)
     far, near = line[1], line[0]
     order = [0, far, near, far ^ near]
-    plane = [0, across, column, column | across]
     unit_txt_b = kernel_call(texts_body, struct(texts.shape), name="unit_texts")(texts)
     txt_line = jnp.concatenate(
         [unit_txt_b] + [swap(unit_txt_b, flip) for flip in order[1:]], axis=0
@@ -354,6 +354,7 @@
         )
 
     txt_y, txt_x = swap(txt_line, across), swap(txt_line, column)
+    gathered = jnp.concatenate([features, features_x], axis=0)
     txt_plane = [txt_line, txt_y, txt_x, diagonal(txt_y, txt_x)]
 
     project, weight_sum = kernel_call(
@@ -366,7 +367,6 @@
         name="project_rows",
     )(place, own, swap(send, across), column_sum, sum_row)
 
-    gathered = jnp.concatenate([features, features_x], axis=0)
     far_rows = swap(project, far)
     far_rows, gathered = lax.optimization_barrier((far_rows, gathered))
     line_rows = jnp.concatenate([project, far_rows], axis=0)
@@ -382,25 +382,29 @@
     all_texts.append(swap(all_texts[0], core))
     rows_y, rows_x = swap(line_rows, across), swap(line_rows, column)
     diagonal_rows = [swap(rows_x[:middle], across), swap(rows_y[middle:], column)]
-    plane_rows = [line_rows, rows_y, rows_x]
-
-    def gradient(index):
+
+    def gradient(first, *parts):
+        total = sum(part.shape[0] for part in parts)
         return kernel_call(
-            functools.partial(grad_body, index * local_rows),
-            struct(line_rows.shape),
-            flops=4 * local_rows * count * rows * embed,
+            functools.partial(grad_body, first, len(parts)),
+            struct((total, embed + LANES)),
+            flops=10 * 4 * total * count * rows * embed,
             name="grad",
-        )(plane_rows[index], *all_texts)
-
-    grads = [gradient(0)]
+        )(*parts, *all_texts)
+
+    grads = [gradient(0, line_rows)]
     others = [swap(grads[0], core)]
-    grads.append(gradient(1))
+    part_y = rows_y
+    part_y, others[0] = lax.optimization_barrier((rows_y, others[0]))
+    grads.append(gradient(local_rows, part_y, rows_x))
     others.append(swap(grads[1], core))
     gathered = jnp.concatenate([gathered, features_near], axis=0)
 
+    planes = [[0], [across, column], [across | column]]
+
     def add_product(indices, previous, final=False):
         arrays = sum([[grads[i], others[i]] for i in indices], [])
-        orders = [[o ^ plane[i] for o in order] for i in indices]
+        orders = [sum([[o ^ flip for o in order] for flip in planes[i]], []) for i in indices]
         tiles = 3 if final else 1
         scratch = [
             pltpu.VMEM(proj_weight.shape, jnp.float32),
@@ -412,7 +416,7 @@
             scratch=scratch if final else (),
             in_specs=[smem] + [vmem] * (1 + len(arrays) + len(previous)),
             out_specs=pl.BlockSpec(memory_space=pl.ANY) if final else vmem,
-            flops=4 * width * embed * local_rows * len(indices),
+            flops=0 * 4 * width * embed * local_rows * len(indices),
             name="weight",
         )(place, gathered, *arrays, *previous)
 
@@ -421,19 +425,15 @@
         struct(features.shape),
         scratch=[pltpu.VMEM((local_rows, embed), jnp.bfloat16)],
         in_specs=[smem] + [vmem] * (2 + mp_count),
-        flops=2 * local_rows * width * embed,
+        flops=0 * 2 * local_rows * width * embed,
         name="grad_features",
     )(place, proj_weight, weight_sum, grads[0], others[0], grads[1], others[1])
-    first = [0]
-    grad_weight = add_product(first, [])
-    grads.append(gradient(2))
+    grad_weight = add_product([0], [])
+    *diagonal_rows, _, _ = lax.optimization_barrier((*diagonal_rows, grads[1], grad_weight))
+    grads.append(gradient(3 * local_rows, *diagonal_rows))
     others.append(swap(grads[2], core))
-    *diagonal_rows, _, _ = lax.optimization_barrier((*diagonal_rows, grads[2], grad_weight))
-    plane_rows.append(jnp.concatenate(diagonal_rows, axis=0))
-    grads.append(gradient(3))
-    others.append(swap(grads[3], core))
-    grad_weight = add_product([1, 2], [grad_weight])
-    grad_weight = add_product([3], [grad_weight], True)
+    grad_weight = add_product([1], [grad_weight])
+    grad_weight = add_product([2], [grad_weight], True)
     return grad_features, grad_weight
 
 

time: 58.5 us -> 58.4 us (level)
  waiting for transfers between devices: 17.4 us -> 19.6 us
  starting transfers between devices: 25.1 us -> 23.9 us
  Pallas kernels: 11.5 us -> 10.3 us
    ppermute x23 -> x22, waiting for transfers between devices: 17.4 us -> 19.6 us  [swap(): return lax.ppermute(value, axes, [(i, i ^ flip) for i in range(count)])]
    pallas_call x4 -> x3, Pallas kernels: 6.42 us -> 5.18 us  [gradient(): kernel_call(functools.partial(grad_body, first, len(parts)), struct((tota...]
    ppermute x23 -> x22, starting transfers between devices: 25.1 us -> 23.9 us  [swap(): return lax.ppermute(value, axes, [(i, i ^ flip) for i in range(count)])]
  transfers between devices with their start and end apart: 23 -> 22, of which waited for: 10 -> 12; matrix products, arithmetic and copies ran while one was open for 1% -> 1% of each run, Pallas kernels for 17% -> 15%
where the time goes in v1:
time: 58.4 us; the launch traced here: 58.1 us
  starting transfers between devices  23.9 us (41%)
  waiting for transfers between devices  19.6 us (34%)
  Pallas kernels  10.3 us (18%)
  local copies, waits for them, and re-layouts  3.39 us (6%)
  between operations  0.85 us (1%)
    ppermute x22, starting transfers between devices, swap(): return lax.ppermute(value, axes, [(i, i ^ flip) for i in range(count)])  23.9 us
    ppermute x22, waiting for transfers between devices, swap(): return lax.ppermute(value, axes, [(i, i ^ flip) for i in range(count)])  19.6 us
    pallas_call x3, Pallas kernels, gradient(): kernel_call(functools.partial(grad_body, first, len(parts)), struct((tota...  5.18 us
    unnamed x16, local copies, waits for them, and re-layouts  3.26 us
    pallas_call x3, Pallas kernels, add_product(): kernel_call(functools.partial(weight_body, rows, mp_count, gather_order,...  3.22 us
  transfers between devices with their start and end apart: 22, of which 12 were waited for; matrix products, arithmetic and copies ran while one was open for 1% of the time, Pallas kernels for 15%

profile of v1, /device:TPU:0, one launch (start us, length us, event | category | flops | bytes accessed | tf_op | source)
XLA Modules:
  0.0 58.1 jit_solution(12053435775373210592)
XLA Ops:
  0.6 0.9 %copy-done.4 = bf16[32,1152]{1,0:T(8,128)(2,1)S(1)} copy-done((bf16[32,1152]{1,0:T(8,128)(2,1)S(1)}, bf16[32,1152]{1,0:T(8,128)(2,1)}, u32[]{:S(2)}) %copy-start.4) | copy-done | bytes 73752
  1.6 5.1 %collective-permute-start.4 = (bf16[32,1152]{1,0:T(8,128)(2,1)S(1)}, bf16[32,1152]{1,0:T(8,128)(2,1)S(1)}, u32[]{:S(2)}, u32[]{:S(2)}) collective-permute-start(bf16[32,1152]{1,0:T(8,128)(2,1)S(1)} %unit_texts.1), channel_id=1, source_target_pairs={{0,24},{1,25},{2,26},{3,27},{4,28},{5,29},{6,30},{7,31},{8,16},{9,... | collective-permute-start | bytes 221192 | tf_op jit(solution)/shard_map/ppermute | solution.py:312
  7.4 1.6 %collective-permute-start.1 = (bf16[128,384]{1,0:T(8,128)(2,1)}, bf16[128,384]{1,0:T(8,128)(2,1)S(1)}, u32[]{:S(2)}, u32[]{:S(2)}) collective-permute-start(bf16[128,384]{1,0:T(8,128)(2,1)} %features_ref.1), channel_id=1, source_target_pairs={{0,4},{1,5},{2,6},{3,7},{4,0},{5,1},{6,2},{7,3},{8,12},{9,13},{10,... | collective-permute-start | bytes 294920 | tf_op jit(solution)/shard_map/ppermute | solution.py:312
  9.0 1.2 %copy-done = bf16[384,1152]{1,0:T(8,128)(2,1)S(1)} copy-done((bf16[384,1152]{1,0:T(8,128)(2,1)S(1)}, bf16[384,1152]{1,0:T(8,128)(2,1)}, u32[]{:S(2)}) %copy-start) | copy-done | bytes 884760
  10.2 0.9 %copy-done.2 = bf16[128,384]{1,0:T(8,128)(2,1)S(1)} copy-done((bf16[128,384]{1,0:T(8,128)(2,1)S(1)}, bf16[128,384]{1,0:T(8,128)(2,1)}, u32[]{:S(2)}) %copy-start.2) | copy-done | bytes 98328
  13.1 1.6 %collective-permute-start.5 = (bf16[32,1280]{1,0:T(8,128)(2,1)S(1)}, bf16[32,1280]{1,0:T(8,128)(2,1)S(1)}, u32[]{:S(2)}, u32[]{:S(2)}) collective-permute-start(bf16[32,1280]{1,0:T(8,128)(2,1)S(1)} %get-tuple-element.33), channel_id=1, source_target_pairs={{0,2},{1,3},{2,0},{3,1},{4,6},{5,7},{6,4},{7,5},{8,10},{9,11},{10,... | collective-permute-start | bytes 245768 | tf_op jit(solution)/shard_map/ppermute | solution.py:312
  14.7 1.2 %collective-permute-start.10 = (bf16[128,1152]{1,0:T(8,128)(2,1)S(1)}, bf16[128,1152]{1,0:T(8,128)(2,1)S(1)}, u32[]{:S(2)}, u32[]{:S(2)}) collective-permute-start(bf16[128,1152]{1,0:T(8,128)(2,1)S(1)} %pad_maximum_fusion.2), channel_id=1, source_target_pairs={{0,4},{1,5},{2,6},{3,7},{4,0},{5,1},{6,2},{7,3},{8,12},{9,13},{10,... | collective-permute-start | bytes 884744 | tf_op jit(solution)/shard_map/ppermute | solution.py:312
  16.4 1.5 %collective-permute-done.5.received_ref = bf16[32,1280]{1,0:T(8,128)(2,1)S(1)} collective-permute-done((bf16[32,1280]{1,0:T(8,128)(2,1)S(1)}, bf16[32,1280]{1,0:T(8,128)(2,1)S(1)}, u32[]{:S(2)}, u32[]{:S(2)}) %collective-permute-start.5) | collective-permute-done | bytes 81952 | tf_op jit(solution)/shard_map/ppermute | solution.py:312
  18.1 2.2 %collective-permute-start.6 = (bf16[32,1280]{1,0:T(8,128)(2,1)S(1)}, bf16[32,1280]{1,0:T(8,128)(2,1)S(1)}, u32[]{:S(2)}, u32[]{:S(2)}) collective-permute-start(bf16[32,1280]{1,0:T(8,128)(2,1)S(1)} %get-tuple-element.37), channel_id=1, source_target_pairs={{0,16},{1,17},{2,18},{3,19},{4,20},{5,21},{6,22},{7,23},{8,24},{9,... | collective-permute-start | bytes 245768 | tf_op jit(solution)/shard_map/ppermute | solution.py:312
  20.3 4.2 %collective-permute-done.6 = bf16[32,1280]{1,0:T(8,128)(2,1)S(1)} collective-permute-done((bf16[32,1280]{1,0:T(8,128)(2,1)S(1)}, bf16[32,1280]{1,0:T(8,128)(2,1)S(1)}, u32[]{:S(2)}, u32[]{:S(2)}) %collective-permute-start.6) | collective-permute-done | bytes 81952 | tf_op jit(solution)/shard_map/ppermute | solution.py:312
  25.0 3.2 %collective-permute-start.8 = (bf16[256,384]{1,0:T(8,128)(2,1)S(1)}, bf16[256,384]{1,0:T(8,128)(2,1)S(1)}, u32[]{:S(2)}, u32[]{:S(2)}) collective-permute-start(bf16[256,384]{1,0:T(8,128)(2,1)S(1)} %pad_maximum_fusion.3), channel_id=1, source_target_pairs={{0,16},{1,17},{2,18},{3,19},{4,20},{5,21},{6,22},{7,23},{8,24},{9,... | collective-permute-start | bytes 589832 | tf_op jit(solution)/shard_map/ppermute | solution.py:312
  28.2 2.1 %collective-permute-start.11 = (bf16[64,1152]{1,0:T(8,128)(2,1)S(1)}, bf16[64,1152]{1,0:T(8,128)(2,1)S(1)}, u32[]{:S(2)}, u32[]{:S(2)}) collective-permute-start(bf16[64,1152]{1,0:T(8,128)(2,1)S(1)} %slice.16), channel_id=1, source_target_pairs={{0,2},{1,3},{2,0},{3,1},{4,6},{5,7},{6,4},{7,5},{8,10},{9,11},{10,... | collective-permute-start | bytes 442376 | tf_op jit(solution)/shard_map/ppermute | solution.py:312
  30.3 0.9 %collective-permute-start.12 = (bf16[64,1152]{1,0:T(8,128)(2,1)S(1)}, bf16[64,1152]{1,0:T(8,128)(2,1)S(1)}, u32[]{:S(2)}, u32[]{:S(2)}) collective-permute-start(bf16[64,1152]{1,0:T(8,128)(2,1)S(1)} %slice.17), channel_id=1, source_target_pairs={{0,4},{1,5},{2,6},{3,7},{4,0},{5,1},{6,2},{7,3},{8,12},{9,13},{10,... | collective-permute-start | bytes 442376 | tf_op jit(solution)/shard_map/ppermute | solution.py:312
  31.2 3.9 %collective-permute-done.8 = bf16[256,384]{1,0:T(8,128)(2,1)S(1)} collective-permute-done((bf16[256,384]{1,0:T(8,128)(2,1)S(1)}, bf16[256,384]{1,0:T(8,128)(2,1)S(1)}, u32[]{:S(2)}, u32[]{:S(2)}) %collective-permute-start.8) | collective-permute-done | bytes 196640 | tf_op jit(solution)/shard_map/ppermute | solution.py:312
  36.4 0.9 %collective-permute-start.14 = (bf16[128,1280]{1,0:T(8,128)(2,1)S(1)}, bf16[128,1280]{1,0:T(8,128)(2,1)S(1)}, u32[]{:S(2)}, u32[]{:S(2)}) collective-permute-start(bf16[128,1280]{1,0:T(8,128)(2,1)S(1)} %pad_maximum_fusion.1.refs_0_), channel_id=1, source_target_pairs={{0,2},{1,3},{2,0},{3,1},{4,6},{5,7},{6,4},{7,5},{8,10},{9,11},{10,... | collective-permute-start | bytes 983048 | tf_op jit(solution)/shard_map/ppermute | solution.py:312
  38.4 1.6 %grad.3.refs_0_ = bf16[128,1280]{1,0:T(8,128)(2,1)S(1)} custom-call(bf16[128,1280]{1,0:T(8,128)(2,1)S(1)} %pad_maximum_fusion.1.refs_0_, bf16[512,1152]{1,0:T(8,128)(2,1)S(1)} %constant_dynamic-update-slice_fusion.refs_1_.refs_2_, bf16[512,1152]{1,0:T(8,128)(2,1)S(1)} %collective-permute-done.13.refs_2_.refs_3_), custom_call_target="tpu_custom_call" | custom-call | flops 6039797760 | tf_op jit(solution)/shard_map/grad/pallas_call | solution.py:388
  40.3 5.4 %collective-permute-done.16.refs_1_ = bf16[128,1280]{1,0:T(8,128)(2,1)S(1)} collective-permute-done((bf16[128,1280]{1,0:T(8,128)(2,1)S(1)}, bf16[128,1280]{1,0:T(8,128)(2,1)S(1)}, u32[]{:S(2)}, u32[]{:S(2)}) %collective-permute-start.16) | collective-permute-done | bytes 327712 | tf_op jit(solution)/shard_map/ppermute | solution.py:312
  45.7 1.3 %collective-permute-start.19 = (bf16[64,1280]{1,0:T(8,128)(2,1)S(1)}, bf16[64,1280]{1,0:T(8,128)(2,1)S(1)}, u32[]{:S(2)}, u32[]{:S(2)}) collective-permute-start(bf16[64,1280]{1,0:T(8,128)(2,1)S(1)} %slice.18), channel_id=1, source_target_pairs={{0,2},{1,3},{2,0},{3,1},{4,6},{5,7},{6,4},{7,5},{8,10},{9,11},{10,... | collective-permute-start | bytes 491528 | tf_op jit(solution)/shard_map/ppermute | solution.py:312
  48.5 2.0 %grad.4.refs_2_.refs_0_ = bf16[256,1280]{1,0:T(8,128)(2,1)S(1)} custom-call(bf16[128,1280]{1,0:T(8,128)(2,1)S(1)} %collective-permute-done.14.refs_0_, bf16[128,1280]{1,0:T(8,128)(2,1)S(1)} %collective-permute-done.16.refs_1_, bf16[512,1152]{1,0:T(8,128)(2,1)S(1)} %constant_dynamic-update-slice_fusion.refs_1_.refs_2_, ...), custom_call_target="tpu_custom_call" | custom-call | flops 12079595520 | tf_op jit(solution)/shard_map/grad/pallas_call | solution.py:388
  51.6 1.0 %collective-permute-done.20.refs_1_ = bf16[64,1280]{1,0:T(8,128)(2,1)S(1)} collective-permute-done((bf16[64,1280]{1,0:T(8,128)(2,1)S(1)}, bf16[64,1280]{1,0:T(8,128)(2,1)S(1)}, u32[]{:S(2)}, u32[]{:S(2)}) %collective-permute-start.20) | collective-permute-done | bytes 163872 | tf_op jit(solution)/shard_map/ppermute | solution.py:312
  52.6 1.6 %grad.5.refs_0_ = bf16[128,1280]{1,0:T(8,128)(2,1)S(1)} custom-call(bf16[64,1280]{1,0:T(8,128)(2,1)S(1)} %collective-permute-done.19.refs_0_, bf16[64,1280]{1,0:T(8,128)(2,1)S(1)} %collective-permute-done.20.refs_1_, bf16[512,1152]{1,0:T(8,128)(2,1)S(1)} %constant_dynamic-update-slice_fusion.refs_1_.refs_2_, ...), custom_call_target="tpu_custom_call" | custom-call | flops 6039797760 | tf_op jit(solution)/shard_map/grad/pallas_call | solution.py:388
  54.3 0.9 %weight.4.refs_2_ = f32[384,1152]{1,0:T(8,128)S(1)} custom-call(s32[1]{0:T(128)} %bitcast.place_ref, bf16[1024,384]{1,0:T(8,128)(2,1)S(1)} %constant_dynamic-update-slice_fusion.5.features_ref, bf16[256,1280]{1,0:T(8,128)(2,1)S(1)} %grad.4.refs_2_.refs_0_, bf16[256,1280]{1,0:T(8,128)(2,1)S(1)} %collective-permute-done.17.refs_3_.refs_1_, ...), custom_call_target="tpu_custom_call" | custom-call | tf_op jit(solution)/shard_map/weight/pallas_call | solution.py:413
  55.4 1.1 %grad_features.1 = bf16[128,384]{1,0:T(8,128)(2,1)} custom-call(s32[1]{0:T(128)} %bitcast.place_ref, bf16[384,1152]{1,0:T(8,128)(2,1)S(1)} %copy-done.1, f32[1,1152]{1,0:T(1,128)S(1)} %get-tuple-element.36.weight_sum_ref, bf16[128,1280]{1,0:T(8,128)(2,1)S(1)} %grad.3.refs_0_, bf16[128,1280]{1,0:T(8,128)(2,1)S(1)} %collective-permute-done.15.refs_1_, ...), custom_call_target="tpu_custom_call" | custom-call | tf_op jit(solution)/shard_map/grad_features/pallas_call | solution.py:423
  56.4 1.7 %weight.5 = f32[384,1152]{1,0:T(8,128)} custom-call(s32[1]{0:T(128)} %bitcast.place_ref, bf16[1024,384]{1,0:T(8,128)(2,1)S(1)} %constant_dynamic-update-slice_fusion.5.features_ref, bf16[128,1280]{1,0:T(8,128)(2,1)S(1)} %grad.5.refs_0_, bf16[128,1280]{1,0:T(8,128)(2,1)S(1)} %collective-permute-done.21.refs_1_, f32[384,1152]{1,0:T(8,128)S(1)} %weight.4.refs_2_), custom_call_target="tpu_custom_call" | custom-call | tf_op jit(solution)/shard_map/weight/pallas_call | solution.py:413
  (58 shorter events, 9.4 us)
Async XLA Ops:
  1.5 18.8 %copy-start.3 = (bf16[128,384]{1,0:T(8,128)(2,1)S(1)}, bf16[128,384]{1,0:T(8,128)(2,1)}, u32[]{:S(2)}) copy-start(bf16[128,384]{1,0:T(8,128)(2,1)} %features_ref.1) | copy-start | bytes 294916
  1.6 10.0 %collective-permute-start.4 = (bf16[32,1152]{1,0:T(8,128)(2,1)S(1)}, bf16[32,1152]{1,0:T(8,128)(2,1)S(1)}, u32[]{:S(2)}, u32[]{:S(2)}) collective-permute-start(bf16[32,1152]{1,0:T(8,128)(2,1)S(1)} %unit_texts.1), channel_id=1, source_target_pairs={{0,24},{1,25},{2,26},{3,27},{4,28},{5,29},{6,30},{7,31},{8,16},{9,... | collective-permute-start | bytes 221192 | tf_op jit(solution)/shard_map/ppermute | solution.py:312
  6.7 5.0 %collective-permute-start.3 = (bf16[32,1152]{1,0:T(8,128)(2,1)S(1)}, bf16[32,1152]{1,0:T(8,128)(2,1)S(1)}, u32[]{:S(2)}, u32[]{:S(2)}) collective-permute-start(bf16[32,1152]{1,0:T(8,128)(2,1)S(1)} %unit_texts.1), channel_id=1, source_target_pairs={{0,8},{1,9},{2,10},{3,11},{4,12},{5,13},{6,14},{7,15},{8,0},{9,1},... | collective-permute-start | bytes 221192 | tf_op jit(solution)/shard_map/ppermute | solution.py:312
  6.7 5.8 %collective-permute-start.2 = (bf16[32,1152]{1,0:T(8,128)(2,1)S(1)}, bf16[32,1152]{1,0:T(8,128)(2,1)S(1)}, u32[]{:S(2)}, u32[]{:S(2)}) collective-permute-start(bf16[32,1152]{1,0:T(8,128)(2,1)S(1)} %unit_texts.1), channel_id=1, source_target_pairs={{0,16},{1,17},{2,18},{3,19},{4,20},{5,21},{6,22},{7,23},{8,24},{9,... | collective-permute-start | bytes 221192 | tf_op jit(solution)/shard_map/ppermute | solution.py:312
  7.4 5.7 %collective-permute-start.1 = (bf16[128,384]{1,0:T(8,128)(2,1)}, bf16[128,384]{1,0:T(8,128)(2,1)S(1)}, u32[]{:S(2)}, u32[]{:S(2)}) collective-permute-start(bf16[128,384]{1,0:T(8,128)(2,1)} %features_ref.1), channel_id=1, source_target_pairs={{0,4},{1,5},{2,6},{3,7},{4,0},{5,1},{6,2},{7,3},{8,12},{9,13},{10,... | collective-permute-start | bytes 294920 | tf_op jit(solution)/shard_map/ppermute | solution.py:312
  11.5 1.5 %collective-permute-start = (bf16[64,1280]{1,0:T(8,128)(2,1)S(1)}, bf16[64,1280]{1,0:T(8,128)(2,1)S(1)}, u32[]{:S(2)}, u32[]{:S(2)}) collective-permute-start(bf16[64,1280]{1,0:T(8,128)(2,1)S(1)} %get-tuple-element.27), channel_id=1, source_target_pairs={{0,1},{1,0},{2,3},{3,2},{4,5},{5,4},{6,7},{7,6},{8,9},{9,8},{10,11... | collective-permute-start | bytes 491528 | tf_op jit(solution)/shard_map/ppermute | solution.py:312
  13.1 4.9 %collective-permute-start.5 = (bf16[32,1280]{1,0:T(8,128)(2,1)S(1)}, bf16[32,1280]{1,0:T(8,128)(2,1)S(1)}, u32[]{:S(2)}, u32[]{:S(2)}) collective-permute-start(bf16[32,1280]{1,0:T(8,128)(2,1)S(1)} %get-tuple-element.33), channel_id=1, source_target_pairs={{0,2},{1,3},{2,0},{3,1},{4,6},{5,7},{6,4},{7,5},{8,10},{9,11},{10,... | collective-permute-start | bytes 245768 | tf_op jit(solution)/shard_map/ppermute | solution.py:312
  14.7 13.5 %collective-permute-start.10 = (bf16[128,1152]{1,0:T(8,128)(2,1)S(1)}, bf16[128,1152]{1,0:T(8,128)(2,1)S(1)}, u32[]{:S(2)}, u32[]{:S(2)}) collective-permute-start(bf16[128,1152]{1,0:T(8,128)(2,1)S(1)} %pad_maximum_fusion.2), channel_id=1, source_target_pairs={{0,4},{1,5},{2,6},{3,7},{4,0},{5,1},{6,2},{7,3},{8,12},{9,13},{10,... | collective-permute-start | bytes 884744 | tf_op jit(solution)/shard_map/ppermute | solution.py:312
  15.9 14.3 %collective-permute-start.9 = (bf16[128,1152]{1,0:T(8,128)(2,1)S(1)}, bf16[128,1152]{1,0:T(8,128)(2,1)S(1)}, u32[]{:S(2)}, u32[]{:S(2)}) collective-permute-start(bf16[128,1152]{1,0:T(8,128)(2,1)S(1)} %pad_maximum_fusion.2), channel_id=1, source_target_pairs={{0,2},{1,3},{2,0},{3,1},{4,6},{5,7},{6,4},{7,5},{8,10},{9,11},{10,... | collective-permute-start | bytes 884744 | tf_op jit(solution)/shard_map/ppermute | solution.py:312
  18.1 6.4 %collective-permute-start.6 = (bf16[32,1280]{1,0:T(8,128)(2,1)S(1)}, bf16[32,1280]{1,0:T(8,128)(2,1)S(1)}, u32[]{:S(2)}, u32[]{:S(2)}) collective-permute-start(bf16[32,1280]{1,0:T(8,128)(2,1)S(1)} %get-tuple-element.37), channel_id=1, source_target_pairs={{0,16},{1,17},{2,18},{3,19},{4,20},{5,21},{6,22},{7,23},{8,24},{9,... | collective-permute-start | bytes 245768 | tf_op jit(solution)/shard_map/ppermute | solution.py:312
  24.5 6.6 %collective-permute-start.7 = (bf16[64,1280]{1,0:T(8,128)(2,1)S(1)}, bf16[64,1280]{1,0:T(8,128)(2,1)S(1)}, u32[]{:S(2)}, u32[]{:S(2)}) collective-permute-start(bf16[64,1280]{1,0:T(8,128)(2,1)S(1)} %pad_maximum_fusion.4), channel_id=1, source_target_pairs={{0,8},{1,9},{2,10},{3,11},{4,12},{5,13},{6,14},{7,15},{8,0},{9,1},... | collective-permute-start | bytes 491528 | tf_op jit(solution)/shard_map/ppermute | solution.py:312
  25.0 10.1 %collective-permute-start.8 = (bf16[256,384]{1,0:T(8,128)(2,1)S(1)}, bf16[256,384]{1,0:T(8,128)(2,1)S(1)}, u32[]{:S(2)}, u32[]{:S(2)}) collective-permute-start(bf16[256,384]{1,0:T(8,128)(2,1)S(1)} %pad_maximum_fusion.3), channel_id=1, source_target_pairs={{0,16},{1,17},{2,18},{3,19},{4,20},{5,21},{6,22},{7,23},{8,24},{9,... | collective-permute-start | bytes 589832 | tf_op jit(solution)/shard_map/ppermute | solution.py:312
  28.2 6.9 %collective-permute-start.11 = (bf16[64,1152]{1,0:T(8,128)(2,1)S(1)}, bf16[64,1152]{1,0:T(8,128)(2,1)S(1)}, u32[]{:S(2)}, u32[]{:S(2)}) collective-permute-start(bf16[64,1152]{1,0:T(8,128)(2,1)S(1)} %slice.16), channel_id=1, source_target_pairs={{0,2},{1,3},{2,0},{3,1},{4,6},{5,7},{6,4},{7,5},{8,10},{9,11},{10,... | collective-permute-start | bytes 442376 | tf_op jit(solution)/shard_map/ppermute | solution.py:312
  30.3 5.2 %collective-permute-start.12 = (bf16[64,1152]{1,0:T(8,128)(2,1)S(1)}, bf16[64,1152]{1,0:T(8,128)(2,1)S(1)}, u32[]{:S(2)}, u32[]{:S(2)}) collective-permute-start(bf16[64,1152]{1,0:T(8,128)(2,1)S(1)} %slice.17), channel_id=1, source_target_pairs={{0,4},{1,5},{2,6},{3,7},{4,0},{5,1},{6,2},{7,3},{8,12},{9,13},{10,... | collective-permute-start | bytes 442376 | tf_op jit(solution)/shard_map/ppermute | solution.py:312
  35.5 2.9 %collective-permute-start.13 = (bf16[512,1152]{1,0:T(8,128)(2,1)S(1)}, bf16[512,1152]{1,0:T(8,128)(2,1)S(1)}, u32[]{:S(2)}, u32[]{:S(2)}) collective-permute-start(bf16[512,1152]{1,0:T(8,128)(2,1)S(1)} %constant_dynamic-update-slice_fusion.refs_1_.refs_2_), channel_id=1, source_target_pairs={{0,1},{1,0},{2,3},{3,2},{4,5},{5,4},{6,7},{7,6},{8,9},{9,8},{10,11... | collective-permute-start | bytes 3538952 | tf_op jit(solution)/shard_map/ppermute | solution.py:312
  35.6 10.1 %collective-permute-start.16 = (bf16[128,1280]{1,0:T(8,128)(2,1)S(1)}, bf16[128,1280]{1,0:T(8,128)(2,1)S(1)}, u32[]{:S(2)}, u32[]{:S(2)}) collective-permute-start(bf16[128,1280]{1,0:T(8,128)(2,1)S(1)} %pad_maximum_fusion.1.refs_0_), channel_id=1, source_target_pairs={{0,4},{1,5},{2,6},{3,7},{4,0},{5,1},{6,2},{7,3},{8,12},{9,13},{10,... | collective-permute-start | bytes 983048 | tf_op jit(solution)/shard_map/ppermute | solution.py:312
  36.4 10.6 %collective-permute-start.14 = (bf16[128,1280]{1,0:T(8,128)(2,1)S(1)}, bf16[128,1280]{1,0:T(8,128)(2,1)S(1)}, u32[]{:S(2)}, u32[]{:S(2)}) collective-permute-start(bf16[128,1280]{1,0:T(8,128)(2,1)S(1)} %pad_maximum_fusion.1.refs_0_), channel_id=1, source_target_pairs={{0,2},{1,3},{2,0},{3,1},{4,6},{5,7},{6,4},{7,5},{8,10},{9,11},{10,... | collective-permute-start | bytes 983048 | tf_op jit(solution)/shard_map/ppermute | solution.py:312
  37.4 11.0 %collective-permute-start.18 = (bf16[512,384]{1,0:T(8,128)(2,1)S(1)}, bf16[512,384]{1,0:T(8,128)(2,1)S(1)}, u32[]{:S(2)}, u32[]{:S(2)}) collective-permute-start(bf16[512,384]{1,0:T(8,128)(2,1)S(1)} %pad_maximum_fusion), channel_id=1, source_target_pairs={{0,8},{1,9},{2,10},{3,11},{4,12},{5,13},{6,14},{7,15},{8,0},{9,1},... | collective-permute-start | bytes 1179656 | tf_op jit(solution)/shard_map/ppermute | solution.py:312
  40.0 8.4 %collective-permute-start.15 = (bf16[128,1280]{1,0:T(8,128)(2,1)S(1)}, bf16[128,1280]{1,0:T(8,128)(2,1)S(1)}, u32[]{:S(2)}, u32[]{:S(2)}) collective-permute-start(bf16[128,1280]{1,0:T(8,128)(2,1)S(1)} %grad.3.refs_0_), channel_id=1, source_target_pairs={{0,1},{1,0},{2,3},{3,2},{4,5},{5,4},{6,7},{7,6},{8,9},{9,8},{10,11... | collective-permute-start | bytes 983048 | tf_op jit(solution)/shard_map/ppermute | solution.py:312
  45.7 5.8 %collective-permute-start.19 = (bf16[64,1280]{1,0:T(8,128)(2,1)S(1)}, bf16[64,1280]{1,0:T(8,128)(2,1)S(1)}, u32[]{:S(2)}, u32[]{:S(2)}) collective-permute-start(bf16[64,1280]{1,0:T(8,128)(2,1)S(1)} %slice.18), channel_id=1, source_target_pairs={{0,2},{1,3},{2,0},{3,1},{4,6},{5,7},{6,4},{7,5},{8,10},{9,11},{10,... | collective-permute-start | bytes 491528 | tf_op jit(solution)/shard_map/ppermute | solution.py:312
  47.0 5.5 %collective-permute-start.20 = (bf16[64,1280]{1,0:T(8,128)(2,1)S(1)}, bf16[64,1280]{1,0:T(8,128)(2,1)S(1)}, u32[]{:S(2)}, u32[]{:S(2)}) collective-permute-start(bf16[64,1280]{1,0:T(8,128)(2,1)S(1)} %slice.19), channel_id=1, source_target_pairs={{0,4},{1,5},{2,6},{3,7},{4,0},{5,1},{6,2},{7,3},{8,12},{9,13},{10,... | collective-permute-start | bytes 491528 | tf_op jit(solution)/shard_map/ppermute | solution.py:312
  50.5 3.8 %collective-permute-start.17 = (bf16[256,1280]{1,0:T(8,128)(2,1)S(1)}, bf16[256,1280]{1,0:T(8,128)(2,1)S(1)}, u32[]{:S(2)}, u32[]{:S(2)}) collective-permute-start(bf16[256,1280]{1,0:T(8,128)(2,1)S(1)} %grad.4.refs_2_.refs_0_), channel_id=1, source_target_pairs={{0,1},{1,0},{2,3},{3,2},{4,5},{5,4},{6,7},{7,6},{8,9},{9,8},{10,11... | collective-permute-start | bytes 1966088 | tf_op jit(solution)/shard_map/ppermute | solution.py:312
  54.2 1.2 %copy-start.1 = (bf16[384,1152]{1,0:T(8,128)(2,1)S(1)}, bf16[384,1152]{1,0:T(8,128)(2,1)}, u32[]{:S(2)}) copy-start(bf16[384,1152]{1,0:T(8,128)(2,1)} %weight_ref.3) | copy-start | bytes 2654212
  54.2 2.2 %collective-permute-start.21 = (bf16[128,1280]{1,0:T(8,128)(2,1)S(1)}, bf16[128,1280]{1,0:T(8,128)(2,1)S(1)}, u32[]{:S(2)}, u32[]{:S(2)}) collective-permute-start(bf16[128,1280]{1,0:T(8,128)(2,1)S(1)} %grad.5.refs_0_), channel_id=1, source_target_pairs={{0,1},{1,0},{2,3},{3,2},{4,5},{5,4},{6,7},{7,6},{8,9},{9,8},{10,11... | collective-permute-start | bytes 983048 | tf_op jit(solution)/shard_map/ppermute | solution.py:312
  (3 other events, 2.9 us)

commit v2 on v1

--- a/solution.py
+++ b/solution.py
@@ -281,11 +281,15 @@
         copy.wait()
 
 
-def features_body(full_width, rows, mp_count, place_ref, weight_ref, weight_sum_ref, *refs):
-    (*parts, out_ref, group_ref) = refs
-    for flip, part in enumerate(parts):
+def features_body(
+    full_width, rows, mp_count, place_ref, weight_ref, weight_sum_ref, own_ref, other_ref,
+    out_ref, group_ref,
+):
+    for flip in range(mp_count):
+        part_ref = other_ref if flip & 1 else own_ref
         start = pl.multiple_of(((place_ref[0] ^ flip) & (mp_count - 1)) * rows, rows)
-        group_ref[pl.ds(start, rows), :] = part[:rows, : group_ref.shape[1]]
+        at = flip // 2 * mp_count * rows
+        group_ref[pl.ds(start, rows), :] = part_ref[at : at + rows, : group_ref.shape[1]]
     group = group_ref[...]
     grad_normed = lax.dot_general(
         group, weight_ref[...], (((1,), (1,)), ((), ())), preferred_element_type=jnp.float32
@@ -378,8 +382,7 @@
     gathered = jnp.concatenate([gathered, features_far], axis=0)
     features_near = swap(gathered, near)
     gather_order = sum([[o, o ^ column] for o in order], [])
-    all_texts = [jnp.concatenate(txt_plane, axis=0)]
-    all_texts.append(swap(all_texts[0], core))
+    all_texts = txt_plane + [swap(part, core) for part in txt_plane]
     rows_y, rows_x = swap(line_rows, across), swap(line_rows, column)
     diagonal_rows = [swap(rows_x[:middle], across), swap(rows_y[middle:], column)]
 
@@ -392,15 +395,11 @@
             name="grad",
         )(*parts, *all_texts)
 
-    grads = [gradient(0, line_rows)]
+    grads = [gradient(0, line_rows, rows_y, rows_x)]
     others = [swap(grads[0], core)]
-    part_y = rows_y
-    part_y, others[0] = lax.optimization_barrier((rows_y, others[0]))
-    grads.append(gradient(local_rows, part_y, rows_x))
-    others.append(swap(grads[1], core))
     gathered = jnp.concatenate([gathered, features_near], axis=0)
 
-    planes = [[0], [across, column], [across | column]]
+    planes = [[0, across, column], [across | column]]
 
     def add_product(indices, previous, final=False):
         arrays = sum([[grads[i], others[i]] for i in indices], [])
@@ -424,16 +423,17 @@
         functools.partial(features_body, full_width, rows, mp_count),
         struct(features.shape),
         scratch=[pltpu.VMEM((local_rows, embed), jnp.bfloat16)],
-        in_specs=[smem] + [vmem] * (2 + mp_count),
+        in_specs=[smem] + [vmem] * 4,
         flops=0 * 2 * local_rows * width * embed,
         name="grad_features",
-    )(place, proj_weight, weight_sum, grads[0], others[0], grads[1], others[1])
+    )(place, proj_weight, weight_sum, grads[0], others[0])
+    *diagonal_rows, _, _ = lax.optimization_barrier(
+        (*diagonal_rows, grads[0], features_near)
+    )
+    grads.append(gradient(3 * local_rows, *diagonal_rows))
+    others.append(swap(grads[1], core))
     grad_weight = add_product([0], [])
-    *diagonal_rows, _, _ = lax.optimization_barrier((*diagonal_rows, grads[1], grad_weight))
-    grads.append(gradient(3 * local_rows, *diagonal_rows))
-    others.append(swap(grads[2], core))
-    grad_weight = add_product([1], [grad_weight])
-    grad_weight = add_product([2], [grad_weight], True)
+    grad_weight = add_product([1], [grad_weight], True)
     return grad_features, grad_weight
 
 

time: 58.4 us -> 67.5 us (1.16)
  Pallas kernels: 10.3 us -> 13.7 us
  waiting for transfers between devices: 19.6 us -> 22.2 us
  starting transfers between devices: 23.9 us -> 26.2 us
  local copies, waits for them, and re-layouts: 3.39 us -> 4.1 us
    pallas_call x3 -> x2, Pallas kernels: 5.18 us -> 8.85 us  [gradient(): kernel_call(functools.partial(grad_body, first, len(parts)), struct((tota...]
    ppermute x22 -> x24, waiting for transfers between devices: 19.6 us -> 22.2 us  [swap(): return lax.ppermute(value, axes, [(i, i ^ flip) for i in range(count)])]
    ppermute x22 -> x24, starting transfers between devices: 23.9 us -> 26.2 us  [swap(): return lax.ppermute(value, axes, [(i, i ^ flip) for i in range(count)])]
    unnamed x16 -> x13, local copies, waits for them, and re-layouts: 3.26 us -> 3.97 us
    pallas_call x3 -> x2, Pallas kernels: 3.22 us -> 3 us  [add_product(): kernel_call(functools.partial(weight_body, rows, mp_count, gather_order,...]
  transfers between devices with their start and end apart: 22 -> 24, of which waited for: 12 -> 9; matrix products, arithmetic and copies ran while one was open for 1% -> 0% of each run, Pallas kernels for 15% -> 18%
where the time goes in v2:
time: 67.5 us; the launch traced here: 67.2 us
  starting transfers between devices  26.2 us (39%)
  waiting for transfers between devices  22.2 us (33%)
  Pallas kernels  13.7 us (20%)
  local copies, waits for them, and re-layouts  4.1 us (6%)
  between operations  0.86 us (1%)
    ppermute x24, starting transfers between devices, swap(): return lax.ppermute(value, axes, [(i, i ^ flip) for i in range(count)])  26.2 us
    ppermute x24, waiting for transfers between devices, swap(): return lax.ppermute(value, axes, [(i, i ^ flip) for i in range(count)])  22.2 us
    pallas_call x2, Pallas kernels, gradient(): kernel_call(functools.partial(grad_body, first, len(parts)), struct((tota...  8.85 us
    unnamed x13, local copies, waits for them, and re-layouts  3.97 us
    pallas_call x2, Pallas kernels, add_product(): kernel_call(functools.partial(weight_body, rows, mp_count, gather_order,...  3 us
  transfers between devices with their start and end apart: 24, of which 9 were waited for; matrix products, arithmetic and copies ran while one was open for 0% of the time, Pallas kernels for 18%

profile of v2, /device:TPU:0, one launch (start us, length us, event | category | flops | bytes accessed | tf_op | source)
XLA Modules:
  0.0 67.2 jit_solution(11743457241225398096)
XLA Ops:
  0.7 0.9 %copy-done.4 = bf16[32,1152]{1,0:T(8,128)(2,1)S(1)} copy-done((bf16[32,1152]{1,0:T(8,128)(2,1)S(1)}, bf16[32,1152]{1,0:T(8,128)(2,1)}, u32[]{:S(2)}) %copy-start.4) | copy-done | bytes 73752
  1.7 5.1 %collective-permute-start.4 = (bf16[32,1152]{1,0:T(8,128)(2,1)S(1)}, bf16[32,1152]{1,0:T(8,128)(2,1)S(1)}, u32[]{:S(2)}, u32[]{:S(2)}) collective-permute-start(bf16[32,1152]{1,0:T(8,128)(2,1)S(1)} %unit_texts.1), channel_id=1, source_target_pairs={{0,24},{1,25},{2,26},{3,27},{4,28},{5,29},{6,30},{7,31},{8,16},{9,... | collective-permute-start | bytes 221192 | tf_op jit(solution)/shard_map/ppermute | solution.py:316
  7.4 1.6 %collective-permute-start.1 = (bf16[128,384]{1,0:T(8,128)(2,1)}, bf16[128,384]{1,0:T(8,128)(2,1)S(1)}, u32[]{:S(2)}, u32[]{:S(2)}) collective-permute-start(bf16[128,384]{1,0:T(8,128)(2,1)} %features_ref.1), channel_id=1, source_target_pairs={{0,4},{1,5},{2,6},{3,7},{4,0},{5,1},{6,2},{7,3},{8,12},{9,13},{10,... | collective-permute-start | bytes 294920 | tf_op jit(solution)/shard_map/ppermute | solution.py:316
  9.1 1.2 %copy-done = bf16[384,1152]{1,0:T(8,128)(2,1)S(1)} copy-done((bf16[384,1152]{1,0:T(8,128)(2,1)S(1)}, bf16[384,1152]{1,0:T(8,128)(2,1)}, u32[]{:S(2)}) %copy-start) | copy-done | bytes 884760
  10.2 0.9 %copy-done.2 = bf16[128,384]{1,0:T(8,128)(2,1)S(1)} copy-done((bf16[128,384]{1,0:T(8,128)(2,1)S(1)}, bf16[128,384]{1,0:T(8,128)(2,1)}, u32[]{:S(2)}) %copy-start.2) | copy-done | bytes 98328
  13.2 1.6 %collective-permute-start.5 = (bf16[32,1280]{1,0:T(8,128)(2,1)S(1)}, bf16[32,1280]{1,0:T(8,128)(2,1)S(1)}, u32[]{:S(2)}, u32[]{:S(2)}) collective-permute-start(bf16[32,1280]{1,0:T(8,128)(2,1)S(1)} %get-tuple-element.31), channel_id=1, source_target_pairs={{0,2},{1,3},{2,0},{3,1},{4,6},{5,7},{6,4},{7,5},{8,10},{9,11},{10,... | collective-permute-start | bytes 245768 | tf_op jit(solution)/shard_map/ppermute | solution.py:316
  14.7 1.2 %collective-permute-start.10 = (bf16[128,1152]{1,0:T(8,128)(2,1)S(1)}, bf16[128,1152]{1,0:T(8,128)(2,1)S(1)}, u32[]{:S(2)}, u32[]{:S(2)}) collective-permute-start(bf16[128,1152]{1,0:T(8,128)(2,1)S(1)} %pad_maximum_fusion.2.refs_3_.refs_2_), channel_id=1, source_target_pairs={{0,4},{1,5},{2,6},{3,7},{4,0},{5,1},{6,2},{7,3},{8,12},{9,13},{10,... | collective-permute-start | bytes 884744 | tf_op jit(solution)/shard_map/ppermute | solution.py:316
  16.5 1.5 %collective-permute-done.5.received_ref = bf16[32,1280]{1,0:T(8,128)(2,1)S(1)} collective-permute-done((bf16[32,1280]{1,0:T(8,128)(2,1)S(1)}, bf16[32,1280]{1,0:T(8,128)(2,1)S(1)}, u32[]{:S(2)}, u32[]{:S(2)}) %collective-permute-start.5) | collective-permute-done | bytes 81952 | tf_op jit(solution)/shard_map/ppermute | solution.py:316
  18.2 2.2 %collective-permute-start.6 = (bf16[32,1280]{1,0:T(8,128)(2,1)S(1)}, bf16[32,1280]{1,0:T(8,128)(2,1)S(1)}, u32[]{:S(2)}, u32[]{:S(2)}) collective-permute-start(bf16[32,1280]{1,0:T(8,128)(2,1)S(1)} %get-tuple-element.35), channel_id=1, source_target_pairs={{0,16},{1,17},{2,18},{3,19},{4,20},{5,21},{6,22},{7,23},{8,24},{9,... | collective-permute-start | bytes 245768 | tf_op jit(solution)/shard_map/ppermute | solution.py:316
  20.4 4.2 %collective-permute-done.6 = bf16[32,1280]{1,0:T(8,128)(2,1)S(1)} collective-permute-done((bf16[32,1280]{1,0:T(8,128)(2,1)S(1)}, bf16[32,1280]{1,0:T(8,128)(2,1)S(1)}, u32[]{:S(2)}, u32[]{:S(2)}) %collective-permute-start.6) | collective-permute-done | bytes 81952 | tf_op jit(solution)/shard_map/ppermute | solution.py:316
  25.0 3.1 %collective-permute-start.8 = (bf16[256,384]{1,0:T(8,128)(2,1)S(1)}, bf16[256,384]{1,0:T(8,128)(2,1)S(1)}, u32[]{:S(2)}, u32[]{:S(2)}) collective-permute-start(bf16[256,384]{1,0:T(8,128)(2,1)S(1)} %pad_maximum_fusion.3), channel_id=1, source_target_pairs={{0,16},{1,17},{2,18},{3,19},{4,20},{5,21},{6,22},{7,23},{8,24},{9,... | collective-permute-start | bytes 589832 | tf_op jit(solution)/shard_map/ppermute | solution.py:316
  28.1 2.1 %collective-permute-start.13 = (bf16[64,1152]{1,0:T(8,128)(2,1)S(1)}, bf16[64,1152]{1,0:T(8,128)(2,1)S(1)}, u32[]{:S(2)}, u32[]{:S(2)}) collective-permute-start(bf16[64,1152]{1,0:T(8,128)(2,1)S(1)} %slice.16), channel_id=1, source_target_pairs={{0,2},{1,3},{2,0},{3,1},{4,6},{5,7},{6,4},{7,5},{8,10},{9,11},{10,... | collective-permute-start | bytes 442376 | tf_op jit(solution)/shard_map/ppermute | solution.py:316
  31.1 6.8 %collective-permute-done.8 = bf16[256,384]{1,0:T(8,128)(2,1)S(1)} collective-permute-done((bf16[256,384]{1,0:T(8,128)(2,1)S(1)}, bf16[256,384]{1,0:T(8,128)(2,1)S(1)}, u32[]{:S(2)}, u32[]{:S(2)}) %collective-permute-start.8) | collective-permute-done | bytes 196640 | tf_op jit(solution)/shard_map/ppermute | solution.py:316
  38.6 2.1 %collective-permute-start.11 = (bf16[128,1280]{1,0:T(8,128)(2,1)S(1)}, bf16[128,1280]{1,0:T(8,128)(2,1)S(1)}, u32[]{:S(2)}, u32[]{:S(2)}) collective-permute-start(bf16[128,1280]{1,0:T(8,128)(2,1)S(1)} %pad_maximum_fusion.1.refs_0_), channel_id=1, source_target_pairs={{0,2},{1,3},{2,0},{3,1},{4,6},{5,7},{6,4},{7,5},{8,10},{9,11},{10,... | collective-permute-start | bytes 983048 | tf_op jit(solution)/shard_map/ppermute | solution.py:316
  41.4 6.1 %collective-permute-done.12.refs_2_ = bf16[128,1280]{1,0:T(8,128)(2,1)S(1)} collective-permute-done((bf16[128,1280]{1,0:T(8,128)(2,1)S(1)}, bf16[128,1280]{1,0:T(8,128)(2,1)S(1)}, u32[]{:S(2)}, u32[]{:S(2)}) %collective-permute-start.12) | collective-permute-done | bytes 327712 | tf_op jit(solution)/shard_map/ppermute | solution.py:316
  48.3 1.8 %collective-permute-start.21 = (bf16[64,1280]{1,0:T(8,128)(2,1)S(1)}, bf16[64,1280]{1,0:T(8,128)(2,1)S(1)}, u32[]{:S(2)}, u32[]{:S(2)}) collective-permute-start(bf16[64,1280]{1,0:T(8,128)(2,1)S(1)} %slice.18), channel_id=1, source_target_pairs={{0,2},{1,3},{2,0},{3,1},{4,6},{5,7},{6,4},{7,5},{8,10},{9,11},{10,... | collective-permute-start | bytes 491528 | tf_op jit(solution)/shard_map/ppermute | solution.py:316
  50.1 1.2 %collective-permute-start.22 = (bf16[64,1280]{1,0:T(8,128)(2,1)S(1)}, bf16[64,1280]{1,0:T(8,128)(2,1)S(1)}, u32[]{:S(2)}, u32[]{:S(2)}) collective-permute-start(bf16[64,1280]{1,0:T(8,128)(2,1)S(1)} %slice.19), channel_id=1, source_target_pairs={{0,4},{1,5},{2,6},{3,7},{4,0},{5,1},{6,2},{7,3},{8,12},{9,13},{10,... | collective-permute-start | bytes 491528 | tf_op jit(solution)/shard_map/ppermute | solution.py:316
  51.3 6.0 %grad.2.own_ref.refs_0_ = bf16[384,1280]{1,0:T(8,128)(2,1)S(1)} custom-call(bf16[128,1280]{1,0:T(8,128)(2,1)S(1)} %pad_maximum_fusion.1.refs_0_, bf16[128,1280]{1,0:T(8,128)(2,1)S(1)} %collective-permute-done.11.refs_1_, bf16[128,1280]{1,0:T(8,128)(2,1)S(1)} %collective-permute-done.12.refs_2_, bf16[128,1152]{1,0:T(8,128)(2,1)S(1)} %pad_maximum_fusion.2.refs_3_.refs_2_, ...), custom_call_target="tpu_custom_call" | custom-call | flops 18119393280 | tf_op jit(solution)/shard_map/grad/pallas_call | solution.py:391
  57.4 1.7 %collective-permute-done.20 = bf16[512,384]{1,0:T(8,128)(2,1)S(1)} collective-permute-done((bf16[512,384]{1,0:T(8,128)(2,1)S(1)}, bf16[512,384]{1,0:T(8,128)(2,1)S(1)}, u32[]{:S(2)}, u32[]{:S(2)}) %collective-permute-start.20) | collective-permute-done | bytes 393248 | tf_op jit(solution)/shard_map/ppermute | solution.py:316
  59.1 2.8 %grad.3.refs_0_ = bf16[128,1280]{1,0:T(8,128)(2,1)S(1)} custom-call(bf16[64,1280]{1,0:T(8,128)(2,1)S(1)} %collective-permute-done.21.refs_0_, bf16[64,1280]{1,0:T(8,128)(2,1)S(1)} %collective-permute-done.22.refs_1_, bf16[128,1152]{1,0:T(8,128)(2,1)S(1)} %pad_maximum_fusion.2.refs_3_.refs_2_, bf16[128,1152]{1,0:T(8,128)(2,1)S(1)} %collective-permute-done.9.refs_4_.refs_3_, ...), custom_call_target="tpu_custom_call" | custom-call | flops 6039797760 | tf_op jit(solution)/shard_map/grad/pallas_call | solution.py:391
  62.2 0.9 %copy-done.1 = bf16[384,1152]{1,0:T(8,128)(2,1)S(1)} copy-done((bf16[384,1152]{1,0:T(8,128)(2,1)S(1)}, bf16[384,1152]{1,0:T(8,128)(2,1)}, u32[]{:S(2)}) %copy-start.1) | copy-done | bytes 884760
  63.2 1.1 %grad_features.1 = bf16[128,384]{1,0:T(8,128)(2,1)} custom-call(s32[1]{0:T(128)} %bitcast.place_ref, bf16[384,1152]{1,0:T(8,128)(2,1)S(1)} %copy-done.1, f32[1,1152]{1,0:T(1,128)S(1)} %get-tuple-element.34.weight_sum_ref, bf16[384,1280]{1,0:T(8,128)(2,1)S(1)} %grad.2.own_ref.refs_0_, bf16[384,1280]{1,0:T(8,128)(2,1)S(1)} %collective-permute-done.19.other_ref.refs_1_), custom_call_target="tpu_custom_call" | custom-call | tf_op jit(solution)/shard_map/grad_features/pallas_call | solution.py:422
  64.2 1.3 %weight.2.refs_2_ = f32[384,1152]{1,0:T(8,128)S(1)} custom-call(s32[1]{0:T(128)} %bitcast.place_ref, bf16[1024,384]{1,0:T(8,128)(2,1)S(1)} %constant_dynamic-update-slice_fusion.2.features_ref, bf16[384,1280]{1,0:T(8,128)(2,1)S(1)} %grad.2.own_ref.refs_0_, bf16[384,1280]{1,0:T(8,128)(2,1)S(1)} %collective-permute-done.19.other_ref.refs_1_), custom_call_target="tpu_custom_call" | custom-call | tf_op jit(solution)/shard_map/weight/pallas_call | solution.py:412
  65.6 1.7 %weight.3 = f32[384,1152]{1,0:T(8,128)} custom-call(s32[1]{0:T(128)} %bitcast.place_ref, bf16[1024,384]{1,0:T(8,128)(2,1)S(1)} %constant_dynamic-update-slice_fusion.2.features_ref, bf16[128,1280]{1,0:T(8,128)(2,1)S(1)} %grad.3.refs_0_, bf16[128,1280]{1,0:T(8,128)(2,1)S(1)} %collective-permute-done.23.refs_1_, f32[384,1152]{1,0:T(8,128)S(1)} %weight.2.refs_2_), custom_call_target="tpu_custom_call" | custom-call | tf_op jit(solution)/shard_map/weight/pallas_call | solution.py:412
  (57 shorter events, 7.2 us)
Async XLA Ops:
  1.7 9.9 %collective-permute-start.4 = (bf16[32,1152]{1,0:T(8,128)(2,1)S(1)}, bf16[32,1152]{1,0:T(8,128)(2,1)S(1)}, u32[]{:S(2)}, u32[]{:S(2)}) collective-permute-start(bf16[32,1152]{1,0:T(8,128)(2,1)S(1)} %unit_texts.1), channel_id=1, source_target_pairs={{0,24},{1,25},{2,26},{3,27},{4,28},{5,29},{6,30},{7,31},{8,16},{9,... | collective-permute-start | bytes 221192 | tf_op jit(solution)/shard_map/ppermute | solution.py:316
  6.8 5.0 %collective-permute-start.3 = (bf16[32,1152]{1,0:T(8,128)(2,1)S(1)}, bf16[32,1152]{1,0:T(8,128)(2,1)S(1)}, u32[]{:S(2)}, u32[]{:S(2)}) collective-permute-start(bf16[32,1152]{1,0:T(8,128)(2,1)S(1)} %unit_texts.1), channel_id=1, source_target_pairs={{0,8},{1,9},{2,10},{3,11},{4,12},{5,13},{6,14},{7,15},{8,0},{9,1},... | collective-permute-start | bytes 221192 | tf_op jit(solution)/shard_map/ppermute | solution.py:316
  6.8 5.8 %collective-permute-start.2 = (bf16[32,1152]{1,0:T(8,128)(2,1)S(1)}, bf16[32,1152]{1,0:T(8,128)(2,1)S(1)}, u32[]{:S(2)}, u32[]{:S(2)}) collective-permute-start(bf16[32,1152]{1,0:T(8,128)(2,1)S(1)} %unit_texts.1), channel_id=1, source_target_pairs={{0,16},{1,17},{2,18},{3,19},{4,20},{5,21},{6,22},{7,23},{8,24},{9,... | collective-permute-start | bytes 221192 | tf_op jit(solution)/shard_map/ppermute | solution.py:316
  7.4 5.7 %collective-permute-start.1 = (bf16[128,384]{1,0:T(8,128)(2,1)}, bf16[128,384]{1,0:T(8,128)(2,1)S(1)}, u32[]{:S(2)}, u32[]{:S(2)}) collective-permute-start(bf16[128,384]{1,0:T(8,128)(2,1)} %features_ref.1), channel_id=1, source_target_pairs={{0,4},{1,5},{2,6},{3,7},{4,0},{5,1},{6,2},{7,3},{8,12},{9,13},{10,... | collective-permute-start | bytes 294920 | tf_op jit(solution)/shard_map/ppermute | solution.py:316
  11.5 1.5 %collective-permute-start = (bf16[64,1280]{1,0:T(8,128)(2,1)S(1)}, bf16[64,1280]{1,0:T(8,128)(2,1)S(1)}, u32[]{:S(2)}, u32[]{:S(2)}) collective-permute-start(bf16[64,1280]{1,0:T(8,128)(2,1)S(1)} %get-tuple-element.25), channel_id=1, source_target_pairs={{0,1},{1,0},{2,3},{3,2},{4,5},{5,4},{6,7},{7,6},{8,9},{9,8},{10,11... | collective-permute-start | bytes 491528 | tf_op jit(solution)/shard_map/ppermute | solution.py:316
  13.2 4.9 %collective-permute-start.5 = (bf16[32,1280]{1,0:T(8,128)(2,1)S(1)}, bf16[32,1280]{1,0:T(8,128)(2,1)S(1)}, u32[]{:S(2)}, u32[]{:S(2)}) collective-permute-start(bf16[32,1280]{1,0:T(8,128)(2,1)S(1)} %get-tuple-element.31), channel_id=1, source_target_pairs={{0,2},{1,3},{2,0},{3,1},{4,6},{5,7},{6,4},{7,5},{8,10},{9,11},{10,... | collective-permute-start | bytes 245768 | tf_op jit(solution)/shard_map/ppermute | solution.py:316
  14.7 13.4 %collective-permute-start.10 = (bf16[128,1152]{1,0:T(8,128)(2,1)S(1)}, bf16[128,1152]{1,0:T(8,128)(2,1)S(1)}, u32[]{:S(2)}, u32[]{:S(2)}) collective-permute-start(bf16[128,1152]{1,0:T(8,128)(2,1)S(1)} %pad_maximum_fusion.2.refs_3_.refs_2_), channel_id=1, source_target_pairs={{0,4},{1,5},{2,6},{3,7},{4,0},{5,1},{6,2},{7,3},{8,12},{9,13},{10,... | collective-permute-start | bytes 884744 | tf_op jit(solution)/shard_map/ppermute | solution.py:316
  16.0 14.3 %collective-permute-start.9 = (bf16[128,1152]{1,0:T(8,128)(2,1)S(1)}, bf16[128,1152]{1,0:T(8,128)(2,1)S(1)}, u32[]{:S(2)}, u32[]{:S(2)}) collective-permute-start(bf16[128,1152]{1,0:T(8,128)(2,1)S(1)} %pad_maximum_fusion.2.refs_3_.refs_2_), channel_id=1, source_target_pairs={{0,2},{1,3},{2,0},{3,1},{4,6},{5,7},{6,4},{7,5},{8,10},{9,11},{10,... | collective-permute-start | bytes 884744 | tf_op jit(solution)/shard_map/ppermute | solution.py:316
  18.2 6.4 %collective-permute-start.6 = (bf16[32,1280]{1,0:T(8,128)(2,1)S(1)}, bf16[32,1280]{1,0:T(8,128)(2,1)S(1)}, u32[]{:S(2)}, u32[]{:S(2)}) collective-permute-start(bf16[32,1280]{1,0:T(8,128)(2,1)S(1)} %get-tuple-element.35), channel_id=1, source_target_pairs={{0,16},{1,17},{2,18},{3,19},{4,20},{5,21},{6,22},{7,23},{8,24},{9,... | collective-permute-start | bytes 245768 | tf_op jit(solution)/shard_map/ppermute | solution.py:316
  24.6 6.5 %collective-permute-start.7 = (bf16[64,1280]{1,0:T(8,128)(2,1)S(1)}, bf16[64,1280]{1,0:T(8,128)(2,1)S(1)}, u32[]{:S(2)}, u32[]{:S(2)}) collective-permute-start(bf16[64,1280]{1,0:T(8,128)(2,1)S(1)} %pad_maximum_fusion.4), channel_id=1, source_target_pairs={{0,8},{1,9},{2,10},{3,11},{4,12},{5,13},{6,14},{7,15},{8,0},{9,1},... | collective-permute-start | bytes 491528 | tf_op jit(solution)/shard_map/ppermute | solution.py:316
  25.0 23.3 %collective-permute-start.15 = (bf16[128,1152]{1,0:T(8,128)(2,1)S(1)}, bf16[128,1152]{1,0:T(8,128)(2,1)S(1)}, u32[]{:S(2)}, u32[]{:S(2)}) collective-permute-start(bf16[128,1152]{1,0:T(8,128)(2,1)S(1)} %pad_maximum_fusion.2.refs_3_.refs_2_), channel_id=1, source_target_pairs={{0,1},{1,0},{2,3},{3,2},{4,5},{5,4},{6,7},{7,6},{8,9},{9,8},{10,11... | collective-permute-start | bytes 884744 | tf_op jit(solution)/shard_map/ppermute | solution.py:316
  25.0 12.9 %collective-permute-start.8 = (bf16[256,384]{1,0:T(8,128)(2,1)S(1)}, bf16[256,384]{1,0:T(8,128)(2,1)S(1)}, u32[]{:S(2)}, u32[]{:S(2)}) collective-permute-start(bf16[256,384]{1,0:T(8,128)(2,1)S(1)} %pad_maximum_fusion.3), channel_id=1, source_target_pairs={{0,16},{1,17},{2,18},{3,19},{4,20},{5,21},{6,22},{7,23},{8,24},{9,... | collective-permute-start | bytes 589832 | tf_op jit(solution)/shard_map/ppermute | solution.py:316
  28.1 12.6 %collective-permute-start.13 = (bf16[64,1152]{1,0:T(8,128)(2,1)S(1)}, bf16[64,1152]{1,0:T(8,128)(2,1)S(1)}, u32[]{:S(2)}, u32[]{:S(2)}) collective-permute-start(bf16[64,1152]{1,0:T(8,128)(2,1)S(1)} %slice.16), channel_id=1, source_target_pairs={{0,2},{1,3},{2,0},{3,1},{4,6},{5,7},{6,4},{7,5},{8,10},{9,11},{10,... | collective-permute-start | bytes 442376 | tf_op jit(solution)/shard_map/ppermute | solution.py:316
  30.2 10.6 %collective-permute-start.14 = (bf16[64,1152]{1,0:T(8,128)(2,1)S(1)}, bf16[64,1152]{1,0:T(8,128)(2,1)S(1)}, u32[]{:S(2)}, u32[]{:S(2)}) collective-permute-start(bf16[64,1152]{1,0:T(8,128)(2,1)S(1)} %slice.17), channel_id=1, source_target_pairs={{0,4},{1,5},{2,6},{3,7},{4,0},{5,1},{6,2},{7,3},{8,12},{9,13},{10,... | collective-permute-start | bytes 442376 | tf_op jit(solution)/shard_map/ppermute | solution.py:316
  37.9 9.5 %collective-permute-start.12 = (bf16[128,1280]{1,0:T(8,128)(2,1)S(1)}, bf16[128,1280]{1,0:T(8,128)(2,1)S(1)}, u32[]{:S(2)}, u32[]{:S(2)}) collective-permute-start(bf16[128,1280]{1,0:T(8,128)(2,1)S(1)} %pad_maximum_fusion.1.refs_0_), channel_id=1, source_target_pairs={{0,4},{1,5},{2,6},{3,7},{4,0},{5,1},{6,2},{7,3},{8,12},{9,13},{10,... | collective-permute-start | bytes 983048 | tf_op jit(solution)/shard_map/ppermute | solution.py:316
  38.6 9.5 %collective-permute-start.11 = (bf16[128,1280]{1,0:T(8,128)(2,1)S(1)}, bf16[128,1280]{1,0:T(8,128)(2,1)S(1)}, u32[]{:S(2)}, u32[]{:S(2)}) collective-permute-start(bf16[128,1280]{1,0:T(8,128)(2,1)S(1)} %pad_maximum_fusion.1.refs_0_), channel_id=1, source_target_pairs={{0,2},{1,3},{2,0},{3,1},{4,6},{5,7},{6,4},{7,5},{8,10},{9,11},{10,... | collective-permute-start | bytes 983048 | tf_op jit(solution)/shard_map/ppermute | solution.py:316
  40.8 9.3 %collective-permute-start.16 = (bf16[128,1152]{1,0:T(8,128)(2,1)S(1)}, bf16[128,1152]{1,0:T(8,128)(2,1)S(1)}, u32[]{:S(2)}, u32[]{:S(2)}) collective-permute-start(bf16[128,1152]{1,0:T(8,128)(2,1)S(1)} %collective-permute-done.9.refs_4_.refs_3_), channel_id=1, source_target_pairs={{0,1},{1,0},{2,3},{3,2},{4,5},{5,4},{6,7},{7,6},{8,9},{9,8},{10,11... | collective-permute-start | bytes 884744 | tf_op jit(solution)/shard_map/ppermute | solution.py:316
  40.8 10.5 %collective-permute-start.17 = (bf16[128,1152]{1,0:T(8,128)(2,1)S(1)}, bf16[128,1152]{1,0:T(8,128)(2,1)S(1)}, u32[]{:S(2)}, u32[]{:S(2)}) collective-permute-start(bf16[128,1152]{1,0:T(8,128)(2,1)S(1)} %collective-permute-done.10.refs_5_.refs_4_), channel_id=1, source_target_pairs={{0,1},{1,0},{2,3},{3,2},{4,5},{5,4},{6,7},{7,6},{8,9},{9,8},{10,11... | collective-permute-start | bytes 884744 | tf_op jit(solution)/shard_map/ppermute | solution.py:316
  47.5 3.9 %collective-permute-start.18 = (bf16[128,1152]{1,0:T(8,128)(2,1)S(1)}, bf16[128,1152]{1,0:T(8,128)(2,1)S(1)}, u32[]{:S(2)}, u32[]{:S(2)}) collective-permute-start(bf16[128,1152]{1,0:T(8,128)(2,1)S(1)} %constant_dynamic-update-slice_fusion.refs_6_.refs_5_), channel_id=1, source_target_pairs={{0,1},{1,0},{2,3},{3,2},{4,5},{5,4},{6,7},{7,6},{8,9},{9,8},{10,11... | collective-permute-start | bytes 884744 | tf_op jit(solution)/shard_map/ppermute | solution.py:316
  48.1 11.0 %collective-permute-start.20 = (bf16[512,384]{1,0:T(8,128)(2,1)S(1)}, bf16[512,384]{1,0:T(8,128)(2,1)S(1)}, u32[]{:S(2)}, u32[]{:S(2)}) collective-permute-start(bf16[512,384]{1,0:T(8,128)(2,1)S(1)} %pad_maximum_fusion), channel_id=1, source_target_pairs={{0,8},{1,9},{2,10},{3,11},{4,12},{5,13},{6,14},{7,15},{8,0},{9,1},... | collective-permute-start | bytes 1179656 | tf_op jit(solution)/shard_map/ppermute | solution.py:316
  48.3 10.9 %collective-permute-start.21 = (bf16[64,1280]{1,0:T(8,128)(2,1)S(1)}, bf16[64,1280]{1,0:T(8,128)(2,1)S(1)}, u32[]{:S(2)}, u32[]{:S(2)}) collective-permute-start(bf16[64,1280]{1,0:T(8,128)(2,1)S(1)} %slice.18), channel_id=1, source_target_pairs={{0,2},{1,3},{2,0},{3,1},{4,6},{5,7},{6,4},{7,5},{8,10},{9,11},{10,... | collective-permute-start | bytes 491528 | tf_op jit(solution)/shard_map/ppermute | solution.py:316
  50.1 9.0 %collective-permute-start.22 = (bf16[64,1280]{1,0:T(8,128)(2,1)S(1)}, bf16[64,1280]{1,0:T(8,128)(2,1)S(1)}, u32[]{:S(2)}, u32[]{:S(2)}) collective-permute-start(bf16[64,1280]{1,0:T(8,128)(2,1)S(1)} %slice.19), channel_id=1, source_target_pairs={{0,4},{1,5},{2,6},{3,7},{4,0},{5,1},{6,2},{7,3},{8,12},{9,13},{10,... | collective-permute-start | bytes 491528 | tf_op jit(solution)/shard_map/ppermute | solution.py:316
  57.3 4.9 %collective-permute-start.19 = (bf16[384,1280]{1,0:T(8,128)(2,1)S(1)}, bf16[384,1280]{1,0:T(8,128)(2,1)S(1)}, u32[]{:S(2)}, u32[]{:S(2)}) collective-permute-start(bf16[384,1280]{1,0:T(8,128)(2,1)S(1)} %grad.2.own_ref.refs_0_), channel_id=1, source_target_pairs={{0,1},{1,0},{2,3},{3,2},{4,5},{5,4},{6,7},{7,6},{8,9},{9,8},{10,11... | collective-permute-start | bytes 2949128 | tf_op jit(solution)/shard_map/ppermute | solution.py:316
  62.0 3.5 %collective-permute-start.23 = (bf16[128,1280]{1,0:T(8,128)(2,1)S(1)}, bf16[128,1280]{1,0:T(8,128)(2,1)S(1)}, u32[]{:S(2)}, u32[]{:S(2)}) collective-permute-start(bf16[128,1280]{1,0:T(8,128)(2,1)S(1)} %grad.3.refs_0_), channel_id=1, source_target_pairs={{0,1},{1,0},{2,3},{3,2},{4,5},{5,4},{6,7},{7,6},{8,9},{9,8},{10,11... | collective-permute-start | bytes 983048 | tf_op jit(solution)/shard_map/ppermute | solution.py:316
  (5 other events, 23.9 us)

commit v3 on v1

--- a/solution.py
+++ b/solution.py
@@ -198,7 +198,7 @@
     weight_sum_ref[...] = columns[0] + columns[1]
 
 
-def grad_body(first, count, *refs):
+def grad_body(first, count, rows, places, *refs):
     projects = refs[:count]
     (*texts, out_ref) = refs[count:]
     embed = texts[0].shape[1]
@@ -207,6 +207,12 @@
     unit_img = project * inv_norm
     unit_img_b = unit_img.astype(jnp.bfloat16)
     grad_unit = jnp.zeros_like(project)
+    row = lax.broadcasted_iota(jnp.int32, (project.shape[0], 1), 0)
+    group = row // rows
+    place = group % len(places)
+    pair = row + first
+    for k, text_place in enumerate(places):
+        pair = jnp.where(place == k, pair + (text_place - k) * rows, pair)
     at = 0
     for ref in texts:
         unit_txt_b = ref[...]
@@ -221,8 +227,7 @@
             + logit_bias
         )
         text = lax.broadcasted_iota(jnp.int32, logits.shape, 1) + at
-        image = lax.broadcasted_iota(jnp.int32, logits.shape, 0) + first
-        labels = jnp.where(text == image, 1.0, -1.0)
+        labels = jnp.where(text == pair, 1.0, -1.0)
         slopes = (-labels / (1.0 + jnp.exp(labels * logits))).astype(jnp.bfloat16)
         grad_unit = grad_unit + jnp.dot(slopes, unit_txt_b, preferred_element_type=jnp.float32)
         at += unit_txt_b.shape[0]
@@ -340,8 +345,9 @@
     far, near = line[1], line[0]
     order = [0, far, near, far ^ near]
     unit_txt_b = kernel_call(texts_body, struct(texts.shape), name="unit_texts")(texts)
+    txt_order = [0, far ^ near, far, near]
     txt_line = jnp.concatenate(
-        [unit_txt_b] + [swap(unit_txt_b, flip) for flip in order[1:]], axis=0
+        [unit_txt_b] + [swap(unit_txt_b, flip) for flip in txt_order[1:]], axis=0
     )
     features_x = swap(features, column)
     send, features_x = lax.optimization_barrier((send, features_x))
@@ -386,7 +392,9 @@
     def gradient(first, *parts):
         total = sum(part.shape[0] for part in parts)
         return kernel_call(
-            functools.partial(grad_body, first, len(parts)),
+            functools.partial(
+                grad_body, first, len(parts), rows, [txt_order.index(o) for o in order]
+            ),
             struct((total, embed + LANES)),
             flops=10 * 4 * total * count * rows * embed,
             name="grad",

time: 58.4 us -> 58.4 us (level)
  no operation moved by 1% of the time
where the time goes in v3:
time: 58.4 us; the launch traced here: 58.1 us
  starting transfers between devices  23.6 us (40%)
  waiting for transfers between devices  20 us (34%)
  Pallas kernels  10.3 us (18%)
  local copies, waits for them, and re-layouts  3.33 us (6%)
  between operations  0.84 us (1%)
    ppermute x22, starting transfers between devices, swap(): return lax.ppermute(value, axes, [(i, i ^ flip) for i in range(count)])  23.6 us
    ppermute x22, waiting for transfers between devices, swap(): return lax.ppermute(value, axes, [(i, i ^ flip) for i in range(count)])  20 us
    pallas_call x3, Pallas kernels, gradient(): kernel_call(functools.partial(grad_body, first, len(parts), rows, [txt_or...  5.17 us
    pallas_call x3, Pallas kernels, add_product(): kernel_call(functools.partial(weight_body, rows, mp_count, gather_order,...  3.21 us
    unnamed x16, local copies, waits for them, and re-layouts  3.2 us
  transfers between devices with their start and end apart: 22, of which 12 were waited for; matrix products, arithmetic and copies ran while one was open for 1% of the time, Pallas kernels for 15%

profile of v3, /device:TPU:0, one launch (start us, length us, event | category | flops | bytes accessed | tf_op | source)
XLA Modules:
  0.0 58.1 jit_solution(6266476179612042034)
XLA Ops:
  1.6 3.1 %collective-permute-start.4 = (bf16[32,1152]{1,0:T(8,128)(2,1)S(1)}, bf16[32,1152]{1,0:T(8,128)(2,1)S(1)}, u32[]{:S(2)}, u32[]{:S(2)}) collective-permute-start(bf16[32,1152]{1,0:T(8,128)(2,1)S(1)} %unit_texts.1), channel_id=1, source_target_pairs={{0,8},{1,9},{2,10},{3,11},{4,12},{5,13},{6,14},{7,15},{8,0},{9,1},... | collective-permute-start | bytes 221192 | tf_op jit(solution)/shard_map/ppermute | solution.py:317
  4.7 2.6 %collective-permute-start.3 = (bf16[32,1152]{1,0:T(8,128)(2,1)S(1)}, bf16[32,1152]{1,0:T(8,128)(2,1)S(1)}, u32[]{:S(2)}, u32[]{:S(2)}) collective-permute-start(bf16[32,1152]{1,0:T(8,128)(2,1)S(1)} %unit_texts.1), channel_id=1, source_target_pairs={{0,16},{1,17},{2,18},{3,19},{4,20},{5,21},{6,22},{7,23},{8,24},{9,... | collective-permute-start | bytes 221192 | tf_op jit(solution)/shard_map/ppermute | solution.py:317
  7.3 1.7 %collective-permute-start.1 = (bf16[128,384]{1,0:T(8,128)(2,1)}, bf16[128,384]{1,0:T(8,128)(2,1)S(1)}, u32[]{:S(2)}, u32[]{:S(2)}) collective-permute-start(bf16[128,384]{1,0:T(8,128)(2,1)} %features_ref.1), channel_id=1, source_target_pairs={{0,4},{1,5},{2,6},{3,7},{4,0},{5,1},{6,2},{7,3},{8,12},{9,13},{10,... | collective-permute-start | bytes 294920 | tf_op jit(solution)/shard_map/ppermute | solution.py:317
  9.0 1.2 %copy-done = bf16[384,1152]{1,0:T(8,128)(2,1)S(1)} copy-done((bf16[384,1152]{1,0:T(8,128)(2,1)S(1)}, bf16[384,1152]{1,0:T(8,128)(2,1)}, u32[]{:S(2)}) %copy-start) | copy-done | bytes 884760
  11.6 0.9 %collective-permute-done.3 = bf16[32,1152]{1,0:T(8,128)(2,1)S(1)} collective-permute-done((bf16[32,1152]{1,0:T(8,128)(2,1)S(1)}, bf16[32,1152]{1,0:T(8,128)(2,1)S(1)}, u32[]{:S(2)}, u32[]{:S(2)}) %collective-permute-start.3) | collective-permute-done | bytes 73760 | tf_op jit(solution)/shard_map/ppermute | solution.py:317
  12.5 1.1 %collective-permute-done.2 = bf16[32,1152]{1,0:T(8,128)(2,1)S(1)} collective-permute-done((bf16[32,1152]{1,0:T(8,128)(2,1)S(1)}, bf16[32,1152]{1,0:T(8,128)(2,1)S(1)}, u32[]{:S(2)}, u32[]{:S(2)}) %collective-permute-start.2) | collective-permute-done | bytes 73760 | tf_op jit(solution)/shard_map/ppermute | solution.py:317
  13.8 1.6 %collective-permute-start.5 = (bf16[32,1280]{1,0:T(8,128)(2,1)S(1)}, bf16[32,1280]{1,0:T(8,128)(2,1)S(1)}, u32[]{:S(2)}, u32[]{:S(2)}) collective-permute-start(bf16[32,1280]{1,0:T(8,128)(2,1)S(1)} %get-tuple-element.33), channel_id=1, source_target_pairs={{0,2},{1,3},{2,0},{3,1},{4,6},{5,7},{6,4},{7,5},{8,10},{9,11},{10,... | collective-permute-start | bytes 245768 | tf_op jit(solution)/shard_map/ppermute | solution.py:317
  15.4 1.5 %collective-permute-start.10 = (bf16[128,1152]{1,0:T(8,128)(2,1)S(1)}, bf16[128,1152]{1,0:T(8,128)(2,1)S(1)}, u32[]{:S(2)}, u32[]{:S(2)}) collective-permute-start(bf16[128,1152]{1,0:T(8,128)(2,1)S(1)} %pad_maximum_fusion.2), channel_id=1, source_target_pairs={{0,4},{1,5},{2,6},{3,7},{4,0},{5,1},{6,2},{7,3},{8,12},{9,13},{10,... | collective-permute-start | bytes 884744 | tf_op jit(solution)/shard_map/ppermute | solution.py:317
  17.4 1.8 %collective-permute-done.5.received_ref = bf16[32,1280]{1,0:T(8,128)(2,1)S(1)} collective-permute-done((bf16[32,1280]{1,0:T(8,128)(2,1)S(1)}, bf16[32,1280]{1,0:T(8,128)(2,1)S(1)}, u32[]{:S(2)}, u32[]{:S(2)}) %collective-permute-start.5) | collective-permute-done | bytes 81952 | tf_op jit(solution)/shard_map/ppermute | solution.py:317
  19.3 2.0 %collective-permute-start.6 = (bf16[32,1280]{1,0:T(8,128)(2,1)S(1)}, bf16[32,1280]{1,0:T(8,128)(2,1)S(1)}, u32[]{:S(2)}, u32[]{:S(2)}) collective-permute-start(bf16[32,1280]{1,0:T(8,128)(2,1)S(1)} %get-tuple-element.37), channel_id=1, source_target_pairs={{0,16},{1,17},{2,18},{3,19},{4,20},{5,21},{6,22},{7,23},{8,24},{9,... | collective-permute-start | bytes 245768 | tf_op jit(solution)/shard_map/ppermute | solution.py:317
  21.3 4.3 %collective-permute-done.6 = bf16[32,1280]{1,0:T(8,128)(2,1)S(1)} collective-permute-done((bf16[32,1280]{1,0:T(8,128)(2,1)S(1)}, bf16[32,1280]{1,0:T(8,128)(2,1)S(1)}, u32[]{:S(2)}, u32[]{:S(2)}) %collective-permute-start.6) | collective-permute-done | bytes 81952 | tf_op jit(solution)/shard_map/ppermute | solution.py:317
  26.0 2.9 %collective-permute-start.8 = (bf16[256,384]{1,0:T(8,128)(2,1)S(1)}, bf16[256,384]{1,0:T(8,128)(2,1)S(1)}, u32[]{:S(2)}, u32[]{:S(2)}) collective-permute-start(bf16[256,384]{1,0:T(8,128)(2,1)S(1)} %pad_maximum_fusion.3), channel_id=1, source_target_pairs={{0,16},{1,17},{2,18},{3,19},{4,20},{5,21},{6,22},{7,23},{8,24},{9,... | collective-permute-start | bytes 589832 | tf_op jit(solution)/shard_map/ppermute | solution.py:317
  28.9 2.1 %collective-permute-start.11 = (bf16[64,1152]{1,0:T(8,128)(2,1)S(1)}, bf16[64,1152]{1,0:T(8,128)(2,1)S(1)}, u32[]{:S(2)}, u32[]{:S(2)}) collective-permute-start(bf16[64,1152]{1,0:T(8,128)(2,1)S(1)} %slice.16), channel_id=1, source_target_pairs={{0,2},{1,3},{2,0},{3,1},{4,6},{5,7},{6,4},{7,5},{8,10},{9,11},{10,... | collective-permute-start | bytes 442376 | tf_op jit(solution)/shard_map/ppermute | solution.py:317
  31.1 1.9 %collective-permute-done.7 = bf16[64,1280]{1,0:T(8,128)(2,1)S(1)} collective-permute-done((bf16[64,1280]{1,0:T(8,128)(2,1)S(1)}, bf16[64,1280]{1,0:T(8,128)(2,1)S(1)}, u32[]{:S(2)}, u32[]{:S(2)}) %collective-permute-start.7) | collective-permute-done | bytes 163872 | tf_op jit(solution)/shard_map/ppermute | solution.py:317
  33.0 1.8 %collective-permute-done.8 = bf16[256,384]{1,0:T(8,128)(2,1)S(1)} collective-permute-done((bf16[256,384]{1,0:T(8,128)(2,1)S(1)}, bf16[256,384]{1,0:T(8,128)(2,1)S(1)}, u32[]{:S(2)}, u32[]{:S(2)}) %collective-permute-start.8) | collective-permute-done | bytes 196640 | tf_op jit(solution)/shard_map/ppermute | solution.py:317
  34.9 1.3 %collective-permute-done.12 = bf16[64,1152]{1,0:T(8,128)(2,1)S(1)} collective-permute-done((bf16[64,1152]{1,0:T(8,128)(2,1)S(1)}, bf16[64,1152]{1,0:T(8,128)(2,1)S(1)}, u32[]{:S(2)}, u32[]{:S(2)}) %collective-permute-start.12) | collective-permute-done | bytes 147488 | tf_op jit(solution)/shard_map/ppermute | solution.py:317
  36.5 1.8 %collective-permute-start.14 = (bf16[128,1280]{1,0:T(8,128)(2,1)S(1)}, bf16[128,1280]{1,0:T(8,128)(2,1)S(1)}, u32[]{:S(2)}, u32[]{:S(2)}) collective-permute-start(bf16[128,1280]{1,0:T(8,128)(2,1)S(1)} %pad_maximum_fusion.1.refs_0_), channel_id=1, source_target_pairs={{0,2},{1,3},{2,0},{3,1},{4,6},{5,7},{6,4},{7,5},{8,10},{9,11},{10,... | collective-permute-start | bytes 983048 | tf_op jit(solution)/shard_map/ppermute | solution.py:317
  39.1 1.6 %grad.3.refs_0_ = bf16[128,1280]{1,0:T(8,128)(2,1)S(1)} custom-call(bf16[128,1280]{1,0:T(8,128)(2,1)S(1)} %pad_maximum_fusion.1.refs_0_, bf16[512,1152]{1,0:T(8,128)(2,1)S(1)} %constant_dynamic-update-slice_fusion.refs_1_.refs_2_, bf16[512,1152]{1,0:T(8,128)(2,1)S(1)} %collective-permute-done.13.refs_2_.refs_3_), custom_call_target="tpu_custom_call" | custom-call | flops 6039797760 | tf_op jit(solution)/shard_map/grad/pallas_call | solution.py:394
  41.0 5.4 %collective-permute-done.16.refs_1_ = bf16[128,1280]{1,0:T(8,128)(2,1)S(1)} collective-permute-done((bf16[128,1280]{1,0:T(8,128)(2,1)S(1)}, bf16[128,1280]{1,0:T(8,128)(2,1)S(1)}, u32[]{:S(2)}, u32[]{:S(2)}) %collective-permute-start.16) | collective-permute-done | bytes 327712 | tf_op jit(solution)/shard_map/ppermute | solution.py:317
  47.1 1.5 %collective-permute-start.20 = (bf16[64,1280]{1,0:T(8,128)(2,1)S(1)}, bf16[64,1280]{1,0:T(8,128)(2,1)S(1)}, u32[]{:S(2)}, u32[]{:S(2)}) collective-permute-start(bf16[64,1280]{1,0:T(8,128)(2,1)S(1)} %slice.19), channel_id=1, source_target_pairs={{0,4},{1,5},{2,6},{3,7},{4,0},{5,1},{6,2},{7,3},{8,12},{9,13},{10,... | collective-permute-start | bytes 491528 | tf_op jit(solution)/shard_map/ppermute | solution.py:317
  49.5 2.0 %grad.4.refs_2_.refs_0_ = bf16[256,1280]{1,0:T(8,128)(2,1)S(1)} custom-call(bf16[128,1280]{1,0:T(8,128)(2,1)S(1)} %collective-permute-done.14.refs_0_, bf16[128,1280]{1,0:T(8,128)(2,1)S(1)} %collective-permute-done.16.refs_1_, bf16[512,1152]{1,0:T(8,128)(2,1)S(1)} %constant_dynamic-update-slice_fusion.refs_1_.refs_2_, ...), custom_call_target="tpu_custom_call" | custom-call | flops 12079595520 | tf_op jit(solution)/shard_map/grad/pallas_call | solution.py:394
  52.6 1.6 %grad.5.refs_0_ = bf16[128,1280]{1,0:T(8,128)(2,1)S(1)} custom-call(bf16[64,1280]{1,0:T(8,128)(2,1)S(1)} %collective-permute-done.19.refs_0_, bf16[64,1280]{1,0:T(8,128)(2,1)S(1)} %collective-permute-done.20.refs_1_, bf16[512,1152]{1,0:T(8,128)(2,1)S(1)} %constant_dynamic-update-slice_fusion.refs_1_.refs_2_, ...), custom_call_target="tpu_custom_call" | custom-call | flops 6039797760 | tf_op jit(solution)/shard_map/grad/pallas_call | solution.py:394
  55.4 1.1 %grad_features.1 = bf16[128,384]{1,0:T(8,128)(2,1)} custom-call(s32[1]{0:T(128)} %bitcast.place_ref, bf16[384,1152]{1,0:T(8,128)(2,1)S(1)} %copy-done.1, f32[1,1152]{1,0:T(1,128)S(1)} %get-tuple-element.36.weight_sum_ref, bf16[128,1280]{1,0:T(8,128)(2,1)S(1)} %grad.3.refs_0_, bf16[128,1280]{1,0:T(8,128)(2,1)S(1)} %collective-permute-done.15.refs_1_, ...), custom_call_target="tpu_custom_call" | custom-call | tf_op jit(solution)/shard_map/grad_features/pallas_call | solution.py:431
  56.5 1.7 %weight.5 = f32[384,1152]{1,0:T(8,128)} custom-call(s32[1]{0:T(128)} %bitcast.place_ref, bf16[1024,384]{1,0:T(8,128)(2,1)S(1)} %constant_dynamic-update-slice_fusion.5.features_ref, bf16[128,1280]{1,0:T(8,128)(2,1)S(1)} %grad.5.refs_0_, bf16[128,1280]{1,0:T(8,128)(2,1)S(1)} %collective-permute-done.21.refs_1_, f32[384,1152]{1,0:T(8,128)S(1)} %weight.4.refs_2_), custom_call_target="tpu_custom_call" | custom-call | tf_op jit(solution)/shard_map/weight/pallas_call | solution.py:421
  (58 shorter events, 8.9 us)
Async XLA Ops:
  1.5 19.8 %copy-start.3 = (bf16[128,384]{1,0:T(8,128)(2,1)S(1)}, bf16[128,384]{1,0:T(8,128)(2,1)}, u32[]{:S(2)}) copy-start(bf16[128,384]{1,0:T(8,128)(2,1)} %features_ref.1) | copy-start | bytes 294916
  1.6 10.0 %collective-permute-start.4 = (bf16[32,1152]{1,0:T(8,128)(2,1)S(1)}, bf16[32,1152]{1,0:T(8,128)(2,1)S(1)}, u32[]{:S(2)}, u32[]{:S(2)}) collective-permute-start(bf16[32,1152]{1,0:T(8,128)(2,1)S(1)} %unit_texts.1), channel_id=1, source_target_pairs={{0,8},{1,9},{2,10},{3,11},{4,12},{5,13},{6,14},{7,15},{8,0},{9,1},... | collective-permute-start | bytes 221192 | tf_op jit(solution)/shard_map/ppermute | solution.py:317
  4.7 7.8 %collective-permute-start.3 = (bf16[32,1152]{1,0:T(8,128)(2,1)S(1)}, bf16[32,1152]{1,0:T(8,128)(2,1)S(1)}, u32[]{:S(2)}, u32[]{:S(2)}) collective-permute-start(bf16[32,1152]{1,0:T(8,128)(2,1)S(1)} %unit_texts.1), channel_id=1, source_target_pairs={{0,16},{1,17},{2,18},{3,19},{4,20},{5,21},{6,22},{7,23},{8,24},{9,... | collective-permute-start | bytes 221192 | tf_op jit(solution)/shard_map/ppermute | solution.py:317
  7.3 6.3 %collective-permute-start.2 = (bf16[32,1152]{1,0:T(8,128)(2,1)S(1)}, bf16[32,1152]{1,0:T(8,128)(2,1)S(1)}, u32[]{:S(2)}, u32[]{:S(2)}) collective-permute-start(bf16[32,1152]{1,0:T(8,128)(2,1)S(1)} %unit_texts.1), channel_id=1, source_target_pairs={{0,24},{1,25},{2,26},{3,27},{4,28},{5,29},{6,30},{7,31},{8,16},{9,... | collective-permute-start | bytes 221192 | tf_op jit(solution)/shard_map/ppermute | solution.py:317
  7.3 6.5 %collective-permute-start.1 = (bf16[128,384]{1,0:T(8,128)(2,1)}, bf16[128,384]{1,0:T(8,128)(2,1)S(1)}, u32[]{:S(2)}, u32[]{:S(2)}) collective-permute-start(bf16[128,384]{1,0:T(8,128)(2,1)} %features_ref.1), channel_id=1, source_target_pairs={{0,4},{1,5},{2,6},{3,7},{4,0},{5,1},{6,2},{7,3},{8,12},{9,13},{10,... | collective-permute-start | bytes 294920 | tf_op jit(solution)/shard_map/ppermute | solution.py:317
  11.5 2.1 %collective-permute-start = (bf16[64,1280]{1,0:T(8,128)(2,1)S(1)}, bf16[64,1280]{1,0:T(8,128)(2,1)S(1)}, u32[]{:S(2)}, u32[]{:S(2)}) collective-permute-start(bf16[64,1280]{1,0:T(8,128)(2,1)S(1)} %get-tuple-element.27), channel_id=1, source_target_pairs={{0,1},{1,0},{2,3},{3,2},{4,5},{5,4},{6,7},{7,6},{8,9},{9,8},{10,11... | collective-permute-start | bytes 491528 | tf_op jit(solution)/shard_map/ppermute | solution.py:317
  13.8 5.4 %collective-permute-start.5 = (bf16[32,1280]{1,0:T(8,128)(2,1)S(1)}, bf16[32,1280]{1,0:T(8,128)(2,1)S(1)}, u32[]{:S(2)}, u32[]{:S(2)}) collective-permute-start(bf16[32,1280]{1,0:T(8,128)(2,1)S(1)} %get-tuple-element.33), channel_id=1, source_target_pairs={{0,2},{1,3},{2,0},{3,1},{4,6},{5,7},{6,4},{7,5},{8,10},{9,11},{10,... | collective-permute-start | bytes 245768 | tf_op jit(solution)/shard_map/ppermute | solution.py:317
  15.4 13.5 %collective-permute-start.10 = (bf16[128,1152]{1,0:T(8,128)(2,1)S(1)}, bf16[128,1152]{1,0:T(8,128)(2,1)S(1)}, u32[]{:S(2)}, u32[]{:S(2)}) collective-permute-start(bf16[128,1152]{1,0:T(8,128)(2,1)S(1)} %pad_maximum_fusion.2), channel_id=1, source_target_pairs={{0,4},{1,5},{2,6},{3,7},{4,0},{5,1},{6,2},{7,3},{8,12},{9,13},{10,... | collective-permute-start | bytes 884744 | tf_op jit(solution)/shard_map/ppermute | solution.py:317
  16.8 14.1 %collective-permute-start.9 = (bf16[128,1152]{1,0:T(8,128)(2,1)S(1)}, bf16[128,1152]{1,0:T(8,128)(2,1)S(1)}, u32[]{:S(2)}, u32[]{:S(2)}) collective-permute-start(bf16[128,1152]{1,0:T(8,128)(2,1)S(1)} %pad_maximum_fusion.2), channel_id=1, source_target_pairs={{0,2},{1,3},{2,0},{3,1},{4,6},{5,7},{6,4},{7,5},{8,10},{9,11},{10,... | collective-permute-start | bytes 884744 | tf_op jit(solution)/shard_map/ppermute | solution.py:317
  19.3 6.4 %collective-permute-start.6 = (bf16[32,1280]{1,0:T(8,128)(2,1)S(1)}, bf16[32,1280]{1,0:T(8,128)(2,1)S(1)}, u32[]{:S(2)}, u32[]{:S(2)}) collective-permute-start(bf16[32,1280]{1,0:T(8,128)(2,1)S(1)} %get-tuple-element.37), channel_id=1, source_target_pairs={{0,16},{1,17},{2,18},{3,19},{4,20},{5,21},{6,22},{7,23},{8,24},{9,... | collective-permute-start | bytes 245768 | tf_op jit(solution)/shard_map/ppermute | solution.py:317
  25.7 7.3 %collective-permute-start.7 = (bf16[64,1280]{1,0:T(8,128)(2,1)S(1)}, bf16[64,1280]{1,0:T(8,128)(2,1)S(1)}, u32[]{:S(2)}, u32[]{:S(2)}) collective-permute-start(bf16[64,1280]{1,0:T(8,128)(2,1)S(1)} %pad_maximum_fusion.4), channel_id=1, source_target_pairs={{0,8},{1,9},{2,10},{3,11},{4,12},{5,13},{6,14},{7,15},{8,0},{9,1},... | collective-permute-start | bytes 491528 | tf_op jit(solution)/shard_map/ppermute | solution.py:317
  26.0 8.8 %collective-permute-start.8 = (bf16[256,384]{1,0:T(8,128)(2,1)S(1)}, bf16[256,384]{1,0:T(8,128)(2,1)S(1)}, u32[]{:S(2)}, u32[]{:S(2)}) collective-permute-start(bf16[256,384]{1,0:T(8,128)(2,1)S(1)} %pad_maximum_fusion.3), channel_id=1, source_target_pairs={{0,16},{1,17},{2,18},{3,19},{4,20},{5,21},{6,22},{7,23},{8,24},{9,... | collective-permute-start | bytes 589832 | tf_op jit(solution)/shard_map/ppermute | solution.py:317
  28.9 6.0 %collective-permute-start.11 = (bf16[64,1152]{1,0:T(8,128)(2,1)S(1)}, bf16[64,1152]{1,0:T(8,128)(2,1)S(1)}, u32[]{:S(2)}, u32[]{:S(2)}) collective-permute-start(bf16[64,1152]{1,0:T(8,128)(2,1)S(1)} %slice.16), channel_id=1, source_target_pairs={{0,2},{1,3},{2,0},{3,1},{4,6},{5,7},{6,4},{7,5},{8,10},{9,11},{10,... | collective-permute-start | bytes 442376 | tf_op jit(solution)/shard_map/ppermute | solution.py:317
  31.0 5.2 %collective-permute-start.12 = (bf16[64,1152]{1,0:T(8,128)(2,1)S(1)}, bf16[64,1152]{1,0:T(8,128)(2,1)S(1)}, u32[]{:S(2)}, u32[]{:S(2)}) collective-permute-start(bf16[64,1152]{1,0:T(8,128)(2,1)S(1)} %slice.17), channel_id=1, source_target_pairs={{0,4},{1,5},{2,6},{3,7},{4,0},{5,1},{6,2},{7,3},{8,12},{9,13},{10,... | collective-permute-start | bytes 442376 | tf_op jit(solution)/shard_map/ppermute | solution.py:317
  36.2 2.9 %collective-permute-start.13 = (bf16[512,1152]{1,0:T(8,128)(2,1)S(1)}, bf16[512,1152]{1,0:T(8,128)(2,1)S(1)}, u32[]{:S(2)}, u32[]{:S(2)}) collective-permute-start(bf16[512,1152]{1,0:T(8,128)(2,1)S(1)} %constant_dynamic-update-slice_fusion.refs_1_.refs_2_), channel_id=1, source_target_pairs={{0,1},{1,0},{2,3},{3,2},{4,5},{5,4},{6,7},{7,6},{8,9},{9,8},{10,11... | collective-permute-start | bytes 3538952 | tf_op jit(solution)/shard_map/ppermute | solution.py:317
  36.3 10.1 %collective-permute-start.16 = (bf16[128,1280]{1,0:T(8,128)(2,1)S(1)}, bf16[128,1280]{1,0:T(8,128)(2,1)S(1)}, u32[]{:S(2)}, u32[]{:S(2)}) collective-permute-start(bf16[128,1280]{1,0:T(8,128)(2,1)S(1)} %pad_maximum_fusion.1.refs_0_), channel_id=1, source_target_pairs={{0,4},{1,5},{2,6},{3,7},{4,0},{5,1},{6,2},{7,3},{8,12},{9,13},{10,... | collective-permute-start | bytes 983048 | tf_op jit(solution)/shard_map/ppermute | solution.py:317
  36.5 10.5 %collective-permute-start.14 = (bf16[128,1280]{1,0:T(8,128)(2,1)S(1)}, bf16[128,1280]{1,0:T(8,128)(2,1)S(1)}, u32[]{:S(2)}, u32[]{:S(2)}) collective-permute-start(bf16[128,1280]{1,0:T(8,128)(2,1)S(1)} %pad_maximum_fusion.1.refs_0_), channel_id=1, source_target_pairs={{0,2},{1,3},{2,0},{3,1},{4,6},{5,7},{6,4},{7,5},{8,10},{9,11},{10,... | collective-permute-start | bytes 983048 | tf_op jit(solution)/shard_map/ppermute | solution.py:317
  38.4 11.0 %collective-permute-start.18 = (bf16[512,384]{1,0:T(8,128)(2,1)S(1)}, bf16[512,384]{1,0:T(8,128)(2,1)S(1)}, u32[]{:S(2)}, u32[]{:S(2)}) collective-permute-start(bf16[512,384]{1,0:T(8,128)(2,1)S(1)} %pad_maximum_fusion), channel_id=1, source_target_pairs={{0,8},{1,9},{2,10},{3,11},{4,12},{5,13},{6,14},{7,15},{8,0},{9,1},... | collective-permute-start | bytes 1179656 | tf_op jit(solution)/shard_map/ppermute | solution.py:317
  40.7 8.8 %collective-permute-start.15 = (bf16[128,1280]{1,0:T(8,128)(2,1)S(1)}, bf16[128,1280]{1,0:T(8,128)(2,1)S(1)}, u32[]{:S(2)}, u32[]{:S(2)}) collective-permute-start(bf16[128,1280]{1,0:T(8,128)(2,1)S(1)} %grad.3.refs_0_), channel_id=1, source_target_pairs={{0,1},{1,0},{2,3},{3,2},{4,5},{5,4},{6,7},{7,6},{8,9},{9,8},{10,11... | collective-permute-start | bytes 983048 | tf_op jit(solution)/shard_map/ppermute | solution.py:317
  46.4 5.8 %collective-permute-start.19 = (bf16[64,1280]{1,0:T(8,128)(2,1)S(1)}, bf16[64,1280]{1,0:T(8,128)(2,1)S(1)}, u32[]{:S(2)}, u32[]{:S(2)}) collective-permute-start(bf16[64,1280]{1,0:T(8,128)(2,1)S(1)} %slice.18), channel_id=1, source_target_pairs={{0,2},{1,3},{2,0},{3,1},{4,6},{5,7},{6,4},{7,5},{8,10},{9,11},{10,... | collective-permute-start | bytes 491528 | tf_op jit(solution)/shard_map/ppermute | solution.py:317
  47.1 5.5 %collective-permute-start.20 = (bf16[64,1280]{1,0:T(8,128)(2,1)S(1)}, bf16[64,1280]{1,0:T(8,128)(2,1)S(1)}, u32[]{:S(2)}, u32[]{:S(2)}) collective-permute-start(bf16[64,1280]{1,0:T(8,128)(2,1)S(1)} %slice.19), channel_id=1, source_target_pairs={{0,4},{1,5},{2,6},{3,7},{4,0},{5,1},{6,2},{7,3},{8,12},{9,13},{10,... | collective-permute-start | bytes 491528 | tf_op jit(solution)/shard_map/ppermute | solution.py:317
  51.5 2.9 %collective-permute-start.17 = (bf16[256,1280]{1,0:T(8,128)(2,1)S(1)}, bf16[256,1280]{1,0:T(8,128)(2,1)S(1)}, u32[]{:S(2)}, u32[]{:S(2)}) collective-permute-start(bf16[256,1280]{1,0:T(8,128)(2,1)S(1)} %grad.4.refs_2_.refs_0_), channel_id=1, source_target_pairs={{0,1},{1,0},{2,3},{3,2},{4,5},{5,4},{6,7},{7,6},{8,9},{9,8},{10,11... | collective-permute-start | bytes 1966088 | tf_op jit(solution)/shard_map/ppermute | solution.py:317
  54.2 1.2 %copy-start.1 = (bf16[384,1152]{1,0:T(8,128)(2,1)S(1)}, bf16[384,1152]{1,0:T(8,128)(2,1)}, u32[]{:S(2)}) copy-start(bf16[384,1152]{1,0:T(8,128)(2,1)} %weight_ref.3) | copy-start | bytes 2654212
  54.2 2.2 %collective-permute-start.21 = (bf16[128,1280]{1,0:T(8,128)(2,1)S(1)}, bf16[128,1280]{1,0:T(8,128)(2,1)S(1)}, u32[]{:S(2)}, u32[]{:S(2)}) collective-permute-start(bf16[128,1280]{1,0:T(8,128)(2,1)S(1)} %grad.5.refs_0_), channel_id=1, source_target_pairs={{0,1},{1,0},{2,3},{3,2},{4,5},{5,4},{6,7},{7,6},{8,9},{9,8},{10,11... | collective-permute-start | bytes 983048 | tf_op jit(solution)/shard_map/ppermute | solution.py:317
  (3 other events, 2.9 us)

commit v4 on v1

--- a/solution.py
+++ b/solution.py
@@ -432,8 +432,8 @@
     *diagonal_rows, _, _ = lax.optimization_barrier((*diagonal_rows, grads[1], grad_weight))
     grads.append(gradient(3 * local_rows, *diagonal_rows))
     others.append(swap(grads[2], core))
-    grad_weight = add_product([1], [grad_weight])
-    grad_weight = add_product([2], [grad_weight], True)
+    grad_weight, grad_features = lax.optimization_barrier((grad_weight, grad_features))
+    grad_weight = add_product([1, 2], [grad_weight], True)
     return grad_features, grad_weight
 
 

time: 58.4 us -> 59 us (1.010)
  waiting for transfers between devices: 19.6 us -> 22.1 us
  starting transfers between devices: 23.9 us -> 22.4 us
    ppermute x22, waiting for transfers between devices: 19.6 us -> 22.1 us  [swap(): return lax.ppermute(value, axes, [(i, i ^ flip) for i in range(count)])]
    ppermute x22, starting transfers between devices: 23.9 us -> 22.4 us  [swap(): return lax.ppermute(value, axes, [(i, i ^ flip) for i in range(count)])]
    pallas_call x3 -> x2, Pallas kernels: 3.22 us -> 2.94 us  [add_product(): kernel_call(functools.partial(weight_body, rows, mp_count, gather_order,...]
  transfers between devices with their start and end apart: 22 -> 22, of which waited for: 12 -> 11; matrix products, arithmetic and copies ran while one was open for 1% -> 1% of each run, Pallas kernels for 15% -> 13%
where the time goes in v4:
time: 59 us; the launch traced here: 58.7 us
  starting transfers between devices  22.4 us (38%)
  waiting for transfers between devices  22.1 us (37%)
  Pallas kernels  10 us (17%)
  local copies, waits for them, and re-layouts  3.23 us (5%)
  between operations  0.88 us (1%)
    ppermute x22, starting transfers between devices, swap(): return lax.ppermute(value, axes, [(i, i ^ flip) for i in range(count)])  22.4 us
    ppermute x22, waiting for transfers between devices, swap(): return lax.ppermute(value, axes, [(i, i ^ flip) for i in range(count)])  22.1 us
    pallas_call x3, Pallas kernels, gradient(): kernel_call(functools.partial(grad_body, first, len(parts)), struct((tota...  5.22 us
    unnamed x16, local copies, waits for them, and re-layouts  3.11 us
    pallas_call x2, Pallas kernels, add_product(): kernel_call(functools.partial(weight_body, rows, mp_count, gather_order,...  2.94 us
  transfers between devices with their start and end apart: 22, of which 11 were waited for; matrix products, arithmetic and copies ran while one was open for 1% of the time, Pallas kernels for 13%

profile of v4, /device:TPU:0, one launch (start us, length us, event | category | flops | bytes accessed | tf_op | source)
XLA Modules:
  0.0 58.7 jit_solution(10021328283019301047)
XLA Ops:
  1.6 4.1 %collective-permute-start.2 = (bf16[32,1152]{1,0:T(8,128)(2,1)S(1)}, bf16[32,1152]{1,0:T(8,128)(2,1)S(1)}, u32[]{:S(2)}, u32[]{:S(2)}) collective-permute-start(bf16[32,1152]{1,0:T(8,128)(2,1)S(1)} %unit_texts.1), channel_id=1, source_target_pairs={{0,16},{1,17},{2,18},{3,19},{4,20},{5,21},{6,22},{7,23},{8,24},{9,... | collective-permute-start | bytes 221192 | tf_op jit(solution)/shard_map/ppermute | solution.py:312
  5.7 1.6 %collective-permute-start.3 = (bf16[32,1152]{1,0:T(8,128)(2,1)S(1)}, bf16[32,1152]{1,0:T(8,128)(2,1)S(1)}, u32[]{:S(2)}, u32[]{:S(2)}) collective-permute-start(bf16[32,1152]{1,0:T(8,128)(2,1)S(1)} %unit_texts.1), channel_id=1, source_target_pairs={{0,8},{1,9},{2,10},{3,11},{4,12},{5,13},{6,14},{7,15},{8,0},{9,1},... | collective-permute-start | bytes 221192 | tf_op jit(solution)/shard_map/ppermute | solution.py:312
  7.3 1.7 %collective-permute-start.1 = (bf16[128,384]{1,0:T(8,128)(2,1)}, bf16[128,384]{1,0:T(8,128)(2,1)S(1)}, u32[]{:S(2)}, u32[]{:S(2)}) collective-permute-start(bf16[128,384]{1,0:T(8,128)(2,1)} %features_ref.1), channel_id=1, source_target_pairs={{0,4},{1,5},{2,6},{3,7},{4,0},{5,1},{6,2},{7,3},{8,12},{9,13},{10,... | collective-permute-start | bytes 294920 | tf_op jit(solution)/shard_map/ppermute | solution.py:312
  9.0 1.2 %copy-done = bf16[384,1152]{1,0:T(8,128)(2,1)S(1)} copy-done((bf16[384,1152]{1,0:T(8,128)(2,1)S(1)}, bf16[384,1152]{1,0:T(8,128)(2,1)}, u32[]{:S(2)}) %copy-start) | copy-done | bytes 884760
  11.6 1.9 %collective-permute-done.4 = bf16[32,1152]{1,0:T(8,128)(2,1)S(1)} collective-permute-done((bf16[32,1152]{1,0:T(8,128)(2,1)S(1)}, bf16[32,1152]{1,0:T(8,128)(2,1)S(1)}, u32[]{:S(2)}, u32[]{:S(2)}) %collective-permute-start.4) | collective-permute-done | bytes 73760 | tf_op jit(solution)/shard_map/ppermute | solution.py:312
  13.7 1.6 %collective-permute-start.5 = (bf16[32,1280]{1,0:T(8,128)(2,1)S(1)}, bf16[32,1280]{1,0:T(8,128)(2,1)S(1)}, u32[]{:S(2)}, u32[]{:S(2)}) collective-permute-start(bf16[32,1280]{1,0:T(8,128)(2,1)S(1)} %get-tuple-element.35), channel_id=1, source_target_pairs={{0,2},{1,3},{2,0},{3,1},{4,6},{5,7},{6,4},{7,5},{8,10},{9,11},{10,... | collective-permute-start | bytes 245768 | tf_op jit(solution)/shard_map/ppermute | solution.py:312
  15.2 1.5 %collective-permute-start.10 = (bf16[128,1152]{1,0:T(8,128)(2,1)S(1)}, bf16[128,1152]{1,0:T(8,128)(2,1)S(1)}, u32[]{:S(2)}, u32[]{:S(2)}) collective-permute-start(bf16[128,1152]{1,0:T(8,128)(2,1)S(1)} %pad_maximum_fusion.2), channel_id=1, source_target_pairs={{0,4},{1,5},{2,6},{3,7},{4,0},{5,1},{6,2},{7,3},{8,12},{9,13},{10,... | collective-permute-start | bytes 884744 | tf_op jit(solution)/shard_map/ppermute | solution.py:312
  17.2 1.7 %collective-permute-done.5.received_ref = bf16[32,1280]{1,0:T(8,128)(2,1)S(1)} collective-permute-done((bf16[32,1280]{1,0:T(8,128)(2,1)S(1)}, bf16[32,1280]{1,0:T(8,128)(2,1)S(1)}, u32[]{:S(2)}, u32[]{:S(2)}) %collective-permute-start.5) | collective-permute-done | bytes 81952 | tf_op jit(solution)/shard_map/ppermute | solution.py:312
  19.1 1.2 %collective-permute-start.6 = (bf16[32,1280]{1,0:T(8,128)(2,1)S(1)}, bf16[32,1280]{1,0:T(8,128)(2,1)S(1)}, u32[]{:S(2)}, u32[]{:S(2)}) collective-permute-start(bf16[32,1280]{1,0:T(8,128)(2,1)S(1)} %get-tuple-element.38), channel_id=1, source_target_pairs={{0,16},{1,17},{2,18},{3,19},{4,20},{5,21},{6,22},{7,23},{8,24},{9,... | collective-permute-start | bytes 245768 | tf_op jit(solution)/shard_map/ppermute | solution.py:312
  20.3 4.9 %collective-permute-done.6 = bf16[32,1280]{1,0:T(8,128)(2,1)S(1)} collective-permute-done((bf16[32,1280]{1,0:T(8,128)(2,1)S(1)}, bf16[32,1280]{1,0:T(8,128)(2,1)S(1)}, u32[]{:S(2)}, u32[]{:S(2)}) %collective-permute-start.6) | collective-permute-done | bytes 81952 | tf_op jit(solution)/shard_map/ppermute | solution.py:312
  25.3 2.8 %collective-permute-start.8 = (bf16[256,384]{1,0:T(8,128)(2,1)S(1)}, bf16[256,384]{1,0:T(8,128)(2,1)S(1)}, u32[]{:S(2)}, u32[]{:S(2)}) collective-permute-start(bf16[256,384]{1,0:T(8,128)(2,1)S(1)} %pad_maximum_fusion.3), channel_id=1, source_target_pairs={{0,16},{1,17},{2,18},{3,19},{4,20},{5,21},{6,22},{7,23},{8,24},{9,... | collective-permute-start | bytes 589832 | tf_op jit(solution)/shard_map/ppermute | solution.py:312
  28.2 2.3 %collective-permute-start.12 = (bf16[64,1152]{1,0:T(8,128)(2,1)S(1)}, bf16[64,1152]{1,0:T(8,128)(2,1)S(1)}, u32[]{:S(2)}, u32[]{:S(2)}) collective-permute-start(bf16[64,1152]{1,0:T(8,128)(2,1)S(1)} %slice.16), channel_id=1, source_target_pairs={{0,2},{1,3},{2,0},{3,1},{4,6},{5,7},{6,4},{7,5},{8,10},{9,11},{10,... | collective-permute-start | bytes 442376 | tf_op jit(solution)/shard_map/ppermute | solution.py:312
  30.8 1.6 %collective-permute-done.7 = bf16[64,1280]{1,0:T(8,128)(2,1)S(1)} collective-permute-done((bf16[64,1280]{1,0:T(8,128)(2,1)S(1)}, bf16[64,1280]{1,0:T(8,128)(2,1)S(1)}, u32[]{:S(2)}, u32[]{:S(2)}) %collective-permute-start.7) | collective-permute-done | bytes 163872 | tf_op jit(solution)/shard_map/ppermute | solution.py:312
  32.4 2.4 %collective-permute-done.8 = bf16[256,384]{1,0:T(8,128)(2,1)S(1)} collective-permute-done((bf16[256,384]{1,0:T(8,128)(2,1)S(1)}, bf16[256,384]{1,0:T(8,128)(2,1)S(1)}, u32[]{:S(2)}, u32[]{:S(2)}) %collective-permute-start.8) | collective-permute-done | bytes 196640 | tf_op jit(solution)/shard_map/ppermute | solution.py:312
  36.7 1.7 %collective-permute-start.11 = (bf16[512,384]{1,0:T(8,128)(2,1)S(1)}, bf16[512,384]{1,0:T(8,128)(2,1)S(1)}, u32[]{:S(2)}, u32[]{:S(2)}) collective-permute-start(bf16[512,384]{1,0:T(8,128)(2,1)S(1)} %pad_maximum_fusion), channel_id=1, source_target_pairs={{0,8},{1,9},{2,10},{3,11},{4,12},{5,13},{6,14},{7,15},{8,0},{9,1},... | collective-permute-start | bytes 1179656 | tf_op jit(solution)/shard_map/ppermute | solution.py:312
  38.6 1.6 %grad.3.refs_0_ = bf16[128,1280]{1,0:T(8,128)(2,1)S(1)} custom-call(bf16[128,1280]{1,0:T(8,128)(2,1)S(1)} %pad_maximum_fusion.1.refs_0_, bf16[512,1152]{1,0:T(8,128)(2,1)S(1)} %constant_dynamic-update-slice_fusion.3.refs_1_.refs_2_, bf16[512,1152]{1,0:T(8,128)(2,1)S(1)} %collective-permute-done.14.refs_2_.refs_3_), custom_call_target="tpu_custom_call" | custom-call | flops 6039797760 | tf_op jit(solution)/shard_map/grad/pallas_call | solution.py:388
  40.5 5.9 %collective-permute-done.17.refs_1_ = bf16[128,1280]{1,0:T(8,128)(2,1)S(1)} collective-permute-done((bf16[128,1280]{1,0:T(8,128)(2,1)S(1)}, bf16[128,1280]{1,0:T(8,128)(2,1)S(1)}, u32[]{:S(2)}, u32[]{:S(2)}) %collective-permute-start.17) | collective-permute-done | bytes 327712 | tf_op jit(solution)/shard_map/ppermute | solution.py:312
  46.4 1.3 %collective-permute-start.19 = (bf16[64,1280]{1,0:T(8,128)(2,1)S(1)}, bf16[64,1280]{1,0:T(8,128)(2,1)S(1)}, u32[]{:S(2)}, u32[]{:S(2)}) collective-permute-start(bf16[64,1280]{1,0:T(8,128)(2,1)S(1)} %slice.18), channel_id=1, source_target_pairs={{0,2},{1,3},{2,0},{3,1},{4,6},{5,7},{6,4},{7,5},{8,10},{9,11},{10,... | collective-permute-start | bytes 491528 | tf_op jit(solution)/shard_map/ppermute | solution.py:312
  48.2 2.0 %grad.4.refs_2_.refs_0_ = bf16[256,1280]{1,0:T(8,128)(2,1)S(1)} custom-call(bf16[128,1280]{1,0:T(8,128)(2,1)S(1)} %collective-permute-done.15.refs_0_, bf16[128,1280]{1,0:T(8,128)(2,1)S(1)} %collective-permute-done.17.refs_1_, bf16[512,1152]{1,0:T(8,128)(2,1)S(1)} %constant_dynamic-update-slice_fusion.3.refs_1_.refs_2_, ...), custom_call_target="tpu_custom_call" | custom-call | flops 12079595520 | tf_op jit(solution)/shard_map/grad/pallas_call | solution.py:388
  50.9 1.0 %collective-permute-done.19.refs_0_ = bf16[64,1280]{1,0:T(8,128)(2,1)S(1)} collective-permute-done((bf16[64,1280]{1,0:T(8,128)(2,1)S(1)}, bf16[64,1280]{1,0:T(8,128)(2,1)S(1)}, u32[]{:S(2)}, u32[]{:S(2)}) %collective-permute-start.19) | collective-permute-done | bytes 163872 | tf_op jit(solution)/shard_map/ppermute | solution.py:312
  51.9 1.2 %collective-permute-done.20.refs_1_ = bf16[64,1280]{1,0:T(8,128)(2,1)S(1)} collective-permute-done((bf16[64,1280]{1,0:T(8,128)(2,1)S(1)}, bf16[64,1280]{1,0:T(8,128)(2,1)S(1)}, u32[]{:S(2)}, u32[]{:S(2)}) %collective-permute-start.20) | collective-permute-done | bytes 163872 | tf_op jit(solution)/shard_map/ppermute | solution.py:312
  53.1 1.6 %grad.5.refs_2_ = bf16[128,1280]{1,0:T(8,128)(2,1)S(1)} custom-call(bf16[64,1280]{1,0:T(8,128)(2,1)S(1)} %collective-permute-done.19.refs_0_, bf16[64,1280]{1,0:T(8,128)(2,1)S(1)} %collective-permute-done.20.refs_1_, bf16[512,1152]{1,0:T(8,128)(2,1)S(1)} %constant_dynamic-update-slice_fusion.3.refs_1_.refs_2_, ...), custom_call_target="tpu_custom_call" | custom-call | flops 6039797760 | tf_op jit(solution)/shard_map/grad/pallas_call | solution.py:388
  54.8 1.1 %grad_features.1 = bf16[128,384]{1,0:T(8,128)(2,1)} custom-call(s32[1]{0:T(128)} %bitcast.place_ref, bf16[384,1152]{1,0:T(8,128)(2,1)S(1)} %copy-done.1, f32[1,1152]{1,0:T(1,128)S(1)} %get-tuple-element.48.weight_sum_ref, bf16[128,1280]{1,0:T(8,128)(2,1)S(1)} %grad.3.refs_0_, bf16[128,1280]{1,0:T(8,128)(2,1)S(1)} %collective-permute-done.16.refs_1_, ...), custom_call_target="tpu_custom_call" | custom-call | tf_op jit(solution)/shard_map/grad_features/pallas_call | solution.py:423
  56.4 2.3 %weight.3 = f32[384,1152]{1,0:T(8,128)} custom-call(s32[1]{0:T(128)} %bitcast.place_ref, bf16[1024,384]{1,0:T(8,128)(2,1)S(1)} %constant_dynamic-update-slice_fusion.features_ref, bf16[256,1280]{1,0:T(8,128)(2,1)S(1)} %grad.4.refs_2_.refs_0_, bf16[256,1280]{1,0:T(8,128)(2,1)S(1)} %collective-permute-done.18.refs_3_.refs_1_, ...), custom_call_target="tpu_custom_call" | custom-call | tf_op jit(solution)/shard_map/weight/pallas_call | solution.py:413
  (57 shorter events, 7.8 us)
Async XLA Ops:
  1.5 18.8 %copy-start.3 = (bf16[128,384]{1,0:T(8,128)(2,1)S(1)}, bf16[128,384]{1,0:T(8,128)(2,1)}, u32[]{:S(2)}) copy-start(bf16[128,384]{1,0:T(8,128)(2,1)} %features_ref.1) | copy-start | bytes 294916
  1.6 10.0 %collective-permute-start.2 = (bf16[32,1152]{1,0:T(8,128)(2,1)S(1)}, bf16[32,1152]{1,0:T(8,128)(2,1)S(1)}, u32[]{:S(2)}, u32[]{:S(2)}) collective-permute-start(bf16[32,1152]{1,0:T(8,128)(2,1)S(1)} %unit_texts.1), channel_id=1, source_target_pairs={{0,16},{1,17},{2,18},{3,19},{4,20},{5,21},{6,22},{7,23},{8,24},{9,... | collective-permute-start | bytes 221192 | tf_op jit(solution)/shard_map/ppermute | solution.py:312
  5.7 5.9 %collective-permute-start.3 = (bf16[32,1152]{1,0:T(8,128)(2,1)S(1)}, bf16[32,1152]{1,0:T(8,128)(2,1)S(1)}, u32[]{:S(2)}, u32[]{:S(2)}) collective-permute-start(bf16[32,1152]{1,0:T(8,128)(2,1)S(1)} %unit_texts.1), channel_id=1, source_target_pairs={{0,8},{1,9},{2,10},{3,11},{4,12},{5,13},{6,14},{7,15},{8,0},{9,1},... | collective-permute-start | bytes 221192 | tf_op jit(solution)/shard_map/ppermute | solution.py:312
  7.3 6.2 %collective-permute-start.4 = (bf16[32,1152]{1,0:T(8,128)(2,1)S(1)}, bf16[32,1152]{1,0:T(8,128)(2,1)S(1)}, u32[]{:S(2)}, u32[]{:S(2)}) collective-permute-start(bf16[32,1152]{1,0:T(8,128)(2,1)S(1)} %unit_texts.1), channel_id=1, source_target_pairs={{0,24},{1,25},{2,26},{3,27},{4,28},{5,29},{6,30},{7,31},{8,16},{9,... | collective-permute-start | bytes 221192 | tf_op jit(solution)/shard_map/ppermute | solution.py:312
  7.3 6.3 %collective-permute-start.1 = (bf16[128,384]{1,0:T(8,128)(2,1)}, bf16[128,384]{1,0:T(8,128)(2,1)S(1)}, u32[]{:S(2)}, u32[]{:S(2)}) collective-permute-start(bf16[128,384]{1,0:T(8,128)(2,1)} %features_ref.1), channel_id=1, source_target_pairs={{0,4},{1,5},{2,6},{3,7},{4,0},{5,1},{6,2},{7,3},{8,12},{9,13},{10,... | collective-permute-start | bytes 294920 | tf_op jit(solution)/shard_map/ppermute | solution.py:312
  11.5 2.0 %collective-permute-start = (bf16[64,1280]{1,0:T(8,128)(2,1)S(1)}, bf16[64,1280]{1,0:T(8,128)(2,1)S(1)}, u32[]{:S(2)}, u32[]{:S(2)}) collective-permute-start(bf16[64,1280]{1,0:T(8,128)(2,1)S(1)} %get-tuple-element.29), channel_id=1, source_target_pairs={{0,1},{1,0},{2,3},{3,2},{4,5},{5,4},{6,7},{7,6},{8,9},{9,8},{10,11... | collective-permute-start | bytes 491528 | tf_op jit(solution)/shard_map/ppermute | solution.py:312
  13.7 5.3 %collective-permute-start.5 = (bf16[32,1280]{1,0:T(8,128)(2,1)S(1)}, bf16[32,1280]{1,0:T(8,128)(2,1)S(1)}, u32[]{:S(2)}, u32[]{:S(2)}) collective-permute-start(bf16[32,1280]{1,0:T(8,128)(2,1)S(1)} %get-tuple-element.35), channel_id=1, source_target_pairs={{0,2},{1,3},{2,0},{3,1},{4,6},{5,7},{6,4},{7,5},{8,10},{9,11},{10,... | collective-permute-start | bytes 245768 | tf_op jit(solution)/shard_map/ppermute | solution.py:312
  15.2 12.9 %collective-permute-start.10 = (bf16[128,1152]{1,0:T(8,128)(2,1)S(1)}, bf16[128,1152]{1,0:T(8,128)(2,1)S(1)}, u32[]{:S(2)}, u32[]{:S(2)}) collective-permute-start(bf16[128,1152]{1,0:T(8,128)(2,1)S(1)} %pad_maximum_fusion.2), channel_id=1, source_target_pairs={{0,4},{1,5},{2,6},{3,7},{4,0},{5,1},{6,2},{7,3},{8,12},{9,13},{10,... | collective-permute-start | bytes 884744 | tf_op jit(solution)/shard_map/ppermute | solution.py:312
  16.7 13.7 %collective-permute-start.9 = (bf16[128,1152]{1,0:T(8,128)(2,1)S(1)}, bf16[128,1152]{1,0:T(8,128)(2,1)S(1)}, u32[]{:S(2)}, u32[]{:S(2)}) collective-permute-start(bf16[128,1152]{1,0:T(8,128)(2,1)S(1)} %pad_maximum_fusion.2), channel_id=1, source_target_pairs={{0,2},{1,3},{2,0},{3,1},{4,6},{5,7},{6,4},{7,5},{8,10},{9,11},{10,... | collective-permute-start | bytes 884744 | tf_op jit(solution)/shard_map/ppermute | solution.py:312
  19.1 6.1 %collective-permute-start.6 = (bf16[32,1280]{1,0:T(8,128)(2,1)S(1)}, bf16[32,1280]{1,0:T(8,128)(2,1)S(1)}, u32[]{:S(2)}, u32[]{:S(2)}) collective-permute-start(bf16[32,1280]{1,0:T(8,128)(2,1)S(1)} %get-tuple-element.38), channel_id=1, source_target_pairs={{0,16},{1,17},{2,18},{3,19},{4,20},{5,21},{6,22},{7,23},{8,24},{9,... | collective-permute-start | bytes 245768 | tf_op jit(solution)/shard_map/ppermute | solution.py:312
  25.2 7.1 %collective-permute-start.7 = (bf16[64,1280]{1,0:T(8,128)(2,1)S(1)}, bf16[64,1280]{1,0:T(8,128)(2,1)S(1)}, u32[]{:S(2)}, u32[]{:S(2)}) collective-permute-start(bf16[64,1280]{1,0:T(8,128)(2,1)S(1)} %pad_maximum_fusion.4), channel_id=1, source_target_pairs={{0,8},{1,9},{2,10},{3,11},{4,12},{5,13},{6,14},{7,15},{8,0},{9,1},... | collective-permute-start | bytes 491528 | tf_op jit(solution)/shard_map/ppermute | solution.py:312
  25.3 9.5 %collective-permute-start.8 = (bf16[256,384]{1,0:T(8,128)(2,1)S(1)}, bf16[256,384]{1,0:T(8,128)(2,1)S(1)}, u32[]{:S(2)}, u32[]{:S(2)}) collective-permute-start(bf16[256,384]{1,0:T(8,128)(2,1)S(1)} %pad_maximum_fusion.3), channel_id=1, source_target_pairs={{0,16},{1,17},{2,18},{3,19},{4,20},{5,21},{6,22},{7,23},{8,24},{9,... | collective-permute-start | bytes 589832 | tf_op jit(solution)/shard_map/ppermute | solution.py:312
  28.2 6.7 %collective-permute-start.12 = (bf16[64,1152]{1,0:T(8,128)(2,1)S(1)}, bf16[64,1152]{1,0:T(8,128)(2,1)S(1)}, u32[]{:S(2)}, u32[]{:S(2)}) collective-permute-start(bf16[64,1152]{1,0:T(8,128)(2,1)S(1)} %slice.16), channel_id=1, source_target_pairs={{0,2},{1,3},{2,0},{3,1},{4,6},{5,7},{6,4},{7,5},{8,10},{9,11},{10,... | collective-permute-start | bytes 442376 | tf_op jit(solution)/shard_map/ppermute | solution.py:312
  30.4 5.2 %collective-permute-start.13 = (bf16[64,1152]{1,0:T(8,128)(2,1)S(1)}, bf16[64,1152]{1,0:T(8,128)(2,1)S(1)}, u32[]{:S(2)}, u32[]{:S(2)}) collective-permute-start(bf16[64,1152]{1,0:T(8,128)(2,1)S(1)} %slice.17), channel_id=1, source_target_pairs={{0,4},{1,5},{2,6},{3,7},{4,0},{5,1},{6,2},{7,3},{8,12},{9,13},{10,... | collective-permute-start | bytes 442376 | tf_op jit(solution)/shard_map/ppermute | solution.py:312
  35.7 2.9 %collective-permute-start.14 = (bf16[512,1152]{1,0:T(8,128)(2,1)S(1)}, bf16[512,1152]{1,0:T(8,128)(2,1)S(1)}, u32[]{:S(2)}, u32[]{:S(2)}) collective-permute-start(bf16[512,1152]{1,0:T(8,128)(2,1)S(1)} %constant_dynamic-update-slice_fusion.3.refs_1_.refs_2_), channel_id=1, source_target_pairs={{0,1},{1,0},{2,3},{3,2},{4,5},{5,4},{6,7},{7,6},{8,9},{9,8},{10,11... | collective-permute-start | bytes 3538952 | tf_op jit(solution)/shard_map/ppermute | solution.py:312
  35.7 12.0 %collective-permute-start.15 = (bf16[128,1280]{1,0:T(8,128)(2,1)S(1)}, bf16[128,1280]{1,0:T(8,128)(2,1)S(1)}, u32[]{:S(2)}, u32[]{:S(2)}) collective-permute-start(bf16[128,1280]{1,0:T(8,128)(2,1)S(1)} %pad_maximum_fusion.1.refs_0_), channel_id=1, source_target_pairs={{0,2},{1,3},{2,0},{3,1},{4,6},{5,7},{6,4},{7,5},{8,10},{9,11},{10,... | collective-permute-start | bytes 983048 | tf_op jit(solution)/shard_map/ppermute | solution.py:312
  36.6 9.8 %collective-permute-start.17 = (bf16[128,1280]{1,0:T(8,128)(2,1)S(1)}, bf16[128,1280]{1,0:T(8,128)(2,1)S(1)}, u32[]{:S(2)}, u32[]{:S(2)}) collective-permute-start(bf16[128,1280]{1,0:T(8,128)(2,1)S(1)} %pad_maximum_fusion.1.refs_0_), channel_id=1, source_target_pairs={{0,4},{1,5},{2,6},{3,7},{4,0},{5,1},{6,2},{7,3},{8,12},{9,13},{10,... | collective-permute-start | bytes 983048 | tf_op jit(solution)/shard_map/ppermute | solution.py:312
  36.7 11.4 %collective-permute-start.11 = (bf16[512,384]{1,0:T(8,128)(2,1)S(1)}, bf16[512,384]{1,0:T(8,128)(2,1)S(1)}, u32[]{:S(2)}, u32[]{:S(2)}) collective-permute-start(bf16[512,384]{1,0:T(8,128)(2,1)S(1)} %pad_maximum_fusion), channel_id=1, source_target_pairs={{0,8},{1,9},{2,10},{3,11},{4,12},{5,13},{6,14},{7,15},{8,0},{9,1},... | collective-permute-start | bytes 1179656 | tf_op jit(solution)/shard_map/ppermute | solution.py:312
  40.2 8.0 %collective-permute-start.16 = (bf16[128,1280]{1,0:T(8,128)(2,1)S(1)}, bf16[128,1280]{1,0:T(8,128)(2,1)S(1)}, u32[]{:S(2)}, u32[]{:S(2)}) collective-permute-start(bf16[128,1280]{1,0:T(8,128)(2,1)S(1)} %grad.3.refs_0_), channel_id=1, source_target_pairs={{0,1},{1,0},{2,3},{3,2},{4,5},{5,4},{6,7},{7,6},{8,9},{9,8},{10,11... | collective-permute-start | bytes 983048 | tf_op jit(solution)/shard_map/ppermute | solution.py:312
  46.4 5.5 %collective-permute-start.19 = (bf16[64,1280]{1,0:T(8,128)(2,1)S(1)}, bf16[64,1280]{1,0:T(8,128)(2,1)S(1)}, u32[]{:S(2)}, u32[]{:S(2)}) collective-permute-start(bf16[64,1280]{1,0:T(8,128)(2,1)S(1)} %slice.18), channel_id=1, source_target_pairs={{0,2},{1,3},{2,0},{3,1},{4,6},{5,7},{6,4},{7,5},{8,10},{9,11},{10,... | collective-permute-start | bytes 491528 | tf_op jit(solution)/shard_map/ppermute | solution.py:312
  47.7 5.4 %collective-permute-start.20 = (bf16[64,1280]{1,0:T(8,128)(2,1)S(1)}, bf16[64,1280]{1,0:T(8,128)(2,1)S(1)}, u32[]{:S(2)}, u32[]{:S(2)}) collective-permute-start(bf16[64,1280]{1,0:T(8,128)(2,1)S(1)} %slice.19), channel_id=1, source_target_pairs={{0,4},{1,5},{2,6},{3,7},{4,0},{5,1},{6,2},{7,3},{8,12},{9,13},{10,... | collective-permute-start | bytes 491528 | tf_op jit(solution)/shard_map/ppermute | solution.py:312
  50.2 4.6 %collective-permute-start.18 = (bf16[256,1280]{1,0:T(8,128)(2,1)S(1)}, bf16[256,1280]{1,0:T(8,128)(2,1)S(1)}, u32[]{:S(2)}, u32[]{:S(2)}) collective-permute-start(bf16[256,1280]{1,0:T(8,128)(2,1)S(1)} %grad.4.refs_2_.refs_0_), channel_id=1, source_target_pairs={{0,1},{1,0},{2,3},{3,2},{4,5},{5,4},{6,7},{7,6},{8,9},{9,8},{10,11... | collective-permute-start | bytes 1966088 | tf_op jit(solution)/shard_map/ppermute | solution.py:312
  50.9 3.9 %copy-start.1 = (bf16[384,1152]{1,0:T(8,128)(2,1)S(1)}, bf16[384,1152]{1,0:T(8,128)(2,1)}, u32[]{:S(2)}) copy-start(bf16[384,1152]{1,0:T(8,128)(2,1)} %weight_ref.3) | copy-start | bytes 2654212
  54.7 1.7 %collective-permute-start.21 = (bf16[128,1280]{1,0:T(8,128)(2,1)S(1)}, bf16[128,1280]{1,0:T(8,128)(2,1)S(1)}, u32[]{:S(2)}, u32[]{:S(2)}) collective-permute-start(bf16[128,1280]{1,0:T(8,128)(2,1)S(1)} %grad.5.refs_2_), channel_id=1, source_target_pairs={{0,1},{1,0},{2,3},{3,2},{4,5},{5,4},{6,7},{7,6},{8,9},{9,8},{10,11... | collective-permute-start | bytes 983048 | tf_op jit(solution)/shard_map/ppermute | solution.py:312
  (3 other events, 2.9 us)

commit v5 on v1

--- a/solution.py
+++ b/solution.py
@@ -263,18 +263,18 @@
         outs[0][...] = total
         return
     out_hbm, total_ref, sent = outs
-    wide = gradient.shape[1] // tiles
+    high = normed.shape[1] // tiles
     copies = []
     for k in range(tiles):
-        here = slice(k * wide, (k + 1) * wide)
+        here = slice(k * high, (k + 1) * high)
         total = lax.dot_general(
-            normed, gradient[:, here], (((0,), (0,)), ((), ())), preferred_element_type=jnp.float32
+            normed[:, here], gradient, (((0,), (0,)), ((), ())), preferred_element_type=jnp.float32
         )
         for ref in previous:
-            total = total + ref[:, here]
-        total_ref[:, here] = total
+            total = total + ref[here, :]
+        total_ref[here, :] = total
         copies.append(
-            pltpu.make_async_copy(total_ref.at[:, here], out_hbm.at[:, here], sent.at[k])
+            pltpu.make_async_copy(total_ref.at[here, :], out_hbm.at[here, :], sent.at[k])
         )
         copies[-1].start()
     for copy in copies:

time: 58.4 us -> 58.4 us (level)
  no operation moved by 1% of the time
where the time goes in v5:
time: 58.4 us; the launch traced here: 58.1 us
  starting transfers between devices  23.9 us (41%)
  waiting for transfers between devices  19.6 us (34%)
  Pallas kernels  10.3 us (18%)
  local copies, waits for them, and re-layouts  3.39 us (6%)
  between operations  0.85 us (1%)
    ppermute x22, starting transfers between devices, swap(): return lax.ppermute(value, axes, [(i, i ^ flip) for i in range(count)])  23.9 us
    ppermute x22, waiting for transfers between devices, swap(): return lax.ppermute(value, axes, [(i, i ^ flip) for i in range(count)])  19.6 us
    pallas_call x3, Pallas kernels, gradient(): kernel_call(functools.partial(grad_body, first, len(parts)), struct((tota...  5.18 us
    unnamed x16, local copies, waits for them, and re-layouts  3.26 us
    pallas_call x3, Pallas kernels, add_product(): kernel_call(functools.partial(weight_body, rows, mp_count, gather_order,...  3.23 us
  transfers between devices with their start and end apart: 22, of which 12 were waited for; matrix products, arithmetic and copies ran while one was open for 1% of the time, Pallas kernels for 15%

profile of v5, /device:TPU:0, one launch (start us, length us, event | category | flops | bytes accessed | tf_op | source)
XLA Modules:
  0.0 58.1 jit_solution(6078543026307696279)
XLA Ops:
  0.6 0.9 %copy-done.4 = bf16[32,1152]{1,0:T(8,128)(2,1)S(1)} copy-done((bf16[32,1152]{1,0:T(8,128)(2,1)S(1)}, bf16[32,1152]{1,0:T(8,128)(2,1)}, u32[]{:S(2)}) %copy-start.4) | copy-done | bytes 73752
  1.6 5.1 %collective-permute-start.4 = (bf16[32,1152]{1,0:T(8,128)(2,1)S(1)}, bf16[32,1152]{1,0:T(8,128)(2,1)S(1)}, u32[]{:S(2)}, u32[]{:S(2)}) collective-permute-start(bf16[32,1152]{1,0:T(8,128)(2,1)S(1)} %unit_texts.1), channel_id=1, source_target_pairs={{0,24},{1,25},{2,26},{3,27},{4,28},{5,29},{6,30},{7,31},{8,16},{9,... | collective-permute-start | bytes 221192 | tf_op jit(solution)/shard_map/ppermute | solution.py:312
  7.4 1.6 %collective-permute-start.1 = (bf16[128,384]{1,0:T(8,128)(2,1)}, bf16[128,384]{1,0:T(8,128)(2,1)S(1)}, u32[]{:S(2)}, u32[]{:S(2)}) collective-permute-start(bf16[128,384]{1,0:T(8,128)(2,1)} %features_ref.1), channel_id=1, source_target_pairs={{0,4},{1,5},{2,6},{3,7},{4,0},{5,1},{6,2},{7,3},{8,12},{9,13},{10,... | collective-permute-start | bytes 294920 | tf_op jit(solution)/shard_map/ppermute | solution.py:312
  9.0 1.2 %copy-done = bf16[384,1152]{1,0:T(8,128)(2,1)S(1)} copy-done((bf16[384,1152]{1,0:T(8,128)(2,1)S(1)}, bf16[384,1152]{1,0:T(8,128)(2,1)}, u32[]{:S(2)}) %copy-start) | copy-done | bytes 884760
  10.2 0.9 %copy-done.2 = bf16[128,384]{1,0:T(8,128)(2,1)S(1)} copy-done((bf16[128,384]{1,0:T(8,128)(2,1)S(1)}, bf16[128,384]{1,0:T(8,128)(2,1)}, u32[]{:S(2)}) %copy-start.2) | copy-done | bytes 98328
  13.1 1.6 %collective-permute-start.5 = (bf16[32,1280]{1,0:T(8,128)(2,1)S(1)}, bf16[32,1280]{1,0:T(8,128)(2,1)S(1)}, u32[]{:S(2)}, u32[]{:S(2)}) collective-permute-start(bf16[32,1280]{1,0:T(8,128)(2,1)S(1)} %get-tuple-element.33), channel_id=1, source_target_pairs={{0,2},{1,3},{2,0},{3,1},{4,6},{5,7},{6,4},{7,5},{8,10},{9,11},{10,... | collective-permute-start | bytes 245768 | tf_op jit(solution)/shard_map/ppermute | solution.py:312
  14.7 1.2 %collective-permute-start.10 = (bf16[128,1152]{1,0:T(8,128)(2,1)S(1)}, bf16[128,1152]{1,0:T(8,128)(2,1)S(1)}, u32[]{:S(2)}, u32[]{:S(2)}) collective-permute-start(bf16[128,1152]{1,0:T(8,128)(2,1)S(1)} %pad_maximum_fusion.2), channel_id=1, source_target_pairs={{0,4},{1,5},{2,6},{3,7},{4,0},{5,1},{6,2},{7,3},{8,12},{9,13},{10,... | collective-permute-start | bytes 884744 | tf_op jit(solution)/shard_map/ppermute | solution.py:312
  16.4 1.5 %collective-permute-done.5.received_ref = bf16[32,1280]{1,0:T(8,128)(2,1)S(1)} collective-permute-done((bf16[32,1280]{1,0:T(8,128)(2,1)S(1)}, bf16[32,1280]{1,0:T(8,128)(2,1)S(1)}, u32[]{:S(2)}, u32[]{:S(2)}) %collective-permute-start.5) | collective-permute-done | bytes 81952 | tf_op jit(solution)/shard_map/ppermute | solution.py:312
  18.1 2.2 %collective-permute-start.6 = (bf16[32,1280]{1,0:T(8,128)(2,1)S(1)}, bf16[32,1280]{1,0:T(8,128)(2,1)S(1)}, u32[]{:S(2)}, u32[]{:S(2)}) collective-permute-start(bf16[32,1280]{1,0:T(8,128)(2,1)S(1)} %get-tuple-element.37), channel_id=1, source_target_pairs={{0,16},{1,17},{2,18},{3,19},{4,20},{5,21},{6,22},{7,23},{8,24},{9,... | collective-permute-start | bytes 245768 | tf_op jit(solution)/shard_map/ppermute | solution.py:312
  20.3 4.2 %collective-permute-done.6 = bf16[32,1280]{1,0:T(8,128)(2,1)S(1)} collective-permute-done((bf16[32,1280]{1,0:T(8,128)(2,1)S(1)}, bf16[32,1280]{1,0:T(8,128)(2,1)S(1)}, u32[]{:S(2)}, u32[]{:S(2)}) %collective-permute-start.6) | collective-permute-done | bytes 81952 | tf_op jit(solution)/shard_map/ppermute | solution.py:312
  25.0 3.2 %collective-permute-start.8 = (bf16[256,384]{1,0:T(8,128)(2,1)S(1)}, bf16[256,384]{1,0:T(8,128)(2,1)S(1)}, u32[]{:S(2)}, u32[]{:S(2)}) collective-permute-start(bf16[256,384]{1,0:T(8,128)(2,1)S(1)} %pad_maximum_fusion.3), channel_id=1, source_target_pairs={{0,16},{1,17},{2,18},{3,19},{4,20},{5,21},{6,22},{7,23},{8,24},{9,... | collective-permute-start | bytes 589832 | tf_op jit(solution)/shard_map/ppermute | solution.py:312
  28.2 2.1 %collective-permute-start.11 = (bf16[64,1152]{1,0:T(8,128)(2,1)S(1)}, bf16[64,1152]{1,0:T(8,128)(2,1)S(1)}, u32[]{:S(2)}, u32[]{:S(2)}) collective-permute-start(bf16[64,1152]{1,0:T(8,128)(2,1)S(1)} %slice.16), channel_id=1, source_target_pairs={{0,2},{1,3},{2,0},{3,1},{4,6},{5,7},{6,4},{7,5},{8,10},{9,11},{10,... | collective-permute-start | bytes 442376 | tf_op jit(solution)/shard_map/ppermute | solution.py:312
  30.3 0.9 %collective-permute-start.12 = (bf16[64,1152]{1,0:T(8,128)(2,1)S(1)}, bf16[64,1152]{1,0:T(8,128)(2,1)S(1)}, u32[]{:S(2)}, u32[]{:S(2)}) collective-permute-start(bf16[64,1152]{1,0:T(8,128)(2,1)S(1)} %slice.17), channel_id=1, source_target_pairs={{0,4},{1,5},{2,6},{3,7},{4,0},{5,1},{6,2},{7,3},{8,12},{9,13},{10,... | collective-permute-start | bytes 442376 | tf_op jit(solution)/shard_map/ppermute | solution.py:312
  31.2 3.9 %collective-permute-done.8 = bf16[256,384]{1,0:T(8,128)(2,1)S(1)} collective-permute-done((bf16[256,384]{1,0:T(8,128)(2,1)S(1)}, bf16[256,384]{1,0:T(8,128)(2,1)S(1)}, u32[]{:S(2)}, u32[]{:S(2)}) %collective-permute-start.8) | collective-permute-done | bytes 196640 | tf_op jit(solution)/shard_map/ppermute | solution.py:312
  36.4 0.9 %collective-permute-start.14 = (bf16[128,1280]{1,0:T(8,128)(2,1)S(1)}, bf16[128,1280]{1,0:T(8,128)(2,1)S(1)}, u32[]{:S(2)}, u32[]{:S(2)}) collective-permute-start(bf16[128,1280]{1,0:T(8,128)(2,1)S(1)} %pad_maximum_fusion.1.refs_0_), channel_id=1, source_target_pairs={{0,2},{1,3},{2,0},{3,1},{4,6},{5,7},{6,4},{7,5},{8,10},{9,11},{10,... | collective-permute-start | bytes 983048 | tf_op jit(solution)/shard_map/ppermute | solution.py:312
  38.4 1.6 %grad.3.refs_0_ = bf16[128,1280]{1,0:T(8,128)(2,1)S(1)} custom-call(bf16[128,1280]{1,0:T(8,128)(2,1)S(1)} %pad_maximum_fusion.1.refs_0_, bf16[512,1152]{1,0:T(8,128)(2,1)S(1)} %constant_dynamic-update-slice_fusion.refs_1_.refs_2_, bf16[512,1152]{1,0:T(8,128)(2,1)S(1)} %collective-permute-done.13.refs_2_.refs_3_), custom_call_target="tpu_custom_call" | custom-call | flops 6039797760 | tf_op jit(solution)/shard_map/grad/pallas_call | solution.py:388
  40.3 5.4 %collective-permute-done.16.refs_1_ = bf16[128,1280]{1,0:T(8,128)(2,1)S(1)} collective-permute-done((bf16[128,1280]{1,0:T(8,128)(2,1)S(1)}, bf16[128,1280]{1,0:T(8,128)(2,1)S(1)}, u32[]{:S(2)}, u32[]{:S(2)}) %collective-permute-start.16) | collective-permute-done | bytes 327712 | tf_op jit(solution)/shard_map/ppermute | solution.py:312
  45.7 1.3 %collective-permute-start.19 = (bf16[64,1280]{1,0:T(8,128)(2,1)S(1)}, bf16[64,1280]{1,0:T(8,128)(2,1)S(1)}, u32[]{:S(2)}, u32[]{:S(2)}) collective-permute-start(bf16[64,1280]{1,0:T(8,128)(2,1)S(1)} %slice.18), channel_id=1, source_target_pairs={{0,2},{1,3},{2,0},{3,1},{4,6},{5,7},{6,4},{7,5},{8,10},{9,11},{10,... | collective-permute-start | bytes 491528 | tf_op jit(solution)/shard_map/ppermute | solution.py:312
  48.5 2.0 %grad.4.refs_2_.refs_0_ = bf16[256,1280]{1,0:T(8,128)(2,1)S(1)} custom-call(bf16[128,1280]{1,0:T(8,128)(2,1)S(1)} %collective-permute-done.14.refs_0_, bf16[128,1280]{1,0:T(8,128)(2,1)S(1)} %collective-permute-done.16.refs_1_, bf16[512,1152]{1,0:T(8,128)(2,1)S(1)} %constant_dynamic-update-slice_fusion.refs_1_.refs_2_, ...), custom_call_target="tpu_custom_call" | custom-call | flops 12079595520 | tf_op jit(solution)/shard_map/grad/pallas_call | solution.py:388
  51.6 1.0 %collective-permute-done.20.refs_1_ = bf16[64,1280]{1,0:T(8,128)(2,1)S(1)} collective-permute-done((bf16[64,1280]{1,0:T(8,128)(2,1)S(1)}, bf16[64,1280]{1,0:T(8,128)(2,1)S(1)}, u32[]{:S(2)}, u32[]{:S(2)}) %collective-permute-start.20) | collective-permute-done | bytes 163872 | tf_op jit(solution)/shard_map/ppermute | solution.py:312
  52.6 1.6 %grad.5.refs_0_ = bf16[128,1280]{1,0:T(8,128)(2,1)S(1)} custom-call(bf16[64,1280]{1,0:T(8,128)(2,1)S(1)} %collective-permute-done.19.refs_0_, bf16[64,1280]{1,0:T(8,128)(2,1)S(1)} %collective-permute-done.20.refs_1_, bf16[512,1152]{1,0:T(8,128)(2,1)S(1)} %constant_dynamic-update-slice_fusion.refs_1_.refs_2_, ...), custom_call_target="tpu_custom_call" | custom-call | flops 6039797760 | tf_op jit(solution)/shard_map/grad/pallas_call | solution.py:388
  54.3 0.9 %weight.4.refs_2_ = f32[384,1152]{1,0:T(8,128)S(1)} custom-call(s32[1]{0:T(128)} %bitcast.place_ref, bf16[1024,384]{1,0:T(8,128)(2,1)S(1)} %constant_dynamic-update-slice_fusion.5.features_ref, bf16[256,1280]{1,0:T(8,128)(2,1)S(1)} %grad.4.refs_2_.refs_0_, bf16[256,1280]{1,0:T(8,128)(2,1)S(1)} %collective-permute-done.17.refs_3_.refs_1_, ...), custom_call_target="tpu_custom_call" | custom-call | tf_op jit(solution)/shard_map/weight/pallas_call | solution.py:413
  55.4 1.1 %grad_features.1 = bf16[128,384]{1,0:T(8,128)(2,1)} custom-call(s32[1]{0:T(128)} %bitcast.place_ref, bf16[384,1152]{1,0:T(8,128)(2,1)S(1)} %copy-done.1, f32[1,1152]{1,0:T(1,128)S(1)} %get-tuple-element.36.weight_sum_ref, bf16[128,1280]{1,0:T(8,128)(2,1)S(1)} %grad.3.refs_0_, bf16[128,1280]{1,0:T(8,128)(2,1)S(1)} %collective-permute-done.15.refs_1_, ...), custom_call_target="tpu_custom_call" | custom-call | tf_op jit(solution)/shard_map/grad_features/pallas_call | solution.py:423
  56.4 1.7 %weight.5 = f32[384,1152]{1,0:T(8,128)} custom-call(s32[1]{0:T(128)} %bitcast.place_ref, bf16[1024,384]{1,0:T(8,128)(2,1)S(1)} %constant_dynamic-update-slice_fusion.5.features_ref, bf16[128,1280]{1,0:T(8,128)(2,1)S(1)} %grad.5.refs_0_, bf16[128,1280]{1,0:T(8,128)(2,1)S(1)} %collective-permute-done.21.refs_1_, f32[384,1152]{1,0:T(8,128)S(1)} %weight.4.refs_2_), custom_call_target="tpu_custom_call" | custom-call | tf_op jit(solution)/shard_map/weight/pallas_call | solution.py:413
  (58 shorter events, 9.4 us)
Async XLA Ops:
  1.5 18.8 %copy-start.3 = (bf16[128,384]{1,0:T(8,128)(2,1)S(1)}, bf16[128,384]{1,0:T(8,128)(2,1)}, u32[]{:S(2)}) copy-start(bf16[128,384]{1,0:T(8,128)(2,1)} %features_ref.1) | copy-start | bytes 294916
  1.6 10.0 %collective-permute-start.4 = (bf16[32,1152]{1,0:T(8,128)(2,1)S(1)}, bf16[32,1152]{1,0:T(8,128)(2,1)S(1)}, u32[]{:S(2)}, u32[]{:S(2)}) collective-permute-start(bf16[32,1152]{1,0:T(8,128)(2,1)S(1)} %unit_texts.1), channel_id=1, source_target_pairs={{0,24},{1,25},{2,26},{3,27},{4,28},{5,29},{6,30},{7,31},{8,16},{9,... | collective-permute-start | bytes 221192 | tf_op jit(solution)/shard_map/ppermute | solution.py:312
  6.7 5.0 %collective-permute-start.3 = (bf16[32,1152]{1,0:T(8,128)(2,1)S(1)}, bf16[32,1152]{1,0:T(8,128)(2,1)S(1)}, u32[]{:S(2)}, u32[]{:S(2)}) collective-permute-start(bf16[32,1152]{1,0:T(8,128)(2,1)S(1)} %unit_texts.1), channel_id=1, source_target_pairs={{0,8},{1,9},{2,10},{3,11},{4,12},{5,13},{6,14},{7,15},{8,0},{9,1},... | collective-permute-start | bytes 221192 | tf_op jit(solution)/shard_map/ppermute | solution.py:312
  6.7 5.8 %collective-permute-start.2 = (bf16[32,1152]{1,0:T(8,128)(2,1)S(1)}, bf16[32,1152]{1,0:T(8,128)(2,1)S(1)}, u32[]{:S(2)}, u32[]{:S(2)}) collective-permute-start(bf16[32,1152]{1,0:T(8,128)(2,1)S(1)} %unit_texts.1), channel_id=1, source_target_pairs={{0,16},{1,17},{2,18},{3,19},{4,20},{5,21},{6,22},{7,23},{8,24},{9,... | collective-permute-start | bytes 221192 | tf_op jit(solution)/shard_map/ppermute | solution.py:312
  7.4 5.7 %collective-permute-start.1 = (bf16[128,384]{1,0:T(8,128)(2,1)}, bf16[128,384]{1,0:T(8,128)(2,1)S(1)}, u32[]{:S(2)}, u32[]{:S(2)}) collective-permute-start(bf16[128,384]{1,0:T(8,128)(2,1)} %features_ref.1), channel_id=1, source_target_pairs={{0,4},{1,5},{2,6},{3,7},{4,0},{5,1},{6,2},{7,3},{8,12},{9,13},{10,... | collective-permute-start | bytes 294920 | tf_op jit(solution)/shard_map/ppermute | solution.py:312
  11.5 1.5 %collective-permute-start = (bf16[64,1280]{1,0:T(8,128)(2,1)S(1)}, bf16[64,1280]{1,0:T(8,128)(2,1)S(1)}, u32[]{:S(2)}, u32[]{:S(2)}) collective-permute-start(bf16[64,1280]{1,0:T(8,128)(2,1)S(1)} %get-tuple-element.27), channel_id=1, source_target_pairs={{0,1},{1,0},{2,3},{3,2},{4,5},{5,4},{6,7},{7,6},{8,9},{9,8},{10,11... | collective-permute-start | bytes 491528 | tf_op jit(solution)/shard_map/ppermute | solution.py:312
  13.1 4.9 %collective-permute-start.5 = (bf16[32,1280]{1,0:T(8,128)(2,1)S(1)}, bf16[32,1280]{1,0:T(8,128)(2,1)S(1)}, u32[]{:S(2)}, u32[]{:S(2)}) collective-permute-start(bf16[32,1280]{1,0:T(8,128)(2,1)S(1)} %get-tuple-element.33), channel_id=1, source_target_pairs={{0,2},{1,3},{2,0},{3,1},{4,6},{5,7},{6,4},{7,5},{8,10},{9,11},{10,... | collective-permute-start | bytes 245768 | tf_op jit(solution)/shard_map/ppermute | solution.py:312
  14.7 13.5 %collective-permute-start.10 = (bf16[128,1152]{1,0:T(8,128)(2,1)S(1)}, bf16[128,1152]{1,0:T(8,128)(2,1)S(1)}, u32[]{:S(2)}, u32[]{:S(2)}) collective-permute-start(bf16[128,1152]{1,0:T(8,128)(2,1)S(1)} %pad_maximum_fusion.2), channel_id=1, source_target_pairs={{0,4},{1,5},{2,6},{3,7},{4,0},{5,1},{6,2},{7,3},{8,12},{9,13},{10,... | collective-permute-start | bytes 884744 | tf_op jit(solution)/shard_map/ppermute | solution.py:312
  15.9 14.3 %collective-permute-start.9 = (bf16[128,1152]{1,0:T(8,128)(2,1)S(1)}, bf16[128,1152]{1,0:T(8,128)(2,1)S(1)}, u32[]{:S(2)}, u32[]{:S(2)}) collective-permute-start(bf16[128,1152]{1,0:T(8,128)(2,1)S(1)} %pad_maximum_fusion.2), channel_id=1, source_target_pairs={{0,2},{1,3},{2,0},{3,1},{4,6},{5,7},{6,4},{7,5},{8,10},{9,11},{10,... | collective-permute-start | bytes 884744 | tf_op jit(solution)/shard_map/ppermute | solution.py:312
  18.1 6.4 %collective-permute-start.6 = (bf16[32,1280]{1,0:T(8,128)(2,1)S(1)}, bf16[32,1280]{1,0:T(8,128)(2,1)S(1)}, u32[]{:S(2)}, u32[]{:S(2)}) collective-permute-start(bf16[32,1280]{1,0:T(8,128)(2,1)S(1)} %get-tuple-element.37), channel_id=1, source_target_pairs={{0,16},{1,17},{2,18},{3,19},{4,20},{5,21},{6,22},{7,23},{8,24},{9,... | collective-permute-start | bytes 245768 | tf_op jit(solution)/shard_map/ppermute | solution.py:312
  24.5 6.6 %collective-permute-start.7 = (bf16[64,1280]{1,0:T(8,128)(2,1)S(1)}, bf16[64,1280]{1,0:T(8,128)(2,1)S(1)}, u32[]{:S(2)}, u32[]{:S(2)}) collective-permute-start(bf16[64,1280]{1,0:T(8,128)(2,1)S(1)} %pad_maximum_fusion.4), channel_id=1, source_target_pairs={{0,8},{1,9},{2,10},{3,11},{4,12},{5,13},{6,14},{7,15},{8,0},{9,1},... | collective-permute-start | bytes 491528 | tf_op jit(solution)/shard_map/ppermute | solution.py:312
  25.0 10.1 %collective-permute-start.8 = (bf16[256,384]{1,0:T(8,128)(2,1)S(1)}, bf16[256,384]{1,0:T(8,128)(2,1)S(1)}, u32[]{:S(2)}, u32[]{:S(2)}) collective-permute-start(bf16[256,384]{1,0:T(8,128)(2,1)S(1)} %pad_maximum_fusion.3), channel_id=1, source_target_pairs={{0,16},{1,17},{2,18},{3,19},{4,20},{5,21},{6,22},{7,23},{8,24},{9,... | collective-permute-start | bytes 589832 | tf_op jit(solution)/shard_map/ppermute | solution.py:312
  28.2 6.9 %collective-permute-start.11 = (bf16[64,1152]{1,0:T(8,128)(2,1)S(1)}, bf16[64,1152]{1,0:T(8,128)(2,1)S(1)}, u32[]{:S(2)}, u32[]{:S(2)}) collective-permute-start(bf16[64,1152]{1,0:T(8,128)(2,1)S(1)} %slice.16), channel_id=1, source_target_pairs={{0,2},{1,3},{2,0},{3,1},{4,6},{5,7},{6,4},{7,5},{8,10},{9,11},{10,... | collective-permute-start | bytes 442376 | tf_op jit(solution)/shard_map/ppermute | solution.py:312
  30.3 5.2 %collective-permute-start.12 = (bf16[64,1152]{1,0:T(8,128)(2,1)S(1)}, bf16[64,1152]{1,0:T(8,128)(2,1)S(1)}, u32[]{:S(2)}, u32[]{:S(2)}) collective-permute-start(bf16[64,1152]{1,0:T(8,128)(2,1)S(1)} %slice.17), channel_id=1, source_target_pairs={{0,4},{1,5},{2,6},{3,7},{4,0},{5,1},{6,2},{7,3},{8,12},{9,13},{10,... | collective-permute-start | bytes 442376 | tf_op jit(solution)/shard_map/ppermute | solution.py:312
  35.5 2.9 %collective-permute-start.13 = (bf16[512,1152]{1,0:T(8,128)(2,1)S(1)}, bf16[512,1152]{1,0:T(8,128)(2,1)S(1)}, u32[]{:S(2)}, u32[]{:S(2)}) collective-permute-start(bf16[512,1152]{1,0:T(8,128)(2,1)S(1)} %constant_dynamic-update-slice_fusion.refs_1_.refs_2_), channel_id=1, source_target_pairs={{0,1},{1,0},{2,3},{3,2},{4,5},{5,4},{6,7},{7,6},{8,9},{9,8},{10,11... | collective-permute-start | bytes 3538952 | tf_op jit(solution)/shard_map/ppermute | solution.py:312
  35.6 10.1 %collective-permute-start.16 = (bf16[128,1280]{1,0:T(8,128)(2,1)S(1)}, bf16[128,1280]{1,0:T(8,128)(2,1)S(1)}, u32[]{:S(2)}, u32[]{:S(2)}) collective-permute-start(bf16[128,1280]{1,0:T(8,128)(2,1)S(1)} %pad_maximum_fusion.1.refs_0_), channel_id=1, source_target_pairs={{0,4},{1,5},{2,6},{3,7},{4,0},{5,1},{6,2},{7,3},{8,12},{9,13},{10,... | collective-permute-start | bytes 983048 | tf_op jit(solution)/shard_map/ppermute | solution.py:312
  36.4 10.6 %collective-permute-start.14 = (bf16[128,1280]{1,0:T(8,128)(2,1)S(1)}, bf16[128,1280]{1,0:T(8,128)(2,1)S(1)}, u32[]{:S(2)}, u32[]{:S(2)}) collective-permute-start(bf16[128,1280]{1,0:T(8,128)(2,1)S(1)} %pad_maximum_fusion.1.refs_0_), channel_id=1, source_target_pairs={{0,2},{1,3},{2,0},{3,1},{4,6},{5,7},{6,4},{7,5},{8,10},{9,11},{10,... | collective-permute-start | bytes 983048 | tf_op jit(solution)/shard_map/ppermute | solution.py:312
  37.4 11.0 %collective-permute-start.18 = (bf16[512,384]{1,0:T(8,128)(2,1)S(1)}, bf16[512,384]{1,0:T(8,128)(2,1)S(1)}, u32[]{:S(2)}, u32[]{:S(2)}) collective-permute-start(bf16[512,384]{1,0:T(8,128)(2,1)S(1)} %pad_maximum_fusion), channel_id=1, source_target_pairs={{0,8},{1,9},{2,10},{3,11},{4,12},{5,13},{6,14},{7,15},{8,0},{9,1},... | collective-permute-start | bytes 1179656 | tf_op jit(solution)/shard_map/ppermute | solution.py:312
  40.0 8.4 %collective-permute-start.15 = (bf16[128,1280]{1,0:T(8,128)(2,1)S(1)}, bf16[128,1280]{1,0:T(8,128)(2,1)S(1)}, u32[]{:S(2)}, u32[]{:S(2)}) collective-permute-start(bf16[128,1280]{1,0:T(8,128)(2,1)S(1)} %grad.3.refs_0_), channel_id=1, source_target_pairs={{0,1},{1,0},{2,3},{3,2},{4,5},{5,4},{6,7},{7,6},{8,9},{9,8},{10,11... | collective-permute-start | bytes 983048 | tf_op jit(solution)/shard_map/ppermute | solution.py:312
  45.7 5.8 %collective-permute-start.19 = (bf16[64,1280]{1,0:T(8,128)(2,1)S(1)}, bf16[64,1280]{1,0:T(8,128)(2,1)S(1)}, u32[]{:S(2)}, u32[]{:S(2)}) collective-permute-start(bf16[64,1280]{1,0:T(8,128)(2,1)S(1)} %slice.18), channel_id=1, source_target_pairs={{0,2},{1,3},{2,0},{3,1},{4,6},{5,7},{6,4},{7,5},{8,10},{9,11},{10,... | collective-permute-start | bytes 491528 | tf_op jit(solution)/shard_map/ppermute | solution.py:312
  47.0 5.5 %collective-permute-start.20 = (bf16[64,1280]{1,0:T(8,128)(2,1)S(1)}, bf16[64,1280]{1,0:T(8,128)(2,1)S(1)}, u32[]{:S(2)}, u32[]{:S(2)}) collective-permute-start(bf16[64,1280]{1,0:T(8,128)(2,1)S(1)} %slice.19), channel_id=1, source_target_pairs={{0,4},{1,5},{2,6},{3,7},{4,0},{5,1},{6,2},{7,3},{8,12},{9,13},{10,... | collective-permute-start | bytes 491528 | tf_op jit(solution)/shard_map/ppermute | solution.py:312
  50.5 3.8 %collective-permute-start.17 = (bf16[256,1280]{1,0:T(8,128)(2,1)S(1)}, bf16[256,1280]{1,0:T(8,128)(2,1)S(1)}, u32[]{:S(2)}, u32[]{:S(2)}) collective-permute-start(bf16[256,1280]{1,0:T(8,128)(2,1)S(1)} %grad.4.refs_2_.refs_0_), channel_id=1, source_target_pairs={{0,1},{1,0},{2,3},{3,2},{4,5},{5,4},{6,7},{7,6},{8,9},{9,8},{10,11... | collective-permute-start | bytes 1966088 | tf_op jit(solution)/shard_map/ppermute | solution.py:312
  54.2 1.2 %copy-start.1 = (bf16[384,1152]{1,0:T(8,128)(2,1)S(1)}, bf16[384,1152]{1,0:T(8,128)(2,1)}, u32[]{:S(2)}) copy-start(bf16[384,1152]{1,0:T(8,128)(2,1)} %weight_ref.3) | copy-start | bytes 2654212
  54.2 2.2 %collective-permute-start.21 = (bf16[128,1280]{1,0:T(8,128)(2,1)S(1)}, bf16[128,1280]{1,0:T(8,128)(2,1)S(1)}, u32[]{:S(2)}, u32[]{:S(2)}) collective-permute-start(bf16[128,1280]{1,0:T(8,128)(2,1)S(1)} %grad.5.refs_0_), channel_id=1, source_target_pairs={{0,1},{1,0},{2,3},{3,2},{4,5},{5,4},{6,7},{7,6},{8,9},{9,8},{10,11... | collective-permute-start | bytes 983048 | tf_op jit(solution)/shard_map/ppermute | solution.py:312
  (3 other events, 2.9 us)
